TPU v7x, 256 devices: a whole 4x4x8 slice. The times are simulated.
256 devices in a mesh: space: 16 (over x, y), spec: 16 (over z, core).
Axes of the slice: x: 4, y: 4, z: 8, core: 2. Of those that a mesh axis runs over, the one named last changes fastest.
Arguments:
- spectrum: float32 [624, 262144], P('spec', 'space'), may hold values from 0.05 to 2
- wind_speed: float32 [262144], P('space'), may hold values from 2 to 25
- wind_dir: float32 [262144], P('space'), may hold values from -3.140625 to 3.140625
- counts: int32 [2048], P('space'), may hold values from 0 to 128, as said below
- send_list: int32 [4096], P('space'), may hold values from 0 to 16383, as said below
- neighbors: int32 [4, 262144], P(None, 'space'), may hold values from 0 to 16639, as said below
- neighbor_mask: int32 [4, 262144], P(None, 'space'), may hold values from 0 to 1
Outputs:
- spectrum_next: float32 [624, 262144], P('spec', 'space')
Inputs may be any that keep to these rules, and one draw needn't show every extreme that they name: The sea points of a tile fill its first counts slots and the other slots are empty. The counts of the 128 tiles of one index of space sum to at most 10240, and to exactly 10240 on at least one index. `send_list`: for each index of space, entries 0 to 127 name live slots of its first tile and entries 128 to 255 live slots of its last tile, in an order of their own; entry e of either half is padding (slot 0) where e is not below the count of that tile. `neighbors`: where the mask is 1, a code below 16384 names a live local slot and a larger code names an entry that is not padding; a slot that is not live has all its masks 0. Where the mask is 1, a west or east code names a slot of the slot's own tile, a south code a slot of the tile before it (an entry below 16512 for a device's first tile), and a north code a slot of the tile after it (an entry of 16512 or more for a device's last tile).
All inputs are finite; a program needn't handle non-finite values.
Results may differ from a plain program's by a relative error of at most 0.0003.
Values sent between devices are 32-bit elements; how exact they have to be, the bound alone decides.
No kernel may reach another device: no remote copies, remote signals or barrier semaphores. Data moves between devices by JAX's collectives and lax.ppermute only.
A program may use at most 128 MiB of HBM per device.

v0:
```python
import math

import jax
import jax.numpy as jnp
import numpy as np
from jax import lax
from jax.sharding import PartitionSpec as P

ND = 24
NF = 26
TILE = 128
K = 624


LOG_RATIO = math.log(1.1)
FREQ_LOW = 0.05
EPS = 1e-06
PLUS_FACTOR = 1.0 / 1.25**4
MINUS_FACTOR = 1.0 / 0.75**4
CROSS_FACTOR = 1.0 / 0.9375**4


def padded(x, sides, width):
    for axis, dim in sides:
        size, length = (lax.axis_size(axis), x.shape[dim])
        up = [(i, (i + 1) % size) for i in range(size)]
        down = [(j, i) for i, j in up]
        last = lax.slice_in_dim(x, length - width, length, axis=dim)
        first = lax.slice_in_dim(x, 0, width, axis=dim)
        before = lax.ppermute(last, axis, up)
        after = lax.ppermute(first, axis, down)
        x = jnp.concatenate([before, x, after], axis=dim)
    return x


def component_tables(comp_index):
    band_level = (comp_index // ND).astype(jnp.float32)
    heading = ((comp_index % ND).astype(jnp.float32) + 0.5) * (2.0 * math.pi / ND)
    frequency = FREQ_LOW * jnp.exp(LOG_RATIO * band_level)
    courant = 0.6 * jnp.exp(-LOG_RATIO * band_level)
    return (frequency, heading, courant)


def interaction_table(dir_count, freq_count):
    comp_total = dir_count * freq_count
    matrix = np.zeros((2 * comp_total, comp_total), np.float32)
    shifts = (
        (math.log(1.25) / math.log(1.1), 33.56 * dir_count / 360.0),
        (math.log(0.75) / math.log(1.1), 11.48 * dir_count / 360.0),
    )
    for which_half, (band_shift, turning) in enumerate(shifts):
        for band_level in range(freq_count):
            band_place = band_level + band_shift
            low_band = math.floor(band_place)
            frac_band = band_place - low_band
            for mirror in (1.0, -1.0):
                for heading in range(dir_count):
                    dir_place = heading + mirror * turning
                    low_dir = math.floor(dir_place)
                    frac_dir = dir_place - low_dir
                    row_index = which_half * comp_total + band_level * dir_count + heading
                    for band_step, band_weight in ((0, 1.0 - frac_band), (1, frac_band)):
                        source_band = low_band + band_step
                        if 0 <= source_band < freq_count:
                            for dir_step, dir_weight in ((0, 1.0 - frac_dir), (1, frac_dir)):
                                source_dir = (low_dir + dir_step) % dir_count
                                matrix[row_index, source_band * dir_count + source_dir] += (
                                    0.5 * band_weight * dir_weight
                                )
    return matrix


def sources(pair_table, frequency, spectra):
    freq_col = frequency[:, None]
    mean_freq = jnp.mean(frequency)
    energy_sum = jnp.mean(spectra, axis=0) + EPS
    first_moment = (jnp.mean(freq_col * spectra, axis=0) + EPS * mean_freq) / energy_sum
    steepness = energy_sum * (first_moment / mean_freq) ** 4
    decay = 0.3 * (freq_col / first_moment) * steepness**2
    shifted = jnp.dot(pair_table, spectra, precision=lax.Precision.HIGHEST)
    upper_part = shifted[:K]
    lower_part = shifted[K:]
    exchange_term = (
        0.05
        * (freq_col / first_moment)
        * (
            spectra * spectra * (upper_part * PLUS_FACTOR + lower_part * MINUS_FACTOR)
            - 2.0 * CROSS_FACTOR * spectra * upper_part * lower_part
        )
    )
    return spectra * jnp.exp(-decay) + exchange_term


def per_device(spectrum, wind_speed, wind_dir, counts, send_list, neighbors, neighbor_mask):
    comp_local, slot_local = spectrum.shape
    tile_count = slot_local // TILE
    spec_count = lax.axis_size("spec")
    position = jnp.arange(TILE, dtype=jnp.int32)
    wet_slot = (position[None, :] < counts[:, None]).reshape(slot_local).astype(jnp.float32)
    energy = spectrum * wet_slot[None, :]
    outgoing = jnp.take(energy, send_list, axis=1)
    widened = padded(outgoing, (("space", 1),), TILE)
    own_tiles = energy.reshape(comp_local, tile_count, TILE)
    from_lower = widened[:, :TILE][:, None, :]
    from_upper = widened[:, 3 * TILE :][:, None, :]
    before_tiles = jnp.concatenate([from_lower, own_tiles[:, :-1]], axis=1)
    after_tiles = jnp.concatenate([own_tiles[:, 1:], from_upper], axis=1)
    windows = (own_tiles, own_tiles, before_tiles, after_tiles)
    comp_index = lax.axis_index("spec") * comp_local + jnp.arange(comp_local, dtype=jnp.int32)
    frequency, heading, courant = component_tables(comp_index)
    east_speed = (courant * jnp.cos(heading))[:, None]
    north_speed = (courant * jnp.sin(heading))[:, None]
    weights = (
        jnp.maximum(east_speed, 0.0),
        jnp.maximum(-east_speed, 0.0),
        jnp.maximum(north_speed, 0.0),
        jnp.maximum(-north_speed, 0.0),
    )
    advected = energy
    for direction in range(4):
        within = (neighbors[direction] % TILE).reshape(tile_count, TILE)
        selector = (within[:, :, None] == position[None, None, :]).astype(jnp.float32)
        picked = jnp.einsum(
            "kts,tps->ktp", windows[direction], selector, precision=lax.Precision.HIGHEST
        )
        nearby = (
            picked.reshape(comp_local, slot_local)
            * neighbor_mask[direction].astype(jnp.float32)[None, :]
        )
        advected = advected - weights[direction] * (energy - nearby)
    advected = advected * wet_slot[None, :]
    wind_drive = (
        wind_speed[None, :]
        * frequency[:, None]
        * jnp.cos(heading[:, None] - wind_dir[None, :])
        / 1.56
        - 1.0
    )
    growth = advected * jnp.exp(0.08 * jnp.maximum(wind_drive, 0.0))
    pair_table = jnp.asarray(interaction_table(ND, NF), dtype=jnp.float32)
    all_freq = component_tables(jnp.arange(K, dtype=jnp.int32))[0]
    group_size = growth.shape[1] // spec_count
    updated = sources(
        pair_table,
        all_freq,
        lax.all_to_all(
            growth.reshape(comp_local, spec_count, group_size),
            "spec",
            split_axis=1,
            concat_axis=0,
            tiled=True,
        )[:, 0, :],
    )
    returned = lax.all_to_all(updated[:, None, :], "spec", split_axis=0, concat_axis=1, tiled=True)
    returned = returned.reshape(comp_local, growth.shape[1])
    return returned * wet_slot[None, :]


def solution(mesh):
    in_specs = (
        P("spec", "space"),
        P("space"),
        P("space"),
        P("space"),
        P("space"),
        P(None, "space"),
        P(None, "space"),
    )
    out_specs = P("spec", "space")
    return jax.shard_map(
        per_device, mesh=mesh, in_specs=in_specs, out_specs=out_specs, check_vma=False
    )
```

profile of v0, /device:TPU:1, one launch (start us, length us, event | category | flops | bytes accessed | tf_op | source)
XLA Modules:
  0.0 266.7 jit_solution(3016593426276597278)
XLA Ops:
  0.0 0.7 compare_select_fusion
  0.7 0.7 compare_and_fusion
  1.4 0.7 convert_bitcast_fusion
  2.1 1.9 broadcast_multiply_fusion.1
  4.0 4.8 %copy.57 = f32[39,16384]{0,1:T(8,128)} copy(f32[39,16384]{1,0:T(8,128)S(1)} %broadcast_multiply_fusion.1) | data formatting | bytes 5111808 | tf_op jit(solution)/shard_map/mul | solution.py:100
  8.8 4.1 %gather_fusion = f32[256,39]{1,0:T(8,128)S(1)} fusion(f32[39,16384]{0,1:T(8,128)} %copy.57, s32[1024]{0:T(1024)S(1)} %pad_clamp_fusion), kind=kCustom, calls=%fused_computation | custom fusion | bytes 80896 | tf_op jit(solution)/shard_map/jit(_take)/gather | solution.py:101
  12.9 0.1 copy.58
  13.1 5.8 %collective-permute-start.1 = (f32[39,128]{1,0:T(8,128)S(1)}, f32[39,128]{1,0:T(8,128)S(1)}, u32[]{:S(2)}, u32[]{:S(2)}) collective-permute-start(f32[39,128]{1,0:T(8,128)S(1)} %get-tuple-element.16), channel_id=1, source_target_pairs={{16,0},{32,16},{48,32},{64,48},{80,64},{96,80},{112,96},{128,112},... | collective-permute-start | bytes 59912 | tf_op jit(solution)/shard_map/ppermute | solution.py:31
  18.9 0.0 collective-permute-start
  18.9 0.1 negate_maximum_fusion
  19.0 0.5 copy.68
  19.5 0.2 slice.64
  19.6 0.0 copy-start.3
  19.6 0.5 fusion.48
  20.2 0.4 copy-done.3
  20.6 0.2 fusion.49
  20.9 11.7 %fusion.20 = f32[39,128,128]{2,0,1:T(8,128)S(1)} fusion(s32[128,128]{1,0:T(8,128)S(1)} %add_select_fusion.2, f32[39,128,128]{2,1,0:T(8,128)S(1)} %slice.64), kind=kOutput, calls=%fused_computation.25 | convolution fusion | flops 983564288 | bytes 5177344 | tf_op jit(solution)/shard_map/kts,tps->ktp/dot_general | solution.py:123
  32.6 0.0 copy-start.4
  32.6 11.9 %fusion.21 = f32[39,128,128]{2,0,1:T(8,128)S(1)} fusion(s32[128,128]{1,0:T(8,128)S(1)} %add_select_fusion.3, f32[39,128,128]{2,1,0:T(8,128)S(1)} %slice.64), kind=kOutput, calls=%fused_computation.26 | convolution fusion | flops 983564288 | bytes 5177344 | tf_op jit(solution)/shard_map/kts,tps->ktp/dot_general | solution.py:123
  44.5 0.2 slice_convert_fusion.3
  44.7 0.1 broadcast_maximum_fusion
  44.8 1.5 copy.80
  46.3 1.5 copy.81
  47.7 0.5 copy.56
  48.3 0.2 pad.6
  48.5 1.5 copy.70
  50.0 0.5 copy.54
  50.5 0.3 pad.5
  50.8 1.5 copy.69
  52.3 8.9 %fusion.14 = f32[39,128,128]{2,0,1:T(8,128)S(1)} fusion(f32[39,1,128]{2,0,1:T(8,128)S(1)} %bitcast.86, f32[39,127,128]{2,0,1:T(8,128)S(1)} %copy.80, s32[128,128]{1,0:T(8,128)S(1)} %add_select_fusion), kind=kOutput, calls=%fused_computation.23 | convolution fusion | flops 984203264 | bytes 5177344 | tf_op jit(solution)/shard_map/kts,tps->ktp/dot_general | solution.py:123
  61.2 0.5 copy.62
  61.7 0.3 pad.8
  62.0 1.5 copy.72
  63.5 8.5 %fusion.17 = f32[39,128,128]{2,0,1:T(8,128)S(1)} fusion(f32[39,127,128]{2,0,1:T(8,128)S(1)} %copy.81, f32[39,1,128]{2,0,1:T(8,128)S(1)} %bitcast.85, s32[128,128]{1,0:T(8,128)S(1)} %add_select_fusion.1), kind=kOutput, calls=%fused_computation.24 | convolution fusion | flops 984203264 | bytes 5177344 | tf_op jit(solution)/shard_map/kts,tps->ktp/dot_general | solution.py:123
  72.0 0.5 copy.60
  72.5 0.3 pad.7
  72.8 0.0 copy-start
  72.8 0.0 copy-start.5
  72.8 0.0 copy-start.6
  72.8 1.5 copy.71
  74.3 0.2 copy-done
  74.5 11.0 %exponential_multiply_fusion = f32[39,16384]{1,0:T(8,128)S(1)} fusion(f32[39,16384]{1,0:T(8,128)S(1)} %bitcast.63, f32[39,16384]{1,0:T(8,128)S(1)} %bitcast.64, f32[39,16384]{1,0:T(8,128)S(1)} %bitcast.61, f32[39,16384]{1,0:T(8,128)S(1)} %bitcast.62, f32[16384]{0:T(1024)S(1)} %copy-done.5, f32[39]{0:T(128)S(1)} %get-tuple-element.19, ...), kind=kLoop, calls=%fused_computation.20 | loop fusion | flops 16613376 | bytes 15795112 | tf_op jit(solution)/shard_map/mul | solution.py:139
  85.6 1.5 copy.73
  87.1 0.2 slice.65
  87.3 3.0 %copy.63 = f32[39,16,1024]{2,0,1:T(8,128)} copy(f32[39,16,1024]{2,1,0:T(8,128)S(1)} %slice.65) | data formatting | bytes 5111808 | tf_op jit(solution)/shard_map/reshape | solution.py:147
  90.2 9.7 %all-to-all-start = ((f32[39,16,1024]{2,0,1:T(8,128)}), f32[39,16,1024]{2,0,1:T(8,128)S(1)}, u32[]{:S(2)}, u32[]{:S(2)}) async-start(f32[39,16,1024]{2,0,1:T(8,128)} %copy.63), calls=%async_computation | async-start | bytes 5242880 | tf_op jit(solution)/shard_map/all_to_all | solution.py:146
  100.0 0.6 fusion.39
  101.8 57.9 %all-to-all-done = f32[39,16,1024]{2,0,1:T(8,128)S(1)} async-done(((f32[39,16,1024]{2,0,1:T(8,128)}), f32[39,16,1024]{2,0,1:T(8,128)S(1)}, u32[]{:S(2)}, u32[]{:S(2)}) %all-to-all-start) | async-done | bytes 2555936 | tf_op jit(solution)/shard_map/all_to_all | solution.py:146
  159.7 1.6 squeeze.23
  161.3 1.5 copy.64
  162.8 0.4 copy-done.2
  163.2 14.0 %fusion.51 = f32[1248,1024]{1,0:T(8,128)} fusion(f32[1248,624]{1,0:T(8,128)S(1)} %copy-done.2, f32[624,1024]{1,0:T(8,128)S(1)} %bitcast.75), kind=kOutput, calls=%fused_computation.102 | convolution fusion | flops 9569304576 | bytes 10782720 | tf_op jit(solution)/shard_map/dot_general | solution.py:80
  177.1 0.2 reduce_sum.29
  177.3 0.3 multiply_reduce_fusion
  177.6 1.4 copy-done.1
  179.1 3.4 %add_bitcast_fusion = f32[624,1,1024]{2,0,1:T(8,128)S(1)} fusion(f32[624,1024]{1,0:T(8,128)S(1)} %copy-done.1, f32[1248,1024]{1,0:T(8,128)} %fusion.51, f32[1024]{0:T(1024)S(1)} %get-tuple-element.18, f32[1024]{0:T(1024)S(1)} %get-tuple-element.17, f32[624]{0:T(1024)S(1)} %fusion.34), kind=kLoop, calls=%fused_computation.22 | loop fusion | flops 10223616 | bytes 10234304 | tf_op jit(solution)/shard_map/broadcast_in_dim | solution.py:154
  182.4 2.6 copy.65
  185.1 66.3 %all_to_all.30 = f32[624,1,1024]{2,1,0:T(1,128)S(1)} all-to-all(f32[624,1,1024]{2,1,0:T(1,128)S(1)} %copy.65), channel_id=1, replica_groups=mesh['space'=16,'spec'=16] {'spec'}, dimensions={0} | all-to-all | bytes 5111808 | tf_op jit(solution)/shard_map/all_to_all | solution.py:154
  251.3 8.1 %reduce.4 = f32[624,1024]{1,0:T(8,128)} reduce(f32[624,1,1024]{2,1,0:T(1,128)S(1)} %all_to_all.30, f32[]{:T(128)} %constant.131), dimensions={1}, to_apply=%all_to_all.25.reduce_sub_computation | reduce | bytes 5111812 | tf_op jit(solution)/shard_map/all_to_all | solution.py:154
  259.5 1.9 all_to_all.26
  261.4 1.5 copy.82
  262.8 0.2 pad.9
  263.0 1.5 copy.74
  264.5 1.7 broadcast_multiply_fusion
  (18 shorter events, 0.2 us)
Async XLA Ops:
  13.1 39.2 %collective-permute-start.1 = (f32[39,128]{1,0:T(8,128)S(1)}, f32[39,128]{1,0:T(8,128)S(1)}, u32[]{:S(2)}, u32[]{:S(2)}) collective-permute-start(f32[39,128]{1,0:T(8,128)S(1)} %get-tuple-element.16), channel_id=1, source_target_pairs={{16,0},{32,16},{48,32},{64,48},{80,64},{96,80},{112,96},{128,112},... | collective-permute-start | bytes 59912 | tf_op jit(solution)/shard_map/ppermute | solution.py:31
  18.9 44.6 %collective-permute-start = (f32[39,128]{1,0:T(8,128)S(1)}, f32[39,128]{1,0:T(8,128)S(1)}, u32[]{:S(2)}, u32[]{:S(2)}) collective-permute-start(f32[39,128]{1,0:T(8,128)S(1)} %get-tuple-element.15), channel_id=1, source_target_pairs={{0,16},{16,32},{32,48},{48,64},{64,80},{80,96},{96,112},{112,128},... | collective-permute-start | bytes 59912 | tf_op jit(solution)/shard_map/ppermute | solution.py:30
  19.6 1.0 copy-start.3
  32.6 11.9 %copy-start.4 = (s32[4,16384]{1,0:T(4,128)S(1)}, s32[4,16384]{1,0:T(4,128)}, u32[]{:S(2)}) copy-start(s32[4,16384]{1,0:T(4,128)} %param.14) | copy-start | bytes 786436
  72.8 1.7 copy-start
  72.8 1.7 copy-start.5
  72.8 1.7 copy-start.6
  90.2 69.4 %all-to-all-start = ((f32[39,16,1024]{2,0,1:T(8,128)}), f32[39,16,1024]{2,0,1:T(8,128)S(1)}, u32[]{:S(2)}, u32[]{:S(2)}) async-start(f32[39,16,1024]{2,0,1:T(8,128)} %copy.63), calls=%async_computation | async-start | bytes 5242880 | tf_op jit(solution)/shard_map/all_to_all | solution.py:146
  161.3 1.9 copy-start.2
  177.3 1.7 copy-start.1
where the time goes:
time: 271 us; the launch traced here: 267 us
  blocking collectives  66.3 us (24%)
  waiting for transfers between devices  57.9 us (21%)
  matrix products  54.9 us (20%)
  local copies, waits for them, and re-layouts  40.2 us (15%)
  other arithmetic  29.9 us (11%)
  starting transfers between devices  15.6 us (6%)
    all_to_all x1, blocking collectives, per_device(): lax.all_to_all(updated[:, None, :], 'spec', split_axis=0, concat_axis=1,...  66.3 us
    all_to_all x1, waiting for transfers between devices, per_device(): lax.all_to_all(growth.reshape(comp_local, spec_count, group_size), 'spec'...  57.9 us
    dot_general x4, matrix products, per_device(): jnp.einsum('kts,tps->ktp', windows[direction], selector, precision=lax.Pr...  40.9 us
    unnamed x28, local copies, waits for them, and re-layouts  16.2 us
    dot_general x1, matrix products, sources(): shifted = jnp.dot(pair_table, spectra, precision=lax.Precision.HIGHEST)  14 us
    mul x1, other arithmetic, per_device(): growth = advected * jnp.exp(0.08 * jnp.maximum(wind_drive, 0.0))  11 us
    all_to_all x1, starting transfers between devices, per_device(): lax.all_to_all(growth.reshape(comp_local, spec_count, group_size), 'spec'...  9.73 us
    all_to_all x1, other arithmetic, per_device(): lax.all_to_all(updated[:, None, :], 'spec', split_axis=0, concat_axis=1,...  8.15 us
  transfers between devices with their start and end apart: 3, of which 1 were waited for; matrix products, arithmetic and copies ran while one was open for 17% of the time, Pallas kernels for 0%

commit v1 on v0

v1 whole, which is shorter than its diff:
```python
import math
from functools import partial

import jax
import jax.numpy as jnp
import ml_dtypes
import numpy as np
from jax import lax
from jax.experimental import pallas as pl
from jax.experimental.pallas import tpu as pltpu
from jax.sharding import PartitionSpec as P

ND = 24
NF = 26
TILE = 128
K = 624
NT = 128
ROWS = 39
PAD = 40
CHIPS = 8
CHIP_ROWS = 78
N_SPACE = 16
N_SPEC = 16

LOG_RATIO = math.log(1.1)
FREQ_LOW = 0.05
EPS = 1e-06
PLUS_FACTOR = 1.0 / 1.25**4
MINUS_FACTOR = 1.0 / 0.75**4
CROSS_FACTOR = 1.0 / 0.9375**4

CHUNKS = (40, 40)
FIRST = CHUNKS[0] * TILE
SEA_TILES = sum(CHUNKS)

RELAY = 24
FAR = 8
PIECES = 6 * PAD + RELAY + FAR


def tables():
    k = np.arange(K)
    level = (k // ND).astype(np.float64)
    heading = ((k % ND) + 0.5) * (2.0 * math.pi / ND)
    frequency = FREQ_LOW * np.exp(LOG_RATIO * level)
    courant = 0.6 * np.exp(-LOG_RATIO * level)
    return frequency, heading, courant


FREQ = tables()[0]
MEAN_FREQ = float(FREQ.mean())


def component_params():
    frequency, heading, courant = tables()
    east = courant * np.cos(heading)
    north = courant * np.sin(heading)
    cols = (
        0.08 * frequency * np.cos(heading) / 1.56,
        0.08 * frequency * np.sin(heading) / 1.56,
        np.abs(east),
        np.abs(north),
        1.0 - np.abs(east) - np.abs(north),
        (east > 0).astype(np.float64),
        (north > 0).astype(np.float64),
        frequency,
    )
    out = np.zeros((N_SPEC, PAD, TILE), np.float32)
    for lane, col in enumerate(cols):
        out[:, :ROWS, lane] = col.reshape(N_SPEC, ROWS)
    return out


def interaction_table(dir_count, freq_count):
    comp_total = dir_count * freq_count
    matrix = np.zeros((2 * comp_total, comp_total), np.float32)
    shifts = (
        (math.log(1.25) / math.log(1.1), 33.56 * dir_count / 360.0),
        (math.log(0.75) / math.log(1.1), 11.48 * dir_count / 360.0),
    )
    for which_half, (band_shift, turning) in enumerate(shifts):
        for band_level in range(freq_count):
            band_place = band_level + band_shift
            low_band = math.floor(band_place)
            frac_band = band_place - low_band
            for mirror in (1.0, -1.0):
                for heading in range(dir_count):
                    dir_place = heading + mirror * turning
                    low_dir = math.floor(dir_place)
                    frac_dir = dir_place - low_dir
                    row_index = which_half * comp_total + band_level * dir_count + heading
                    for band_step, band_weight in ((0, 1.0 - frac_band), (1, frac_band)):
                        source_band = low_band + band_step
                        if 0 <= source_band < freq_count:
                            for dir_step, dir_weight in ((0, 1.0 - frac_dir), (1, frac_dir)):
                                source_dir = (low_dir + dir_step) % dir_count
                                matrix[row_index, source_band * dir_count + source_dir] += (
                                    0.5 * band_weight * dir_weight
                                )
    return matrix


def piece_columns(dev):
    chip, core = divmod(dev, 2)

    def rows(offset, which):
        first = ((chip + offset) % CHIPS) * CHIP_ROWS + ROWS * which
        return list(range(first, first + ROWS)) + [-1]

    cols = []
    for offset in (0, -1, 1):
        cols += rows(offset, core) + rows(offset, 1 - core)
    below = rows(-2, 1)
    turn = 6 * (chip % 4)
    cols += [below[21 - turn] if turn else -1, -1, -1, -1] + below[20:40]
    above = rows(2, 0)
    cols += [-1] + above[9:12] + above[3:6] + [-1]
    return cols


def interaction_weights():
    table = interaction_table(ND, NF)
    out = np.zeros((N_SPEC, 4 * PAD, PIECES), np.float32)
    for dev in range(N_SPEC):
        cols = np.array(piece_columns(dev))
        held = cols[cols >= 0]
        assert len(cols) == PIECES and len(set(held.tolist())) == len(held)
        for half, factor in ((0, PLUS_FACTOR), (1, MINUS_FACTOR)):
            for slot, owner in enumerate((dev, dev ^ 1)):
                want = table[half * K + ROWS * owner : half * K + ROWS * owner + ROWS]
                got = np.where(cols >= 0, want[:, np.maximum(cols, 0)], 0.0)
                assert np.array_equal((got != 0).sum(1), (want != 0).sum(1))
                at = half * 2 * PAD + slot * PAD
                out[dev, at : at + ROWS] = got * factor
    high = out.astype(ml_dtypes.bfloat16)
    low = (out - high.astype(np.float32)).astype(ml_dtypes.bfloat16)
    return np.concatenate([high, low], axis=1)


VMEM = pl.BlockSpec(memory_space=pltpu.VMEM)
SMEM = pl.BlockSpec(memory_space=pltpu.SMEM)
PARAMS = pltpu.CompilerParams(vmem_limit_bytes=48 * 1024 * 1024)


def lanes(tile):
    return pl.ds(pl.multiple_of(tile * TILE, TILE), TILE)


def gather(x, index):
    return jnp.take_along_axis(x, index, axis=1, mode="promise_in_bounds")


def edges_kernel(first_ref, last_ref, list_ref, low_ref, high_ref):
    for src, row, out in ((first_ref, 0, low_ref), (last_ref, 1, high_ref)):
        index = jnp.broadcast_to(list_ref[row : row + 1, :] & (TILE - 1), (PAD, TILE))
        out[...] = gather(src[...], index)


def edges(spectrum, send_list):
    return pl.pallas_call(
        edges_kernel,
        grid=(1,),
        in_specs=[
            pl.BlockSpec((PAD, TILE), lambda i: (0, 0)),
            pl.BlockSpec((PAD, TILE), lambda i: (0, NT - 1)),
            pl.BlockSpec((2, TILE), lambda i: (0, 0)),
        ],
        out_specs=[pl.BlockSpec((PAD, TILE), lambda i: (0, 0))] * 2,
        out_shape=[jax.ShapeDtypeStruct((PAD, TILE), jnp.float32)] * 2,
        name="edges",
    )(spectrum, spectrum, send_list.reshape(2, TILE))


def advect_kernel(first, last, base, tiles, *refs):
    if last:
        (dev_ref, counts_ref, state_ref, x_ref, code_ref, mask_ref, wa_ref, wb_ref, tab_ref, lower_ref, upper_ref,
         keep_ref, send_ref, par, dst) = refs
    else:
        (dev_ref, counts_ref, x_ref, code_ref, mask_ref, wa_ref, wb_ref, tab_ref,
         keep_ref, send_ref, next_ref, par, dst) = refs
    table = tab_ref[0]
    for i in range(7):
        par[i] = jnp.broadcast_to(table[:, i : i + 1], (PAD, TILE))
    real = lax.broadcasted_iota(jnp.int32, (PAD, TILE), 0) < ROWS
    lane = lax.broadcasted_iota(jnp.int32, (PAD, TILE), 1)

    def process(t, off, before, after):
        own = x_ref[:, lanes(t)]
        code = code_ref[:, lanes(t)] & (TILE - 1)
        sea = mask_ref[:, lanes(t)].astype(jnp.float32)
        to_east = par[5] > 0.5
        to_north = par[6] > 0.5
        near_x = gather(own, jnp.where(to_east, code[0:1], code[1:2]))
        near_x = near_x * jnp.where(to_east, sea[0:1], sea[1:2])
        near_y = gather(jnp.where(to_north, before, after), jnp.where(to_north, code[2:3], code[3:4]))
        near_y = near_y * jnp.where(to_north, sea[2:3], sea[3:4])
        value = own * par[4] + par[2] * near_x + par[3] * near_y
        drive = par[0] * wa_ref[pl.ds(t, 1), :] + par[1] * wb_ref[pl.ds(t, 1), :]
        value = value * jnp.exp(jnp.maximum(drive - 0.08, 0.0))
        value = jnp.where(real, value, 0.0)
        shift = off & (TILE - 1)
        at = (off >> 7) - base + 1
        value = pltpu.roll(value, shift, 1)
        dst[at] = jnp.where(lane < shift, dst[at], value)
        dst[at + 1] = value

    def inner(t, off):
        process(t, off, x_ref[:, lanes(t - 1)], x_ref[:, lanes(t + 1)])
        return off + counts_ref[t]

    limit = (base + tiles) * TILE
    if first:
        t0, off0 = jnp.int32(1), jnp.int32(0)
    else:
        t0, off0 = state_ref[0], state_ref[1]
    if last:
        _, off = lax.while_loop(
            lambda c: c[0] < NT - 1, lambda c: (c[0] + 1, inner(c[0], c[1])), (t0, off0)
        )
        off = jnp.maximum(off, FIRST)
        process(0, off, lower_ref[...], x_ref[:, lanes(1)])
        off = off + counts_ref[0]
        process(NT - 1, off, x_ref[:, lanes(NT - 2)], upper_ref[...])
    else:
        t, off, back = lax.while_loop(
            lambda c: (c[0] < NT - 1) & (c[1] < limit),
            lambda c: (c[0] + 1, inner(c[0], c[1]), c[1]),
            (t0, off0, off0),
        )
        straddles = off > limit
        next_ref[0] = jnp.where(straddles, t - 1, t)
        next_ref[1] = jnp.where(straddles, back, jnp.maximum(off, limit))
    half = tiles // 2
    core = dev_ref[0] & 1

    def emit(j, _):
        keep_ref[:, lanes(j)] = dst[1 + core * half + j]
        send_ref[:, lanes(j)] = dst[1 + (1 - core) * half + j]
        return 0

    lax.fori_loop(0, half, emit, 0)


def advect(first, last, base, tiles, dev, counts, state, spectrum, codes, mask, wa, wb, tab, lower, upper):
    half = tiles // 2 * TILE
    whole = lambda shape: pl.BlockSpec(shape, lambda i, d: (0,) * len(shape))
    tab_spec = pl.BlockSpec((1, PAD, TILE), lambda i, d: (d[0], 0, 0))
    args = [counts] + ([] if first else [state]) + [spectrum, codes, mask, wa, wb, tab]
    specs = [SMEM] + ([] if first else [SMEM])
    specs += [whole((PAD, NT * TILE)), whole((4, NT * TILE)), whole((4, NT * TILE)), whole((NT, TILE)), whole((NT, TILE)), tab_spec]
    outs = [jax.ShapeDtypeStruct((PAD, half), jnp.float32)] * 2
    out_specs = [whole((PAD, half))] * 2
    if last:
        args += [lower, upper]
        specs += [whole((PAD, TILE))] * 2
    else:
        outs = outs + [jax.ShapeDtypeStruct((2,), jnp.int32)]
        out_specs = out_specs + [SMEM]
    return pl.pallas_call(
        partial(advect_kernel, first, last, base, tiles),
        grid_spec=pltpu.PrefetchScalarGridSpec(
            num_scalar_prefetch=1,
            grid=(1,),
            in_specs=specs,
            out_specs=out_specs,
            scratch_shapes=[
                pltpu.VMEM((7, PAD, TILE), jnp.float32),
                pltpu.VMEM((tiles + 4, PAD, TILE), jnp.float32),
            ],
        ),
        out_shape=outs,
        compiler_params=PARAMS,
        name="advect",
    )(dev, *args)


def moments_kernel(dev_ref, mine_ref, other_ref, tab_a, tab_b, out_ref):
    mine, other = mine_ref[...], other_ref[...]
    fa, fb = tab_a[0][:, 7:8], tab_b[0][:, 7:8]
    out_ref[0:1, :] = jnp.sum(mine, axis=0, keepdims=True) + jnp.sum(other, axis=0, keepdims=True)
    out_ref[1:2, :] = jnp.sum(fa * mine, axis=0, keepdims=True) + jnp.sum(fb * other, axis=0, keepdims=True)


def tab_specs():
    return [
        pl.BlockSpec((1, PAD, TILE), lambda i, d: (d[0], 0, 0)),
        pl.BlockSpec((1, PAD, TILE), lambda i, d: (d[0] ^ 1, 0, 0)),
    ]


def moments(dev, mine, other, tab):
    n = mine.shape[1]
    return pl.pallas_call(
        moments_kernel,
        grid_spec=pltpu.PrefetchScalarGridSpec(
            num_scalar_prefetch=1,
            grid=(1,),
            in_specs=[pl.BlockSpec((PAD, n), lambda i, d: (0, 0))] * 2 + tab_specs(),
            out_specs=pl.BlockSpec((2, n), lambda i, d: (0, 0)),
        ),
        out_shape=jax.ShapeDtypeStruct((2, n), jnp.float32),
        compiler_params=PARAMS,
        name="moments",
    )(dev, mine, other, tab, tab)


def far_kernel(dev_ref, mine_ref, other_ref, sum_ref, got_ref, out_ref):
    core = dev_ref[0] & 1
    low = jnp.where(core == 0, mine_ref[...], other_ref[...])
    total = sum_ref[...] + got_ref[...]
    out_ref[0:1, :] = total[0:1]
    out_ref[1:4, :] = low[9:12]
    out_ref[4:7, :] = low[3:6]
    out_ref[7:8, :] = total[1:2]


def far_pack(dev, mine, other, sums, got):
    n = mine.shape[1]
    return pl.pallas_call(
        far_kernel,
        grid_spec=pltpu.PrefetchScalarGridSpec(
            num_scalar_prefetch=1,
            grid=(1,),
            in_specs=[pl.BlockSpec((16, n), lambda i, d: (0, 0))] * 2 + [pl.BlockSpec((2, n), lambda i, d: (0, 0))] * 2,
            out_specs=pl.BlockSpec((FAR, n), lambda i, d: (0, 0)),
        ),
        out_shape=jax.ShapeDtypeStruct((FAR, n), jnp.float32),
        compiler_params=PARAMS,
        name="far_pack",
    )(dev, mine, other, sums, got)


def relay_kernel(dev_ref, mine_ref, other_ref, sent_ref, got_ref, out_ref):
    core = dev_ref[0] & 1
    turn = ((dev_ref[0] >> 1) + 1) & 3
    rows = jnp.where(core == 1, mine_ref[...], other_ref[...])
    out_ref[...] = rows[16:40]
    out_ref[0:1, :] = jnp.where(turn == 1, rows[15:16], jnp.where(turn == 2, rows[9:10], rows[3:4]))
    out_ref[1:2, :] = sent_ref[0:1] + got_ref[0:1]
    out_ref[2:3, :] = sent_ref[7:8] + got_ref[7:8]


def relay_pack(dev, mine, other, sent, got):
    n = mine.shape[1]
    return pl.pallas_call(
        relay_kernel,
        grid_spec=pltpu.PrefetchScalarGridSpec(
            num_scalar_prefetch=1,
            grid=(1,),
            in_specs=[pl.BlockSpec((PAD, n), lambda i, d: (0, 0))] * 2 + [pl.BlockSpec((FAR, n), lambda i, d: (0, 0))] * 2,
            out_specs=pl.BlockSpec((RELAY, n), lambda i, d: (0, 0)),
        ),
        out_shape=jax.ShapeDtypeStruct((RELAY, n), jnp.float32),
        compiler_params=PARAMS,
        name="relay_pack",
    )(dev, mine, other, sent, got)


def sources_kernel(dev_ref, w_ref, tab_a, tab_b, sent_ref, *refs):
    pieces, (mine_out, other_out) = refs[:8], refs[8:]
    relay = pieces[6]
    stacked = jnp.concatenate([p[...] for p in pieces], axis=0)
    high = stacked.astype(jnp.bfloat16)
    low = (stacked - high.astype(jnp.float32)).astype(jnp.bfloat16)
    main = jnp.dot(w_ref[0], high, preferred_element_type=jnp.float32)
    rest = jnp.dot(w_ref[0, : 4 * PAD, :], low, preferred_element_type=jnp.float32)
    shifted = main[: 4 * PAD] + main[4 * PAD :] + rest
    energy_sum = (sent_ref[1:2, :] + relay[1:2, :]) * (1.0 / K) + EPS
    first_moment = ((sent_ref[2:3, :] + relay[2:3, :]) * (1.0 / K) + EPS * MEAN_FREQ) / energy_sum
    ratio = first_moment * (1.0 / MEAN_FREQ)
    ratio = ratio * ratio
    steepness = energy_sum * (ratio * ratio)
    inverse = 1.0 / first_moment
    fade = -0.3 * inverse * (steepness * steepness)
    gain = 0.05 * inverse
    cross = 2.0 * CROSS_FACTOR / (PLUS_FACTOR * MINUS_FACTOR)
    for at, tab, g_ref, out in ((0, tab_a, pieces[0], mine_out), (PAD, tab_b, pieces[1], other_out)):
        freq = tab[0][:, 7:8]
        g = g_ref[...]
        upper = shifted[at : at + PAD]
        lower = shifted[2 * PAD + at : 2 * PAD + at + PAD]
        out[...] = g * (jnp.exp(freq * fade) + (freq * gain) * (g * (upper + lower) - cross * (upper * lower)))


def sources(dev, weights, tab, sent, pieces, block):
    n = sent.shape[1]
    spec = lambda rows: pl.BlockSpec((rows, block), lambda i, d: (0, i))
    return pl.pallas_call(
        sources_kernel,
        grid_spec=pltpu.PrefetchScalarGridSpec(
            num_scalar_prefetch=1,
            grid=(n // block,),
            in_specs=[pl.BlockSpec((1, 8 * PAD, PIECES), lambda i, d: (d[0], 0, 0))]
            + tab_specs()
            + [spec(8)]
            + [spec(PAD)] * 6
            + [spec(RELAY), spec(FAR)],
            out_specs=[spec(PAD)] * 2,
        ),
        out_shape=[jax.ShapeDtypeStruct((PAD, n), jnp.float32)] * 2,
        compiler_params=PARAMS,
        name="sources",
    )(dev, weights, tab, tab, sent, *pieces)


def expand_kernel(dev_ref, counts_ref, *refs):
    count = 2 * len(CHUNKS)
    pieces, out_ref, held = refs[:count], refs[count], refs[count + 1]
    core = dev_ref[0] & 1
    base = 0
    for i, tiles in enumerate(CHUNKS):
        half = tiles // 2
        mine, other = pieces[2 * i], pieces[2 * i + 1]

        def fill(j, _, mine=mine, other=other, base=base, half=half):
            held[base + core * half + j] = mine[:, lanes(j)]
            held[base + (1 - core) * half + j] = other[:, lanes(j)]
            return 0

        lax.fori_loop(0, half, fill, 0)
        base += tiles
    lane = lax.broadcasted_iota(jnp.int32, (PAD, TILE), 1)

    def place(t, off):
        shift = off & (TILE - 1)
        at = off >> 7
        value = jnp.where(lane >= shift, held[at], held[at + 1])
        value = pltpu.roll(value, (TILE - shift) & (TILE - 1), 1)
        value = jnp.where(lane < counts_ref[t], value, 0.0)
        out_ref[:, lanes(t)] = value
        return off + counts_ref[t]

    off = lax.fori_loop(1, NT - 1, place, jnp.int32(0))
    off = jnp.maximum(off, FIRST)
    off = place(0, off)
    place(NT - 1, off)


def expand(dev, counts, pieces):
    whole = lambda shape: pl.BlockSpec(shape, lambda i, d: (0,) * len(shape))
    return pl.pallas_call(
        expand_kernel,
        grid_spec=pltpu.PrefetchScalarGridSpec(
            num_scalar_prefetch=1,
            grid=(1,),
            in_specs=[SMEM] + [whole(p.shape) for p in pieces],
            out_specs=whole((PAD, NT * TILE)),
            scratch_shapes=[pltpu.VMEM((SEA_TILES + 4, PAD, TILE), jnp.float32)],
        ),
        out_shape=jax.ShapeDtypeStruct((ROWS, NT * TILE), jnp.float32),
        compiler_params=PARAMS,
        name="expand",
    )(dev, counts, *pieces)


def per_device(spectrum, wind_speed, wind_dir, counts, send_list, neighbors, neighbor_mask):
    dev = lax.axis_index("spec").astype(jnp.int32).reshape(1)
    tab = jnp.asarray(component_params())
    weights = jnp.asarray(interaction_weights())

    def shift(x, hops):
        return lax.ppermute(x, "spec", [(s, (s + hops) % N_SPEC) for s in range(N_SPEC)])

    def swap(x):
        return lax.ppermute(x, "spec", [(s, s ^ 1) for s in range(N_SPEC)])

    to_lower, to_upper = edges(spectrum, send_list)
    lower = lax.ppermute(to_upper, "space", [(s, (s + 1) % N_SPACE) for s in range(N_SPACE)])
    upper = lax.ppermute(to_lower, "space", [(s, (s - 1) % N_SPACE) for s in range(N_SPACE)])
    wa = (wind_speed * jnp.cos(wind_dir)).reshape(NT, TILE)
    wb = (wind_speed * jnp.sin(wind_dir)).reshape(NT, TILE)

    results = []
    state = None
    base = 0
    for i, tiles in enumerate(CHUNKS):
        last = i == len(CHUNKS) - 1
        got = advect(i == 0, last, base, tiles, dev, counts, state, spectrum, neighbors, neighbor_mask, wa, wb, tab, lower, upper)
        base += tiles
        if last:
            mine, send = got
        else:
            mine, send, state = got
        other = swap(send)
        sums = moments(dev, mine, other, tab)
        far_sums = shift(sums, 8)
        up_mine, down_mine = shift(mine, 2), shift(mine, -2)
        up_other, down_other = shift(other, 2), shift(other, -2)
        sent_far = far_pack(dev, mine, other, sums, far_sums)
        far = shift(sent_far, -4)
        sent = relay_pack(dev, up_mine, up_other, sent_far, far)
        relay = shift(sent, 2)
        mine, other = sources(
            dev, weights, tab, sent, [mine, other, up_mine, up_other, down_mine, down_other, relay, far], 512
        )
        results += [mine, swap(other)]
    return expand(dev, counts, results)


def solution(mesh):
    in_specs = (
        P("spec", "space"),
        P("space"),
        P("space"),
        P("space"),
        P("space"),
        P(None, "space"),
        P(None, "space"),
    )
    out_specs = P("spec", "space")
    return jax.shard_map(
        per_device, mesh=mesh, in_specs=in_specs, out_specs=out_specs, check_vma=False
    )
```

time: 271 us -> 154 us (0.57); the launches traced: 267 us -> 154 us
  blocking collectives: 66.3 us -> 0 us
  matrix products: 54.9 us -> 0 us
  Pallas kernels: 0 us -> 48.1 us
  local copies, waits for them, and re-layouts: 40.2 us -> 7.17 us
  other arithmetic: 29.9 us -> 1.11 us
  starting transfers between devices: 15.6 us -> 40.7 us
    all_to_all x1 -> x0, blocking collectives: 66.3 us -> none  [per_device(): lax.all_to_all(updated[:, None, :], 'spec', split_axis=0, concat_axis=1,...]
    all_to_all x1 -> x0, waiting for transfers between devices: 57.9 us -> none  [per_device(): lax.all_to_all(growth.reshape(comp_local, spec_count, group_size), 'spec'...]
    ppermute x2 -> x20, waiting for transfers between devices: 0.01 us -> 57.2 us  [the longest x14 53 us: shift(): lax.ppermute(x, 'spec', [(s, (s + hops) % N_SPEC) for s in range(N_SPEC)])]
    dot_general x5 -> x0, matrix products: 54.9 us -> none  [the longest x4 40.9 us: per_device(): jnp.einsum('kts,tps->ktp', windows[direction], selector, precision=lax.Pr...]
    pallas_call x0 -> x12, Pallas kernels: none -> 48.1 us  [the longest x2 24.3 us: advect(): pl.pallas_call(partial(advect_kernel, first, last, base, tiles), grid_spe...]
    ppermute x2 -> x20, starting transfers between devices: 5.84 us -> 40.7 us  [the longest x14 15.7 us: shift(): lax.ppermute(x, 'spec', [(s, (s + hops) % N_SPEC) for s in range(N_SPEC)])]
    mul x6 -> x0, other arithmetic: 14.7 us -> none  [the longest x1 11 us: per_device(): growth = advected * jnp.exp(0.08 * jnp.maximum(wind_drive, 0.0))]
    all_to_all x1 -> x0, starting transfers between devices: 9.73 us -> none  [per_device(): lax.all_to_all(growth.reshape(comp_local, spec_count, group_size), 'spec'...]
  transfers between devices with their start and end apart: 3 -> 20, of which waited for: 1 -> 10; matrix products, arithmetic and copies ran while one was open for 17% -> 0% of each run, Pallas kernels for 0% -> 15%
where the time goes in v1:
time: 154 us
  waiting for transfers between devices  57.2 us (37%)
  Pallas kernels  48.1 us (31%)
  starting transfers between devices  40.7 us (26%)
  local copies, waits for them, and re-layouts  7.17 us (5%)
    ppermute x14, waiting for transfers between devices, shift(): lax.ppermute(x, 'spec', [(s, (s + hops) % N_SPEC) for s in range(N_SPEC)])  53 us
    pallas_call x2, Pallas kernels, advect(): pl.pallas_call(partial(advect_kernel, first, last, base, tiles), grid_spe...  24.3 us
    ppermute x14, starting transfers between devices, shift(): lax.ppermute(x, 'spec', [(s, (s + hops) % N_SPEC) for s in range(N_SPEC)])  15.7 us
    ppermute x4, starting transfers between devices, swap(): return lax.ppermute(x, 'spec', [(s, s ^ 1) for s in range(N_SPEC)])  14.9 us
    pallas_call x1, Pallas kernels, expand(): pl.pallas_call(expand_kernel, grid_spec=pltpu.PrefetchScalarGridSpec(num_...  11.9 us
    ppermute x1, starting transfers between devices, per_device(): lax.ppermute(to_upper, 'space', [(s, (s + 1) % N_SPACE) for s in range(N_...  10.2 us
    pallas_call x2, Pallas kernels, sources(): pl.pallas_call(sources_kernel, grid_spec=pltpu.PrefetchScalarGridSpec(num...  7.83 us
    unnamed x20, local copies, waits for them, and re-layouts  7.17 us
  transfers between devices with their start and end apart: 20, of which 10 were waited for; matrix products, arithmetic and copies ran while one was open for 0% of the time, Pallas kernels for 15%

profile of v1, /device:TPU:1, one launch (start us, length us, event | category | flops | bytes accessed | tf_op | source)
XLA Modules:
  0.0 154.4 jit_solution(7754762237498659937)
XLA Ops:
  0.0 1.1 multiply_bitcast_fusion
  1.1 0.0 copy-start
  1.1 1.7 %copy-done = f32[39,16384]{1,0:T(8,128)S(1)} copy-done((f32[39,16384]{1,0:T(8,128)S(1)}, f32[39,16384]{1,0:T(8,128)}, u32[]{:S(2)}) %copy-start) | copy-done | bytes 2555928
  2.9 1.0 copy-done.2
  3.8 0.9 copy-done.4
  4.8 0.9 copy-done.6
  5.7 0.7 copy-done.8
  6.4 12.5 %advect.2 = (f32[40,2560]{1,0:T(8,128)S(1)}, f32[40,2560]{1,0:T(8,128)}, s32[2]{0:T(128)S(1)}) custom-call(s32[1]{0:T(128)} %bitcast.refs_0_.dev_ref, s32[128]{0:T(128)S(1)} %copy-done.8, f32[39,16384]{1,0:T(8,128)S(1)} %copy-done, s32[4,16384]{1,0:T(4,128)S(1)} %copy-done.4, s32[4,16384]{1,0:T(4,128)S(1)} %copy-done.6, ...), custom_call_target="tpu_custom_call" | custom-call | tf_op jit(solution)/shard_map/advect/pallas_call | solution.py:259
  18.9 3.3 %collective-permute-start.1 = (f32[40,2560]{1,0:T(8,128)}, f32[40,2560]{1,0:T(8,128)}, u32[]{:S(2)}, u32[]{:S(2)}) collective-permute-start(f32[40,2560]{1,0:T(8,128)} %get-tuple-element.17), channel_id=1, source_target_pairs={{0,1},{1,0},{2,3},{3,2},{4,5},{5,4},{6,7},{7,6},{8,9},{9,8},{10,11... | collective-permute-start | bytes 1228808 | tf_op jit(solution)/shard_map/ppermute | solution.py:465
  22.3 1.6 %edges.1 = (f32[40,128]{1,0:T(8,128)}, f32[40,128]{1,0:T(8,128)}) custom-call(f32[39,16384]{1,0:T(8,128)} %refs_3_.3, f32[39,16384]{1,0:T(8,128)} %refs_3_.3, s32[2,128]{1,0:T(2,128)} %bitcast.6), custom_call_target="tpu_custom_call" | custom-call | tf_op jit(solution)/shard_map/edges/pallas_call | solution.py:160
  23.9 10.2 %collective-permute-start.9 = (f32[40,128]{1,0:T(8,128)}, f32[40,128]{1,0:T(8,128)S(1)}, u32[]{:S(2)}, u32[]{:S(2)}) collective-permute-start(f32[40,128]{1,0:T(8,128)} %get-tuple-element.21), channel_id=1, source_target_pairs={{0,16},{16,32},{32,48},{48,64},{64,80},{80,96},{96,112},{112,128},... | collective-permute-start | bytes 61448 | tf_op jit(solution)/shard_map/ppermute | solution.py:468
  34.0 0.0 collective-permute-start.10
  34.0 1.1 collective-permute-done.9.refs_9_
  35.2 1.7 %collective-permute-done.10.refs_10_ = f32[40,128]{1,0:T(8,128)S(1)} collective-permute-done((f32[40,128]{1,0:T(8,128)}, f32[40,128]{1,0:T(8,128)S(1)}, u32[]{:S(2)}, u32[]{:S(2)}) %collective-permute-start.10) | collective-permute-done | bytes 20512 | tf_op jit(solution)/shard_map/ppermute | solution.py:469
  36.9 0.0 copy-done.1
  36.9 0.0 copy-done.3
  36.9 0.0 copy-done.9
  36.9 0.0 copy-start.5
  36.9 0.9 copy-done.5
  37.9 0.9 copy-done.7
  38.8 11.8 %advect.3 = (f32[40,2560]{1,0:T(8,128)S(1)}, f32[40,2560]{1,0:T(8,128)S(1)}) custom-call(s32[1]{0:T(128)} %bitcast.refs_0_.dev_ref, s32[128]{0:T(128)S(1)} %copy-done.9, s32[2]{0:T(128)S(1)} %get-tuple-element.20.refs_2_, f32[39,16384]{1,0:T(8,128)S(1)} %copy-done.1, s32[4,16384]{1,0:T(4,128)S(1)} %copy-done.5, s32[4,16384]{1,0:T(4,128)S(1)} %copy-done.7, ...), custom_call_target="tpu_custom_call" | custom-call | tf_op jit(solution)/shard_map/advect/pallas_call | solution.py:259
  50.6 1.6 %collective-permute-start.12 = (f32[40,2560]{1,0:T(8,128)S(1)}, f32[40,2560]{1,0:T(8,128)S(1)}, u32[]{:S(2)}, u32[]{:S(2)}) collective-permute-start(f32[40,2560]{1,0:T(8,128)S(1)} %get-tuple-element.24), channel_id=1, source_target_pairs={{0,1},{1,0},{2,3},{3,2},{4,5},{5,4},{6,7},{7,6},{8,9},{9,8},{10,11... | collective-permute-start | bytes 1228808 | tf_op jit(solution)/shard_map/ppermute | solution.py:465
  52.2 1.7 %collective-permute-start = (f32[40,2560]{1,0:T(8,128)S(1)}, f32[40,2560]{1,0:T(8,128)S(1)}, u32[]{:S(2)}, u32[]{:S(2)}) collective-permute-start(f32[40,2560]{1,0:T(8,128)S(1)} %get-tuple-element.16.mine_ref.refs_0_), channel_id=1, source_target_pairs={{0,2},{1,3},{2,4},{3,5},{4,6},{5,7},{6,8},{7,9},{8,10},{9,11},{10,... | collective-permute-start | bytes 1228808 | tf_op jit(solution)/shard_map/ppermute | solution.py:462
  53.8 1.6 %collective-permute-start.11 = (f32[40,2560]{1,0:T(8,128)S(1)}, f32[40,2560]{1,0:T(8,128)S(1)}, u32[]{:S(2)}, u32[]{:S(2)}) collective-permute-start(f32[40,2560]{1,0:T(8,128)S(1)} %get-tuple-element.23.mine_ref.refs_0_), channel_id=1, source_target_pairs={{0,2},{1,3},{2,4},{3,5},{4,6},{5,7},{6,8},{7,9},{8,10},{9,11},{10,... | collective-permute-start | bytes 1228808 | tf_op jit(solution)/shard_map/ppermute | solution.py:462
  55.5 0.0 collective-permute-done.1.other_ref.refs_1_
  55.5 1.6 %collective-permute-start.2 = (f32[40,2560]{1,0:T(8,128)}, f32[40,2560]{1,0:T(8,128)S(1)}, u32[]{:S(2)}, u32[]{:S(2)}) collective-permute-start(f32[40,2560]{1,0:T(8,128)} %collective-permute-done.1.other_ref.refs_1_), channel_id=1, source_target_pairs={{0,2},{1,3},{2,4},{3,5},{4,6},{5,7},{6,8},{7,9},{8,10},{9,11},{10,... | collective-permute-start | bytes 1228808 | tf_op jit(solution)/shard_map/ppermute | solution.py:462
  57.1 0.0 collective-permute-done.12.other_ref.refs_1_
  57.1 2.9 %collective-permute-start.13 = (f32[40,2560]{1,0:T(8,128)S(1)}, f32[40,2560]{1,0:T(8,128)S(1)}, u32[]{:S(2)}, u32[]{:S(2)}) collective-permute-start(f32[40,2560]{1,0:T(8,128)S(1)} %collective-permute-done.12.other_ref.refs_1_), channel_id=1, source_target_pairs={{0,2},{1,3},{2,4},{3,5},{4,6},{5,7},{6,8},{7,9},{8,10},{9,11},{10,... | collective-permute-start | bytes 1228808 | tf_op jit(solution)/shard_map/ppermute | solution.py:462
  60.0 0.0 collective-permute-start.5
  60.0 1.2 moments.2.sum_ref
  61.1 6.4 %collective-permute-done.mine_ref.refs_2_ = f32[40,2560]{1,0:T(8,128)S(1)} collective-permute-done((f32[40,2560]{1,0:T(8,128)S(1)}, f32[40,2560]{1,0:T(8,128)S(1)}, u32[]{:S(2)}, u32[]{:S(2)}) %collective-permute-start) | collective-permute-done | bytes 409632 | tf_op jit(solution)/shard_map/ppermute | solution.py:462
  67.5 3.8 %collective-permute-start.3 = (f32[2,2560]{1,0:T(2,128)S(1)}, f32[2,2560]{1,0:T(2,128)S(1)}, u32[]{:S(2)}, u32[]{:S(2)}) collective-permute-start(f32[2,2560]{1,0:T(2,128)S(1)} %moments.2.sum_ref), channel_id=1, source_target_pairs={{0,8},{1,9},{2,10},{3,11},{4,12},{5,13},{6,14},{7,15},{8,0},{9,1},... | collective-permute-start | bytes 61448 | tf_op jit(solution)/shard_map/ppermute | solution.py:462
  71.3 0.2 moments.3.sum_ref
  71.5 24.4 %collective-permute-done.3.got_ref = f32[2,2560]{1,0:T(2,128)S(1)} collective-permute-done((f32[2,2560]{1,0:T(2,128)S(1)}, f32[2,2560]{1,0:T(2,128)S(1)}, u32[]{:S(2)}, u32[]{:S(2)}) %collective-permute-start.3) | collective-permute-done | bytes 20512 | tf_op jit(solution)/shard_map/ppermute | solution.py:462
  95.9 0.0 collective-permute-start.14
  95.9 0.9 far_pack.2.sent_ref
  96.8 5.6 %collective-permute-done.14.got_ref = f32[2,2560]{1,0:T(2,128)S(1)} collective-permute-done((f32[2,2560]{1,0:T(2,128)S(1)}, f32[2,2560]{1,0:T(2,128)S(1)}, u32[]{:S(2)}, u32[]{:S(2)}) %collective-permute-start.14) | collective-permute-done | bytes 20512 | tf_op jit(solution)/shard_map/ppermute | solution.py:462
  102.4 0.7 collective-permute-start.4
  103.2 0.0 collective-permute-done.11.mine_ref.refs_2_
  103.2 0.1 collective-permute-start.15
  103.3 3.3 %collective-permute-done.4.got_ref.refs_7_ = f32[8,2560]{1,0:T(8,128)S(1)} collective-permute-done((f32[8,2560]{1,0:T(8,128)S(1)}, f32[8,2560]{1,0:T(8,128)S(1)}, u32[]{:S(2)}, u32[]{:S(2)}) %collective-permute-start.4) | collective-permute-done | bytes 81952 | tf_op jit(solution)/shard_map/ppermute | solution.py:462
  106.6 0.0 collective-permute-start.6
  106.6 0.9 collective-permute-done.15.got_ref.refs_7_
  107.5 1.3 collective-permute-start.16
  108.8 0.0 collective-permute-done.2.other_ref.refs_3_
  108.8 0.9 collective-permute-start.17
  109.7 0.1 relay_pack.2.sent_ref
  109.7 0.0 collective-permute-done.13.other_ref.refs_3_
  109.8 0.7 collective-permute-start.7
  110.4 0.1 relay_pack.3.sent_ref
  110.5 0.0 collective-permute-done.5.refs_4_
  110.5 0.4 collective-permute-start.18
  110.9 5.7 %collective-permute-done.6.refs_5_ = f32[40,2560]{1,0:T(8,128)S(1)} collective-permute-done((f32[40,2560]{1,0:T(8,128)}, f32[40,2560]{1,0:T(8,128)S(1)}, u32[]{:S(2)}, u32[]{:S(2)}) %collective-permute-start.6) | collective-permute-done | bytes 409632 | tf_op jit(solution)/shard_map/ppermute | solution.py:462
  116.5 0.0 collective-permute-done.7.refs_6_
  116.6 4.3 %sources.2 = (f32[40,2560]{1,0:T(8,128)S(1)}, f32[40,2560]{1,0:T(8,128)S(1)}) custom-call(s32[1]{0:T(128)} %bitcast.refs_0_.dev_ref, bf16[16,320,272]{2,1,0:T(8,128)(2,1)} %constant.9.clone.w_ref, f32[16,40,128]{2,1,0:T(8,128)S(1)} %copy-done.3, f32[16,40,128]{2,1,0:T(8,128)S(1)} %copy-done.3, f32[24,2560]{1,0:T(8,128)S(1)} %relay_pack.2.sent_ref, ...), custom_call_target="tpu_custom_call" | custom-call | tf_op jit(solution)/shard_map/sources/pallas_call | solution.py:388
  120.8 6.5 %collective-permute-start.8 = (f32[40,2560]{1,0:T(8,128)S(1)}, f32[40,2560]{1,0:T(8,128)S(1)}, u32[]{:S(2)}, u32[]{:S(2)}) collective-permute-start(f32[40,2560]{1,0:T(8,128)S(1)} %get-tuple-element.19), channel_id=1, source_target_pairs={{0,1},{1,0},{2,3},{3,2},{4,5},{5,4},{6,7},{7,6},{8,9},{9,8},{10,11... | collective-permute-start | bytes 1228808 | tf_op jit(solution)/shard_map/ppermute | solution.py:465
  127.3 0.0 collective-permute-done.16.refs_4_
  127.3 6.8 %collective-permute-done.17.refs_5_ = f32[40,2560]{1,0:T(8,128)S(1)} collective-permute-done((f32[40,2560]{1,0:T(8,128)S(1)}, f32[40,2560]{1,0:T(8,128)S(1)}, u32[]{:S(2)}, u32[]{:S(2)}) %collective-permute-start.17) | collective-permute-done | bytes 409632 | tf_op jit(solution)/shard_map/ppermute | solution.py:462
  134.1 0.0 collective-permute-done.18.refs_6_
  134.1 3.6 %sources.3 = (f32[40,2560]{1,0:T(8,128)S(1)}, f32[40,2560]{1,0:T(8,128)S(1)}) custom-call(s32[1]{0:T(128)} %bitcast.refs_0_.dev_ref, bf16[16,320,272]{2,1,0:T(8,128)(2,1)} %constant.9.clone.w_ref, f32[16,40,128]{2,1,0:T(8,128)S(1)} %copy-done.3, f32[16,40,128]{2,1,0:T(8,128)S(1)} %copy-done.3, f32[24,2560]{1,0:T(8,128)S(1)} %relay_pack.3.sent_ref, ...), custom_call_target="tpu_custom_call" | custom-call | tf_op jit(solution)/shard_map/sources/pallas_call | solution.py:388
  137.7 3.5 %collective-permute-start.19 = (f32[40,2560]{1,0:T(8,128)S(1)}, f32[40,2560]{1,0:T(8,128)S(1)}, u32[]{:S(2)}, u32[]{:S(2)}) collective-permute-start(f32[40,2560]{1,0:T(8,128)S(1)} %get-tuple-element.26), channel_id=1, source_target_pairs={{0,1},{1,0},{2,3},{3,2},{4,5},{5,4},{6,7},{7,6},{8,9},{9,8},{10,11... | collective-permute-start | bytes 1228808 | tf_op jit(solution)/shard_map/ppermute | solution.py:465
  141.2 0.0 collective-permute-done.8.refs_1_
  141.2 1.4 collective-permute-done.19.refs_3_
  142.5 11.9 %expand.1 = f32[39,16384]{1,0:T(8,128)} custom-call(s32[1]{0:T(128)} %bitcast.refs_0_.dev_ref, s32[128]{0:T(128)S(1)} %copy-done.9, f32[40,2560]{1,0:T(8,128)S(1)} %get-tuple-element.18.refs_0_, f32[40,2560]{1,0:T(8,128)S(1)} %collective-permute-done.8.refs_1_, f32[40,2560]{1,0:T(8,128)S(1)} %get-tuple-element.25.refs_2_, ...), custom_call_target="tpu_custom_call" | custom-call | tf_op jit(solution)/shard_map/expand/pallas_call | solution.py:441
  (9 shorter events, 0.0 us)
Async XLA Ops:
  1.1 1.7 %copy-start = (f32[39,16384]{1,0:T(8,128)S(1)}, f32[39,16384]{1,0:T(8,128)}, u32[]{:S(2)}) copy-start(f32[39,16384]{1,0:T(8,128)} %refs_3_.3) | copy-start | bytes 7667716
  2.9 1.0 copy-start.2
  3.8 0.9 copy-start.4
  4.8 0.9 copy-start.6
  5.7 0.7 copy-start.8
  18.9 36.5 %collective-permute-start.1 = (f32[40,2560]{1,0:T(8,128)}, f32[40,2560]{1,0:T(8,128)}, u32[]{:S(2)}, u32[]{:S(2)}) collective-permute-start(f32[40,2560]{1,0:T(8,128)} %get-tuple-element.17), channel_id=1, source_target_pairs={{0,1},{1,0},{2,3},{3,2},{4,5},{5,4},{6,7},{7,6},{8,9},{9,8},{10,11... | collective-permute-start | bytes 1228808 | tf_op jit(solution)/shard_map/ppermute | solution.py:465
  22.3 14.6 %copy-start.1 = (f32[39,16384]{1,0:T(8,128)S(1)}, f32[39,16384]{1,0:T(8,128)}, u32[]{:S(2)}) copy-start(f32[39,16384]{1,0:T(8,128)} %refs_3_.3) | copy-start | bytes 7667716
  22.3 14.6 %copy-start.3 = (f32[16,40,128]{2,1,0:T(8,128)S(1)}, f32[16,40,128]{2,1,0:T(8,128)}, u32[]{:S(2)}) copy-start(f32[16,40,128]{2,1,0:T(8,128)} %constant.8.clone.refs_7_.tab_a.tab_b.refs_8_) | copy-start | bytes 983044
  22.3 14.6 %copy-start.9 = (s32[128]{0:T(128)S(1)}, s32[128]{0:T(128)}, u32[]{:S(2)}) copy-start(s32[128]{0:T(128)} %counts_ref.1) | copy-start | bytes 1540
  23.9 11.3 %collective-permute-start.9 = (f32[40,128]{1,0:T(8,128)}, f32[40,128]{1,0:T(8,128)S(1)}, u32[]{:S(2)}, u32[]{:S(2)}) collective-permute-start(f32[40,128]{1,0:T(8,128)} %get-tuple-element.21), channel_id=1, source_target_pairs={{0,16},{16,32},{32,48},{48,64},{64,80},{80,96},{96,112},{112,128},... | collective-permute-start | bytes 61448 | tf_op jit(solution)/shard_map/ppermute | solution.py:468
  34.0 2.8 %collective-permute-start.10 = (f32[40,128]{1,0:T(8,128)}, f32[40,128]{1,0:T(8,128)S(1)}, u32[]{:S(2)}, u32[]{:S(2)}) collective-permute-start(f32[40,128]{1,0:T(8,128)} %get-tuple-element.22), channel_id=1, source_target_pairs={{0,240},{16,0},{32,16},{48,32},{64,48},{80,64},{96,80},{112,96},{1... | collective-permute-start | bytes 61448 | tf_op jit(solution)/shard_map/ppermute | solution.py:469
  36.9 1.0 copy-start.5
  37.9 0.9 copy-start.7
  50.6 6.5 %collective-permute-start.12 = (f32[40,2560]{1,0:T(8,128)S(1)}, f32[40,2560]{1,0:T(8,128)S(1)}, u32[]{:S(2)}, u32[]{:S(2)}) collective-permute-start(f32[40,2560]{1,0:T(8,128)S(1)} %get-tuple-element.24), channel_id=1, source_target_pairs={{0,1},{1,0},{2,3},{3,2},{4,5},{5,4},{6,7},{7,6},{8,9},{9,8},{10,11... | collective-permute-start | bytes 1228808 | tf_op jit(solution)/shard_map/ppermute | solution.py:465
  52.2 15.3 %collective-permute-start = (f32[40,2560]{1,0:T(8,128)S(1)}, f32[40,2560]{1,0:T(8,128)S(1)}, u32[]{:S(2)}, u32[]{:S(2)}) collective-permute-start(f32[40,2560]{1,0:T(8,128)S(1)} %get-tuple-element.16.mine_ref.refs_0_), channel_id=1, source_target_pairs={{0,2},{1,3},{2,4},{3,5},{4,6},{5,7},{6,8},{7,9},{8,10},{9,11},{10,... | collective-permute-start | bytes 1228808 | tf_op jit(solution)/shard_map/ppermute | solution.py:462
  53.8 49.3 %collective-permute-start.11 = (f32[40,2560]{1,0:T(8,128)S(1)}, f32[40,2560]{1,0:T(8,128)S(1)}, u32[]{:S(2)}, u32[]{:S(2)}) collective-permute-start(f32[40,2560]{1,0:T(8,128)S(1)} %get-tuple-element.23.mine_ref.refs_0_), channel_id=1, source_target_pairs={{0,2},{1,3},{2,4},{3,5},{4,6},{5,7},{6,8},{7,9},{8,10},{9,11},{10,... | collective-permute-start | bytes 1228808 | tf_op jit(solution)/shard_map/ppermute | solution.py:462
  55.5 53.3 %collective-permute-start.2 = (f32[40,2560]{1,0:T(8,128)}, f32[40,2560]{1,0:T(8,128)S(1)}, u32[]{:S(2)}, u32[]{:S(2)}) collective-permute-start(f32[40,2560]{1,0:T(8,128)} %collective-permute-done.1.other_ref.refs_1_), channel_id=1, source_target_pairs={{0,2},{1,3},{2,4},{3,5},{4,6},{5,7},{6,8},{7,9},{8,10},{9,11},{10,... | collective-permute-start | bytes 1228808 | tf_op jit(solution)/shard_map/ppermute | solution.py:462
  57.1 52.6 %collective-permute-start.13 = (f32[40,2560]{1,0:T(8,128)S(1)}, f32[40,2560]{1,0:T(8,128)S(1)}, u32[]{:S(2)}, u32[]{:S(2)}) collective-permute-start(f32[40,2560]{1,0:T(8,128)S(1)} %collective-permute-done.12.other_ref.refs_1_), channel_id=1, source_target_pairs={{0,2},{1,3},{2,4},{3,5},{4,6},{5,7},{6,8},{7,9},{8,10},{9,11},{10,... | collective-permute-start | bytes 1228808 | tf_op jit(solution)/shard_map/ppermute | solution.py:462
  60.0 50.5 %collective-permute-start.5 = (f32[40,2560]{1,0:T(8,128)S(1)}, f32[40,2560]{1,0:T(8,128)S(1)}, u32[]{:S(2)}, u32[]{:S(2)}) collective-permute-start(f32[40,2560]{1,0:T(8,128)S(1)} %get-tuple-element.16.mine_ref.refs_0_), channel_id=1, source_target_pairs={{0,14},{1,15},{2,0},{3,1},{4,2},{5,3},{6,4},{7,5},{8,6},{9,7},{10,... | collective-permute-start | bytes 1228808 | tf_op jit(solution)/shard_map/ppermute | solution.py:462
  67.5 28.4 %collective-permute-start.3 = (f32[2,2560]{1,0:T(2,128)S(1)}, f32[2,2560]{1,0:T(2,128)S(1)}, u32[]{:S(2)}, u32[]{:S(2)}) collective-permute-start(f32[2,2560]{1,0:T(2,128)S(1)} %moments.2.sum_ref), channel_id=1, source_target_pairs={{0,8},{1,9},{2,10},{3,11},{4,12},{5,13},{6,14},{7,15},{8,0},{9,1},... | collective-permute-start | bytes 61448 | tf_op jit(solution)/shard_map/ppermute | solution.py:462
  95.9 6.5 %collective-permute-start.14 = (f32[2,2560]{1,0:T(2,128)S(1)}, f32[2,2560]{1,0:T(2,128)S(1)}, u32[]{:S(2)}, u32[]{:S(2)}) collective-permute-start(f32[2,2560]{1,0:T(2,128)S(1)} %moments.3.sum_ref), channel_id=1, source_target_pairs={{0,8},{1,9},{2,10},{3,11},{4,12},{5,13},{6,14},{7,15},{8,0},{9,1},... | collective-permute-start | bytes 61448 | tf_op jit(solution)/shard_map/ppermute | solution.py:462
  102.4 4.2 %collective-permute-start.4 = (f32[8,2560]{1,0:T(8,128)S(1)}, f32[8,2560]{1,0:T(8,128)S(1)}, u32[]{:S(2)}, u32[]{:S(2)}) collective-permute-start(f32[8,2560]{1,0:T(8,128)S(1)} %far_pack.2.sent_ref), channel_id=1, source_target_pairs={{0,12},{1,13},{2,14},{3,15},{4,0},{5,1},{6,2},{7,3},{8,4},{9,5},{1... | collective-permute-start | bytes 245768 | tf_op jit(solution)/shard_map/ppermute | solution.py:462
  103.2 4.3 %collective-permute-start.15 = (f32[8,2560]{1,0:T(8,128)S(1)}, f32[8,2560]{1,0:T(8,128)S(1)}, u32[]{:S(2)}, u32[]{:S(2)}) collective-permute-start(f32[8,2560]{1,0:T(8,128)S(1)} %far_pack.3.sent_ref), channel_id=1, source_target_pairs={{0,12},{1,13},{2,14},{3,15},{4,0},{5,1},{6,2},{7,3},{8,4},{9,5},{1... | collective-permute-start | bytes 245768 | tf_op jit(solution)/shard_map/ppermute | solution.py:462
  106.6 9.9 %collective-permute-start.6 = (f32[40,2560]{1,0:T(8,128)}, f32[40,2560]{1,0:T(8,128)S(1)}, u32[]{:S(2)}, u32[]{:S(2)}) collective-permute-start(f32[40,2560]{1,0:T(8,128)} %collective-permute-done.1.other_ref.refs_1_), channel_id=1, source_target_pairs={{0,14},{1,15},{2,0},{3,1},{4,2},{5,3},{6,4},{7,5},{8,6},{9,7},{10,... | collective-permute-start | bytes 1228808 | tf_op jit(solution)/shard_map/ppermute | solution.py:462
  107.5 19.8 %collective-permute-start.16 = (f32[40,2560]{1,0:T(8,128)S(1)}, f32[40,2560]{1,0:T(8,128)S(1)}, u32[]{:S(2)}, u32[]{:S(2)}) collective-permute-start(f32[40,2560]{1,0:T(8,128)S(1)} %get-tuple-element.23.mine_ref.refs_0_), channel_id=1, source_target_pairs={{0,14},{1,15},{2,0},{3,1},{4,2},{5,3},{6,4},{7,5},{8,6},{9,7},{10,... | collective-permute-start | bytes 1228808 | tf_op jit(solution)/shard_map/ppermute | solution.py:462
  108.8 25.3 %collective-permute-start.17 = (f32[40,2560]{1,0:T(8,128)S(1)}, f32[40,2560]{1,0:T(8,128)S(1)}, u32[]{:S(2)}, u32[]{:S(2)}) collective-permute-start(f32[40,2560]{1,0:T(8,128)S(1)} %collective-permute-done.12.other_ref.refs_1_), channel_id=1, source_target_pairs={{0,14},{1,15},{2,0},{3,1},{4,2},{5,3},{6,4},{7,5},{8,6},{9,7},{10,... | collective-permute-start | bytes 1228808 | tf_op jit(solution)/shard_map/ppermute | solution.py:462
  109.8 6.8 %collective-permute-start.7 = (f32[24,2560]{1,0:T(8,128)S(1)}, f32[24,2560]{1,0:T(8,128)S(1)}, u32[]{:S(2)}, u32[]{:S(2)}) collective-permute-start(f32[24,2560]{1,0:T(8,128)S(1)} %relay_pack.2.sent_ref), channel_id=1, source_target_pairs={{0,2},{1,3},{2,4},{3,5},{4,6},{5,7},{6,8},{7,9},{8,10},{9,11},{10,... | collective-permute-start | bytes 737288 | tf_op jit(solution)/shard_map/ppermute | solution.py:462
  110.5 23.6 %collective-permute-start.18 = (f32[24,2560]{1,0:T(8,128)S(1)}, f32[24,2560]{1,0:T(8,128)S(1)}, u32[]{:S(2)}, u32[]{:S(2)}) collective-permute-start(f32[24,2560]{1,0:T(8,128)S(1)} %relay_pack.3.sent_ref), channel_id=1, source_target_pairs={{0,2},{1,3},{2,4},{3,5},{4,6},{5,7},{6,8},{7,9},{8,10},{9,11},{10,... | collective-permute-start | bytes 737288 | tf_op jit(solution)/shard_map/ppermute | solution.py:462
  120.8 20.3 %collective-permute-start.8 = (f32[40,2560]{1,0:T(8,128)S(1)}, f32[40,2560]{1,0:T(8,128)S(1)}, u32[]{:S(2)}, u32[]{:S(2)}) collective-permute-start(f32[40,2560]{1,0:T(8,128)S(1)} %get-tuple-element.19), channel_id=1, source_target_pairs={{0,1},{1,0},{2,3},{3,2},{4,5},{5,4},{6,7},{7,6},{8,9},{9,8},{10,11... | collective-permute-start | bytes 1228808 | tf_op jit(solution)/shard_map/ppermute | solution.py:465
  137.7 4.9 %collective-permute-start.19 = (f32[40,2560]{1,0:T(8,128)S(1)}, f32[40,2560]{1,0:T(8,128)S(1)}, u32[]{:S(2)}, u32[]{:S(2)}) collective-permute-start(f32[40,2560]{1,0:T(8,128)S(1)} %get-tuple-element.26), channel_id=1, source_target_pairs={{0,1},{1,0},{2,3},{3,2},{4,5},{5,4},{6,7},{7,6},{8,9},{9,8},{10,11... | collective-permute-start | bytes 1228808 | tf_op jit(solution)/shard_map/ppermute | solution.py:465

commit v2 on v1

v2 whole, which is shorter than its diff:
```python
import math
from functools import partial

import jax
import jax.numpy as jnp
import ml_dtypes
import numpy as np
from jax import lax
from jax.experimental import pallas as pl
from jax.experimental.pallas import tpu as pltpu
from jax.sharding import PartitionSpec as P

ND = 24
NF = 26
TILE = 128
K = 624
NT = 128
ROWS = 39
PAD = 40
CHIPS = 8
CHIP_ROWS = 78
N_SPACE = 16
N_SPEC = 16

LOG_RATIO = math.log(1.1)
FREQ_LOW = 0.05
EPS = 1e-06
PLUS_FACTOR = 1.0 / 1.25**4
MINUS_FACTOR = 1.0 / 0.75**4
CROSS_FACTOR = 1.0 / 0.9375**4

CHUNKS = (40, 40)
FIRST = CHUNKS[0] * TILE
SEA_TILES = sum(CHUNKS)
BLOCK = 1280

RELAY = 24
FAR = 4
PIECES = 6 * PAD + RELAY + 8


def tables():
    k = np.arange(K)
    level = (k // ND).astype(np.float64)
    heading = ((k % ND) + 0.5) * (2.0 * math.pi / ND)
    frequency = FREQ_LOW * np.exp(LOG_RATIO * level)
    courant = 0.6 * np.exp(-LOG_RATIO * level)
    return frequency, heading, courant


FREQ = tables()[0]
MEAN_FREQ = float(FREQ.mean())


def component_params():
    frequency, heading, courant = tables()
    east = courant * np.cos(heading)
    north = courant * np.sin(heading)
    cols = (
        0.08 * frequency * np.cos(heading) / 1.56,
        0.08 * frequency * np.sin(heading) / 1.56,
        np.abs(east),
        np.abs(north),
        1.0 - np.abs(east) - np.abs(north),
        (east > 0).astype(np.float64),
        (north > 0).astype(np.float64),
        frequency,
    )
    out = np.zeros((N_SPEC, PAD, TILE), np.float32)
    for lane, col in enumerate(cols):
        out[:, :ROWS, lane] = col.reshape(N_SPEC, ROWS)
    out[:, :, 8] = np.roll(out[:, :, 7], 2, axis=0)
    out[:, :, 9] = np.roll(out[:, :, 7], -2, axis=0)
    return out


def interaction_table(dir_count, freq_count):
    comp_total = dir_count * freq_count
    matrix = np.zeros((2 * comp_total, comp_total), np.float32)
    shifts = (
        (math.log(1.25) / math.log(1.1), 33.56 * dir_count / 360.0),
        (math.log(0.75) / math.log(1.1), 11.48 * dir_count / 360.0),
    )
    for which_half, (band_shift, turning) in enumerate(shifts):
        for band_level in range(freq_count):
            band_place = band_level + band_shift
            low_band = math.floor(band_place)
            frac_band = band_place - low_band
            for mirror in (1.0, -1.0):
                for heading in range(dir_count):
                    dir_place = heading + mirror * turning
                    low_dir = math.floor(dir_place)
                    frac_dir = dir_place - low_dir
                    row_index = which_half * comp_total + band_level * dir_count + heading
                    for band_step, band_weight in ((0, 1.0 - frac_band), (1, frac_band)):
                        source_band = low_band + band_step
                        if 0 <= source_band < freq_count:
                            for dir_step, dir_weight in ((0, 1.0 - frac_dir), (1, frac_dir)):
                                source_dir = (low_dir + dir_step) % dir_count
                                matrix[row_index, source_band * dir_count + source_dir] += (
                                    0.5 * band_weight * dir_weight
                                )
    return matrix


def piece_columns(dev):
    chip, core = divmod(dev, 2)

    def rows(offset, which):
        first = ((chip + offset) % CHIPS) * CHIP_ROWS + ROWS * which
        return list(range(first, first + ROWS)) + [-1]

    cols = []
    for offset in (0, -1, 1):
        cols += rows(offset, core) + rows(offset, 1 - core)
    below = rows(-2, 1)
    turn = 6 * (chip % 4)
    cols += [below[21 - turn] if turn else -1, -1, -1, -1] + below[20:40]
    above = rows(2, 0)
    turn = 6 * ((chip + 1) % 4)
    cols += (above[9:12] if turn == 6 else above[3:6] if turn == 12 else [-1] * 3) + [-1] * 5
    return cols


def interaction_weights():
    table = interaction_table(ND, NF)
    out = np.zeros((N_SPEC, 4 * PAD, PIECES), np.float32)
    for dev in range(N_SPEC):
        cols = np.array(piece_columns(dev))
        held = cols[cols >= 0]
        assert len(cols) == PIECES and len(set(held.tolist())) == len(held)
        for half, factor in ((0, PLUS_FACTOR), (1, MINUS_FACTOR)):
            for slot, owner in enumerate((dev, dev ^ 1)):
                want = table[half * K + ROWS * owner : half * K + ROWS * owner + ROWS]
                got = np.where(cols >= 0, want[:, np.maximum(cols, 0)], 0.0)
                assert np.array_equal((got != 0).sum(1), (want != 0).sum(1))
                at = half * 2 * PAD + slot * PAD
                out[dev, at : at + ROWS] = got * factor
    high = out.astype(ml_dtypes.bfloat16)
    low = (out - high.astype(np.float32)).astype(ml_dtypes.bfloat16)
    return np.concatenate([high, low, high], axis=2)


VMEM = pl.BlockSpec(memory_space=pltpu.VMEM)
SMEM = pl.BlockSpec(memory_space=pltpu.SMEM)


def cost(us):
    return pl.CostEstimate(flops=0, bytes_accessed=int(us * 3.69e6), transcendentals=0)


PARAMS = pltpu.CompilerParams(vmem_limit_bytes=60 * 1024 * 1024)
SMALL = pltpu.CompilerParams(vmem_limit_bytes=24 * 1024 * 1024)


def lanes(tile):
    return pl.ds(pl.multiple_of(tile * TILE, TILE), TILE)


def gather(x, index):
    return jnp.take_along_axis(x, index, axis=1, mode="promise_in_bounds")


def edges_kernel(dev_ref, first_ref, last_ref, list_ref, speed_ref, dir_ref, tab_ref,
                 low_ref, high_ref, wa_ref, wb_ref, mine_ref, other_ref, sems):
    copies = [
        pltpu.make_async_copy(tab_ref.at[dev_ref[0]], mine_ref, sems.at[0]),
        pltpu.make_async_copy(tab_ref.at[dev_ref[0] ^ 1], other_ref, sems.at[1]),
    ]
    for copy in copies:
        copy.start()
    for src, row, out in ((first_ref, 0, low_ref), (last_ref, 1, high_ref)):
        index = jnp.broadcast_to(list_ref[row : row + 1, :] & (TILE - 1), (PAD, TILE))
        out[...] = gather(src[...], index)
    speed, turn = speed_ref[...], dir_ref[...]
    wa_ref[...] = speed * jnp.cos(turn)
    wb_ref[...] = speed * jnp.sin(turn)
    for copy in copies:
        copy.wait()


def edges(dev, spectrum, send_list, wind_speed, wind_dir, tab):
    whole = lambda rows: pl.BlockSpec((rows, TILE), lambda i, d: (0, 0))
    shape = lambda rows: jax.ShapeDtypeStruct((rows, TILE), jnp.float32)
    return pl.pallas_call(
        edges_kernel,
        grid_spec=pltpu.PrefetchScalarGridSpec(
            num_scalar_prefetch=1,
            grid=(1,),
            in_specs=[
                pl.BlockSpec((PAD, TILE), lambda i, d: (0, 0)),
                pl.BlockSpec((PAD, TILE), lambda i, d: (0, NT - 1)),
                whole(2),
                whole(NT),
                whole(NT),
                pl.BlockSpec(memory_space=pltpu.HBM),
            ],
            out_specs=[whole(PAD)] * 2 + [whole(NT)] * 2 + [whole(PAD)] * 2,
            scratch_shapes=[pltpu.SemaphoreType.DMA((2,))],
        ),
        out_shape=[shape(PAD)] * 2 + [shape(NT)] * 2 + [shape(PAD)] * 2,
        compiler_params=PARAMS,
        cost_estimate=cost(0),
        name="edges",
    )(dev, spectrum, spectrum, send_list.reshape(2, TILE), wind_speed.reshape(NT, TILE), wind_dir.reshape(NT, TILE), tab)


GROUP = 8
GROUPS = NT // GROUP
SEGMENTS = 8
SEG_TILES = NT // SEGMENTS
MARGIN = GROUP + 1


def advect_kernel(last, base, tiles, *refs):
    if last:
        (dev_ref, counts_ref, state_ref, x_hbm, code_hbm, mask_hbm, wa_ref, wb_ref, tab_ref, lower_ref, upper_ref, order_ref,
         keep_ref, send_ref, par, dst, x_ref, code_ref, mask_ref, sems) = refs
    else:
        (dev_ref, counts_ref, x_hbm, code_hbm, mask_hbm, wa_ref, wb_ref, tab_ref, order_ref,
         keep_ref, send_ref, next_ref, par, dst, x_ref, code_ref, mask_ref, sems) = refs

    def copies(seg):
        at = pl.ds(pl.multiple_of(seg * (SEG_TILES * TILE), SEG_TILES * TILE), SEG_TILES * TILE)
        return (
            pltpu.make_async_copy(x_hbm.at[:, at], x_ref.at[:, at], sems.at[seg, 0]),
            pltpu.make_async_copy(code_hbm.at[:, at], code_ref.at[:, at], sems.at[seg, 1]),
            pltpu.make_async_copy(mask_hbm.at[:, at], mask_ref.at[:, at], sems.at[seg, 2]),
        )

    def start(seg, _):
        for copy in copies(seg):
            copy.start()
        return 0

    def wait(seg, _):
        for copy in copies(seg):
            copy.wait()
        return 0

    if last:
        g0, off0 = state_ref[0], state_ref[1]
        seg0 = jnp.maximum(g0 * GROUP - 1, 0) // SEG_TILES
    else:
        g0, off0, seg0 = jnp.int32(0), jnp.int32(0), jnp.int32(0)
    lax.fori_loop(seg0, SEGMENTS, start, 0)
    if last:
        edge = [
            pltpu.make_async_copy(x_hbm.at[:, pl.ds(0, 2 * TILE)], x_ref.at[:, pl.ds(NT * TILE, 2 * TILE)], sems.at[SEGMENTS, 0]),
            pltpu.make_async_copy(code_hbm.at[:, pl.ds(0, TILE)], code_ref.at[:, pl.ds(NT * TILE, TILE)], sems.at[SEGMENTS, 1]),
            pltpu.make_async_copy(mask_hbm.at[:, pl.ds(0, TILE)], mask_ref.at[:, pl.ds(NT * TILE, TILE)], sems.at[SEGMENTS, 2]),
        ]
        for copy in edge:
            copy.start()

    table = tab_ref[...]
    for i in range(7):
        par[i] = jnp.broadcast_to(table[:ROWS, i : i + 1], (ROWS, TILE))
    lane = lax.broadcasted_iota(jnp.int32, (ROWS, TILE), 1)

    def grown(t, at, before, after):
        own = x_ref[:, at]
        code = code_ref[:, at] & (TILE - 1)
        sea = mask_ref[:, at].astype(jnp.float32)
        to_east = par[5] > 0.5
        to_north = par[6] > 0.5
        near_x = gather(own, jnp.where(to_east, code[0:1], code[1:2]))
        near_x = near_x * jnp.where(to_east, sea[0:1], sea[1:2])
        near_y = gather(jnp.where(to_north, before, after), jnp.where(to_north, code[2:3], code[3:4]))
        near_y = near_y * jnp.where(to_north, sea[2:3], sea[3:4])
        value = own * par[4] + par[2] * near_x + par[3] * near_y
        drive = par[0] * wa_ref[pl.ds(t, 1), :] + par[1] * wb_ref[pl.ds(t, 1), :]
        return value * jnp.exp(jnp.maximum(drive - 0.08, 0.0))

    def store(value, off):
        shift = off & (TILE - 1)
        at = (off >> 7) - base + MARGIN
        dst[at] = jnp.where(lane < shift, dst[at], value)
        dst[at + 1] = value

    def step(g, off):
        values, offs = [], []
        for i in range(GROUP):
            t = g * GROUP + i
            before = x_ref[:, lanes(jnp.maximum(t - 1, 0))]
            after = x_ref[:, lanes(jnp.minimum(t + 1, NT - 1))]
            value = grown(t, lanes(t), before, after)
            values.append(pltpu.roll(value, off & (TILE - 1), 1))
            offs.append(off)
            inner = counts_ref[t]
            if i == 0:
                inner = jnp.where(g == 0, 0, inner)
            if i == GROUP - 1:
                inner = jnp.where(g == GROUPS - 1, 0, inner)
            off = off + inner
        for value, at in zip(values, offs):
            store(value, at)
        return off

    limit = (base + tiles) * TILE

    def body(c):
        g, off, _, ready = c
        need = jnp.minimum((g * GROUP + GROUP) // SEG_TILES, SEGMENTS - 1) + 1
        lax.fori_loop(ready, need, wait, 0)
        return g + 1, step(g, off), off, jnp.maximum(ready, need)

    if last:
        more = lambda c: c[0] < GROUPS
    else:
        total = lax.fori_loop(0, NT, lambda t, n: n + counts_ref[t], jnp.int32(0), unroll=8)
        share, rest = GROUPS * tiles // SEA_TILES, (SEA_TILES - tiles) * TILE
        more = lambda c: (c[0] < GROUPS) & (c[1] < limit) & ((c[0] < share) | (total - c[1] > rest))
    g, off, back, ready = lax.while_loop(
        more,
        body,
        (g0, off0, off0, seg0),
    )
    lax.fori_loop(ready, SEGMENTS, wait, 0)
    if last:
        for copy in edge:
            copy.wait()
        off = jnp.maximum(off, FIRST)
        value = grown(0, pl.ds(NT * TILE, TILE), lower_ref[:ROWS, :], x_ref[:, pl.ds((NT + 1) * TILE, TILE)])
        store(pltpu.roll(value, off & (TILE - 1), 1), off)
        off = off + counts_ref[0]
        value = grown(NT - 1, lanes(NT - 1), x_ref[:, lanes(NT - 2)], upper_ref[:ROWS, :])
        store(pltpu.roll(value, off & (TILE - 1), 1), off)
    else:
        straddles = off > limit
        next_ref[0] = jnp.where(straddles, g - 1, g)
        next_ref[1] = jnp.where(straddles, back, jnp.maximum(off, limit))
    half = tiles // 2
    core = dev_ref[0] & 1

    def emit(j, _):
        keep_ref[:ROWS, lanes(j)] = dst[MARGIN + core * half + j]
        send_ref[:ROWS, lanes(j)] = dst[MARGIN + (1 - core) * half + j]
        return 0

    lax.fori_loop(0, half, emit, 0, unroll=2)
    for out in (keep_ref, send_ref):
        out[ROWS:PAD, :] = jnp.zeros((PAD - ROWS, out.shape[1]), jnp.float32)


def advect(last, base, tiles, dev, counts, state, spectrum, codes, mask, wa, wb, tab, extra):
    half = tiles // 2 * TILE
    whole = lambda shape: pl.BlockSpec(shape, lambda i, d: (0,) * len(shape))
    hbm = pl.BlockSpec(memory_space=pltpu.HBM)
    tab_spec = whole((PAD, TILE))
    args = [counts] + ([state] if last else []) + [spectrum, codes, mask, wa, wb, tab] + extra
    specs = [SMEM] + ([SMEM] if last else [])
    specs += [hbm, hbm, hbm, whole((NT, TILE)), whole((NT, TILE)), tab_spec]
    specs += ([whole((PAD, TILE))] * 2 if last else []) + [pl.BlockSpec(memory_space=pl.ANY)]
    outs = [jax.ShapeDtypeStruct((PAD, half), jnp.float32)] * 2
    out_specs = [whole((PAD, half))] * 2
    if not last:
        outs = outs + [jax.ShapeDtypeStruct((2,), jnp.int32)]
        out_specs = out_specs + [SMEM]
    return pl.pallas_call(
        partial(advect_kernel, last, base, tiles),
        grid_spec=pltpu.PrefetchScalarGridSpec(
            num_scalar_prefetch=1,
            grid=(1,),
            in_specs=specs,
            out_specs=out_specs,
            scratch_shapes=[
                pltpu.VMEM((7, ROWS, TILE), jnp.float32),
                pltpu.VMEM((tiles + 2 * MARGIN + 2, ROWS, TILE), jnp.float32),
                pltpu.VMEM((ROWS, (NT + 2) * TILE), jnp.float32),
                pltpu.VMEM((4, (NT + 2) * TILE), jnp.int32),
                pltpu.VMEM((4, (NT + 2) * TILE), jnp.int32),
                pltpu.SemaphoreType.DMA((SEGMENTS + 1, 3)),
            ],
        ),
        out_shape=outs,
        compiler_params=PARAMS,
        cost_estimate=cost(0),
        name="advect",
    )(dev, *args)


def join_kernel(mine_ref, other_ref, tab_a, tab_b, *refs):
    both_ref, out_ref = refs[-2:]
    mine, other = mine_ref[...], other_ref[...]
    both_ref[:PAD] = mine
    both_ref[PAD:] = other
    fa, fb = tab_a[:, 7:8], tab_b[:, 7:8]
    out_ref[0:1, :] = jnp.sum(mine, axis=0, keepdims=True) + jnp.sum(other, axis=0, keepdims=True)
    out_ref[1:2, :] = jnp.sum(fa * mine, axis=0, keepdims=True) + jnp.sum(fb * other, axis=0, keepdims=True)


def join(mine, other, tabs, after=()):
    n = mine.shape[1]
    return pl.pallas_call(
        join_kernel,
        in_specs=[VMEM] * 4 + [pl.BlockSpec(memory_space=pl.ANY)] * len(after),
        out_specs=[VMEM] * 2,
        out_shape=[jax.ShapeDtypeStruct((2 * PAD, n), jnp.float32), jax.ShapeDtypeStruct((2, n), jnp.float32)],
        compiler_params=SMALL,
        cost_estimate=cost(0),
        name="join",
    )(mine, other, *tabs, *after)


def windows_kernel(*refs):
    tm, to, three_ref, two_ref = refs[-4:]

    def sums(mine, other, lane):
        fa, fb = tm[:, lane : lane + 1], to[:, lane : lane + 1]
        return (
            jnp.sum(mine, axis=0, keepdims=True) + jnp.sum(other, axis=0, keepdims=True),
            jnp.sum(fa * mine, axis=0, keepdims=True) + jnp.sum(fb * other, axis=0, keepdims=True),
        )

    at = 0
    for j in range(0, len(refs) - 4, 4):
        own, um, uo, down = refs[j : j + 4]
        n = own.shape[1]
        below = sums(um[...], uo[...], 8)
        above = sums(down[:PAD], down[PAD:], 9)
        for i in range(2):
            two = own[i : i + 1, :] + above[i]
            two_ref[i : i + 1, at : at + n] = two
            three_ref[i : i + 1, at : at + n] = two + below[i]
        at += n


def moment_windows(chunks, tabs):
    args = [x for own, up, down in chunks for x in (own, *up, down)]
    total = sum(own.shape[1] for own, _, _ in chunks)
    return pl.pallas_call(
        windows_kernel,
        in_specs=[VMEM] * (len(args) + 2),
        out_specs=[VMEM] * 2,
        out_shape=[jax.ShapeDtypeStruct((2, total), jnp.float32)] * 2,
        compiler_params=SMALL,
        cost_estimate=cost(0),
        name="moment_windows",
    )(*args, *tabs)


def far_kernel(dev_ref, *refs):
    out_ref = refs[-1]
    core = dev_ref[0] & 1
    turn = ((dev_ref[0] >> 1) - 1) & 3

    def fill(parts):
        at = 0
        for low in parts:
            n = low.shape[1]
            out_ref[0:3, at : at + n] = jnp.where(turn == 1, low[9:12, :], low[3:6, :])
            out_ref[3:4, at : at + n] = jnp.zeros((1, n), jnp.float32)
            at += n

    @pl.when(core == 0)
    def _():
        fill(refs[0:-1:2])

    @pl.when(core == 1)
    def _():
        fill(refs[1:-1:2])


def far_pack(dev, *pairs):
    total = sum(p[0].shape[1] for p in pairs)
    whole = lambda shape: pl.BlockSpec(shape, lambda i, d: (0, 0))
    return pl.pallas_call(
        far_kernel,
        grid_spec=pltpu.PrefetchScalarGridSpec(
            num_scalar_prefetch=1,
            grid=(1,),
            in_specs=[whole((16, x.shape[1])) for pair in pairs for x in pair],
            out_specs=whole((FAR, total)),
        ),
        out_shape=jax.ShapeDtypeStruct((FAR, total), jnp.float32),
        compiler_params=SMALL,
        cost_estimate=cost(0),
        name="far_pack",
    )(dev, *[x for pair in pairs for x in pair])


def relay_kernel(dev_ref, mine_ref, other_ref, *refs):
    out_ref = refs[-1]
    core = dev_ref[0] & 1
    turn = ((dev_ref[0] >> 1) + 1) & 3

    def fill(rows):
        row = lambda i: rows[i : i + 1, :]
        out_ref[...] = rows[16:40, :]
        out_ref[0:1, :] = jnp.where(turn == 1, row(15), jnp.where(turn == 2, row(9), row(3)))

    @pl.when(core == 1)
    def _():
        fill(mine_ref)

    @pl.when(core == 0)
    def _():
        fill(other_ref)


def relay_pack(dev, up, after=()):
    n = up[0].shape[1]
    return pl.pallas_call(
        relay_kernel,
        grid_spec=pltpu.PrefetchScalarGridSpec(
            num_scalar_prefetch=1,
            grid=(1,),
            in_specs=[pl.BlockSpec(x.shape, lambda i, d: (0, 0)) for x in up]
            + [pl.BlockSpec(memory_space=pl.ANY)] * len(after),
            out_specs=pl.BlockSpec((RELAY, n), lambda i, d: (0, 0)),
        ),
        out_shape=jax.ShapeDtypeStruct((RELAY, n), jnp.float32),
        compiler_params=SMALL,
        cost_estimate=cost(0),
        name="relay_pack",
    )(dev, *up, *after)


def sources_kernel(dev_ref, w_ref, tab_a, tab_b, sum_a, sum_b, sum_c, *refs):
    pieces, (mine_out, other_out) = refs[:-2], refs[-2:]
    far = pieces[-1][...]
    stacked_in = jnp.concatenate([p[...] for p in pieces[:-1]] + [far, jnp.zeros_like(far)], axis=0)
    high = stacked_in.astype(jnp.bfloat16)
    low = (stacked_in - high.astype(jnp.float32)).astype(jnp.bfloat16)
    stacked = jnp.concatenate([high, high, low], axis=0)
    shifted = jnp.dot(w_ref[0], stacked, preferred_element_type=jnp.float32)
    energy_sum = (sum_a[0:1, :] + sum_b[0:1, :] + sum_c[0:1, :]) * (1.0 / K) + EPS
    first_moment = ((sum_a[1:2, :] + sum_b[1:2, :] + sum_c[1:2, :]) * (1.0 / K) + EPS * MEAN_FREQ) / energy_sum
    ratio = first_moment * (1.0 / MEAN_FREQ)
    ratio = ratio * ratio
    steepness = energy_sum * (ratio * ratio)
    inverse = 1.0 / first_moment
    fade = -0.3 * inverse * (steepness * steepness)
    gain = 0.05 * inverse
    cross = 2.0 * CROSS_FACTOR / (PLUS_FACTOR * MINUS_FACTOR)
    for at, tab, out in ((0, tab_a, mine_out), (PAD, tab_b, other_out)):
        freq = tab[:, 7:8]
        g = stacked_in[at : at + PAD]
        upper = shifted[at : at + PAD]
        lower = shifted[2 * PAD + at : 2 * PAD + at + PAD]
        out[...] = g * (jnp.exp(freq * fade) + (freq * gain) * (g * (upper + lower) - cross * (upper * lower)))


def sources(dev, weights, tabs, sums, pieces, far, start):
    n = pieces[0].shape[1]
    block = BLOCK
    skip = start // block
    spec = lambda rows: pl.BlockSpec((rows, block), lambda i, d: (0, i))
    wide = lambda rows: pl.BlockSpec((rows, block), lambda i, d: (0, i + skip))
    return pl.pallas_call(
        sources_kernel,
        grid_spec=pltpu.PrefetchScalarGridSpec(
            num_scalar_prefetch=1,
            grid=(n // block,),
            in_specs=[pl.BlockSpec((1, 4 * PAD, 3 * PIECES), lambda i, d: (d[0], 0, 0))]
            + [pl.BlockSpec((PAD, TILE), lambda i, d: (0, 0))] * 2
            + [wide(2)] * 3
            + [spec(p.shape[0]) for p in pieces]
            + [wide(FAR)],
            out_specs=[spec(PAD)] * 2,
        ),
        out_shape=[jax.ShapeDtypeStruct((PAD, n), jnp.float32)] * 2,
        compiler_params=SMALL,
        cost_estimate=cost(0),
        name="sources",
    )(dev, weights, *tabs, *sums, *pieces, far)


def expand_kernel(dev_ref, counts_ref, state_ref, *refs):
    count = 2 * len(CHUNKS)
    pieces = refs[:count]
    out_ref, held, room, sems = refs[count:]
    core = dev_ref[0] & 1
    base = 0
    for i, tiles in enumerate(CHUNKS):
        half = tiles // 2
        mine, other = pieces[2 * i], pieces[2 * i + 1]

        def fill(j, _, mine=mine, other=other, base=base, half=half):
            held[base + core * half + j] = mine[:, lanes(j)]
            held[base + (1 - core) * half + j] = other[:, lanes(j)]
            return 0

        lax.fori_loop(0, half, fill, 0, unroll=2)
        base += tiles
    lane = lax.broadcasted_iota(jnp.int32, (PAD, TILE), 1)

    def placed(t, off):
        shift = off & (TILE - 1)
        at = off >> 7
        value = jnp.where(lane >= shift, held[at], held[at + 1])
        value = pltpu.roll(value, (TILE - shift) & (TILE - 1), 1)
        return jnp.where(lane < counts_ref[t], value, 0.0)

    def copy(seg):
        at = pl.ds(pl.multiple_of(seg * (SEG_TILES * TILE), SEG_TILES * TILE), SEG_TILES * TILE)
        return pltpu.make_async_copy(room.at[:, at], out_ref.at[:, at], sems.at[seg])

    def step(g, off):
        values = []
        off = jnp.where(g == state_ref[0], state_ref[1], off)
        for i in range(GROUP):
            t = g * GROUP + i
            values.append(placed(t, off))
            inner = counts_ref[t]
            if i == 0:
                inner = jnp.where(g == 0, 0, inner)
            if i == GROUP - 1:
                inner = jnp.where(g == GROUPS - 1, 0, inner)
            off = off + inner
        for i, value in enumerate(values):
            room[:, lanes(g * GROUP + i)] = value[:ROWS]
        return off

    per = SEG_TILES // GROUP

    def segment(seg, off):
        off = lax.fori_loop(seg * per, seg * per + per, step, off)

        @pl.when((seg > 0) & (seg < SEGMENTS - 1))
        def _():
            copy(seg).start()

        return off

    off = lax.fori_loop(0, SEGMENTS, segment, jnp.int32(0))
    off = jnp.maximum(off, FIRST)
    room[:, lanes(0)] = placed(0, off)[:ROWS]
    copy(0).start()
    off = off + counts_ref[0]
    room[:, lanes(NT - 1)] = placed(NT - 1, off)[:ROWS]
    copy(SEGMENTS - 1).start()
    for seg in range(SEGMENTS):
        copy(seg).wait()


def expand(dev, counts, state, pieces):
    whole = lambda shape: pl.BlockSpec(shape, lambda i, d: (0,) * len(shape))
    return pl.pallas_call(
        expand_kernel,
        grid_spec=pltpu.PrefetchScalarGridSpec(
            num_scalar_prefetch=1,
            grid=(1,),
            in_specs=[SMEM, SMEM] + [whole(p.shape) for p in pieces],
            out_specs=pl.BlockSpec(memory_space=pltpu.HBM),
            scratch_shapes=[
                pltpu.VMEM((SEA_TILES + 4, PAD, TILE), jnp.float32),
                pltpu.VMEM((ROWS, NT * TILE), jnp.float32),
                pltpu.SemaphoreType.DMA((SEGMENTS,)),
            ],
        ),
        out_shape=jax.ShapeDtypeStruct((ROWS, NT * TILE), jnp.float32),
        compiler_params=SMALL,
        cost_estimate=cost(0),
        name="expand",
    )(dev, counts, state, *pieces)


def per_device(spectrum, wind_speed, wind_dir, counts, send_list, neighbors, neighbor_mask):
    dev = lax.axis_index("spec").astype(jnp.int32).reshape(1)
    tab = jnp.asarray(component_params())
    weights = jnp.asarray(interaction_weights())

    def shift(x, hops):
        return lax.ppermute(x, "spec", [(s, (s + hops) % N_SPEC) for s in range(N_SPEC)])

    def cross(x, hops):
        return lax.ppermute(x, "spec", [(s, ((s + hops) % N_SPEC) ^ 1) for s in range(N_SPEC)])

    def swap(x):
        return lax.ppermute(x, "spec", [(s, s ^ 1) for s in range(N_SPEC)])

    to_lower, to_upper, wa, wb, *tabs = edges(dev, spectrum, send_list, wind_speed, wind_dir, tab)
    lower = lax.ppermute(to_upper, "space", [(s, (s + 1) % N_SPACE) for s in range(N_SPACE)])
    upper = lax.ppermute(to_lower, "space", [(s, (s - 1) % N_SPACE) for s in range(N_SPACE)])

    mine, send, state = advect(
        False, 0, CHUNKS[0], dev, counts, None, spectrum, neighbors, neighbor_mask, wa, wb, tabs[0], [wa]
    )
    up1 = shift(mine, 2), cross(send, 2)
    own1 = mine, swap(send)
    both1, sums1 = join(*own1, tabs)
    down1 = shift(both1, -2)
    mine, send = advect(
        True, CHUNKS[0], CHUNKS[1], dev, counts, state, spectrum, neighbors, neighbor_mask, wa, wb, tabs[0],
        [lower, upper, sums1],
    )
    up2 = shift(mine, 2), cross(send, 2)
    own2 = mine, swap(send)
    both2, sums2 = join(*own2, tabs, up1)
    down2 = shift(both2, -2)
    far = shift(far_pack(dev, own1, own2), -4)
    three, two = moment_windows([(sums1, up1, down1), (sums2, up2, down2)], tabs)
    sums = three, shift(three, -6), shift(two, 6)
    relay1 = shift(relay_pack(dev, up1), 2)
    relay2 = shift(relay_pack(dev, up2, [far, three]), 2)
    results, start = [], 0
    for pieces in ([both1, *up1, down1, relay1], [both2, *up2, down2, relay2]):
        mine, other = sources(dev, weights, tabs, sums, pieces, far, start)
        start += mine.shape[1]
        results += [mine, swap(other)]
    return expand(dev, counts, state, results)


def solution(mesh):
    in_specs = (
        P("spec", "space"),
        P("space"),
        P("space"),
        P("space"),
        P("space"),
        P(None, "space"),
        P(None, "space"),
    )
    out_specs = P("spec", "space")
    return jax.shard_map(
        per_device, mesh=mesh, in_specs=in_specs, out_specs=out_specs, check_vma=False
    )
```

time: 154 us -> 94.8 us (0.62)
  Pallas kernels: 48.1 us -> 25 us
  waiting for transfers between devices: 57.2 us -> 37.9 us
  starting transfers between devices: 40.7 us -> 28.2 us
  local copies, waits for them, and re-layouts: 7.17 us -> 3.24 us
    ppermute x14 -> x9, waiting for transfers between devices: 53 us -> 26.9 us  [shift(): lax.ppermute(x, 'spec', [(s, (s + hops) % N_SPEC) for s in range(N_SPEC)])]
    ppermute x1, starting transfers between devices: 10.2 us -> 0.01 us  [per_device(): lax.ppermute(to_upper, 'space', [(s, (s + 1) % N_SPACE) for s in range(N_...]
    pallas_call x5 -> x6, Pallas kernels: 27.3 us -> 17.9 us  [the longest x2 14.4 us: advect(): pl.pallas_call(partial(advect_kernel, last, base, tiles), grid_spec=pltpu...]
    ppermute x0 -> x2, waiting for transfers between devices: none -> 9.22 us  [cross(): lax.ppermute(x, 'spec', [(s, (s + hops) % N_SPEC ^ 1) for s in range(N_SP...]
    ppermute x4, starting transfers between devices: 14.9 us -> 6.61 us  [swap(): return lax.ppermute(x, 'spec', [(s, s ^ 1) for s in range(N_SPEC)])]
    pallas_call x1, Pallas kernels: 11.9 us -> 3.75 us  [expand(): pl.pallas_call(expand_kernel, grid_spec=pltpu.PrefetchScalarGridSpec(num_...]
    ppermute x1, starting transfers between devices: 0.01 us -> 4.8 us  [per_device(): lax.ppermute(to_lower, 'space', [(s, (s - 1) % N_SPACE) for s in range(N_...]
    pallas_call x2, Pallas kernels: 7.83 us -> 3.27 us  [sources(): pl.pallas_call(sources_kernel, grid_spec=pltpu.PrefetchScalarGridSpec(num...]
  transfers between devices with their start and end apart: 20 -> 17, of which waited for: 10 -> 8; matrix products, arithmetic and copies ran while one was open for 0% -> 0% of each run, Pallas kernels for 15% -> 12%
where the time goes in v2:
time: 94.8 us; the launch traced here: 94.7 us
  waiting for transfers between devices  37.9 us (40%)
  starting transfers between devices  28.2 us (30%)
  Pallas kernels  25 us (26%)
  local copies, waits for them, and re-layouts  3.24 us (3%)
    ppermute x9, waiting for transfers between devices, shift(): lax.ppermute(x, 'spec', [(s, (s + hops) % N_SPEC) for s in range(N_SPEC)])  26.9 us
    ppermute x9, starting transfers between devices, shift(): lax.ppermute(x, 'spec', [(s, (s + hops) % N_SPEC) for s in range(N_SPEC)])  16.3 us
    pallas_call x2, Pallas kernels, advect(): pl.pallas_call(partial(advect_kernel, last, base, tiles), grid_spec=pltpu...  14.4 us
    ppermute x2, waiting for transfers between devices, cross(): lax.ppermute(x, 'spec', [(s, (s + hops) % N_SPEC ^ 1) for s in range(N_SP...  9.22 us
    ppermute x4, starting transfers between devices, swap(): return lax.ppermute(x, 'spec', [(s, s ^ 1) for s in range(N_SPEC)])  6.61 us
    ppermute x1, starting transfers between devices, per_device(): lax.ppermute(to_lower, 'space', [(s, (s - 1) % N_SPACE) for s in range(N_...  4.8 us
    pallas_call x1, Pallas kernels, expand(): pl.pallas_call(expand_kernel, grid_spec=pltpu.PrefetchScalarGridSpec(num_...  3.75 us
    pallas_call x2, Pallas kernels, sources(): pl.pallas_call(sources_kernel, grid_spec=pltpu.PrefetchScalarGridSpec(num...  3.27 us
  transfers between devices with their start and end apart: 17, of which 8 were waited for; matrix products, arithmetic and copies ran while one was open for 0% of the time, Pallas kernels for 12%

profile of v2, /device:TPU:1, one launch (start us, length us, event | category | flops | bytes accessed | tf_op | source)
XLA Modules:
  0.0 94.7 jit_solution(2248149737737396115)
XLA Ops:
  0.0 2.4 %edges.1 = (f32[40,128]{1,0:T(8,128)}, f32[40,128]{1,0:T(8,128)}, f32[128,128]{1,0:T(8,128)}, f32[128,128]{1,0:T(8,128)}, f32[40,128]{1,0:T(8,128)}, /*index=5*/f32[40,128]{1,0:T(8,128)}) custom-call(s32[1]{0:T(128)} %bitcast.dev_ref.refs_0_, f32[39,16384]{1,0:T(8,128)} %refs_3_.3, f32[39,16384]{1,0:T(8,128)} %refs_3_.3, s32[2,128]{1,0:T(2,128)} %bitcast.8, ...), custom_call_target="tpu_custom_call" | custom-call | tf_op jit(solution)/shard_map/edges/pallas_call | solution.py:185
  2.4 0.0 copy-start.13
  2.4 0.0 copy-start.12
  2.4 0.0 copy-start.3
  2.4 0.0 copy-start.5
  2.4 0.0 copy-start.4
  2.4 0.0 slice-start
  2.5 7.2 %advect.2 = (f32[40,2560]{1,0:T(8,128)}, f32[40,2560]{1,0:T(8,128)}, s32[2]{0:T(128)}) custom-call(s32[1]{0:T(128)} %bitcast.dev_ref.refs_0_, s32[128]{0:T(128)} %counts_ref.1, f32[39,16384]{1,0:T(8,128)} %refs_3_.3, s32[4,16384]{1,0:T(4,128)} %refs_4_.3, s32[4,16384]{1,0:T(4,128)} %refs_5_.1, f32[128,128]{1,0:T(8,128)} %get-tuple-element.26.refs_5_.refs_8_.refs_6_, ...), custom_call_target="tpu_custom_call" | custom-call | tf_op jit(solution)/shard_map/advect/pallas_call | solution.py:360
  9.7 3.3 %collective-permute-start = (f32[40,2560]{1,0:T(8,128)}, f32[40,2560]{1,0:T(8,128)S(1)}, u32[]{:S(2)}, u32[]{:S(2)}) collective-permute-start(f32[40,2560]{1,0:T(8,128)} %get-tuple-element.32), channel_id=1, source_target_pairs={{0,1},{1,0},{2,3},{3,2},{4,5},{5,4},{6,7},{7,6},{8,9},{9,8},{10,11... | collective-permute-start | bytes 1228808 | tf_op jit(solution)/shard_map/ppermute | solution.py:672
  13.0 0.0 copy-done.13
  13.0 0.0 collective-permute-start.4
  13.0 0.0 copy-done.12
  13.1 4.8 %collective-permute-start.5 = (f32[40,128]{1,0:T(8,128)S(1)}, f32[40,128]{1,0:T(8,128)S(1)}, u32[]{:S(2)}, u32[]{:S(2)}) collective-permute-start(f32[40,128]{1,0:T(8,128)S(1)} %copy-done.12), channel_id=1, source_target_pairs={{0,240},{16,0},{32,16},{48,32},{64,48},{80,64},{96,80},{112,96},{1... | collective-permute-start | bytes 61448 | tf_op jit(solution)/shard_map/ppermute | solution.py:676
  17.9 0.4 collective-permute-start.2
  18.3 1.6 %collective-permute-start.1 = (f32[40,2560]{1,0:T(8,128)}, f32[40,2560]{1,0:T(8,128)S(1)}, u32[]{:S(2)}, u32[]{:S(2)}) collective-permute-start(f32[40,2560]{1,0:T(8,128)} %get-tuple-element.31.mine_ref.refs_0_), channel_id=1, source_target_pairs={{0,2},{1,3},{2,4},{3,5},{4,6},{5,7},{6,8},{7,9},{8,10},{9,11},{10,... | collective-permute-start | bytes 1228808 | tf_op jit(solution)/shard_map/ppermute | solution.py:666
  19.9 0.0 collective-permute-done.other_ref.refs_1_
  19.9 0.0 copy-done.3
  19.9 0.0 copy-done.5
  19.9 0.0 copy-start
  19.9 1.0 %copy-done = f32[40,2560]{1,0:T(8,128)S(1)} copy-done((f32[40,2560]{1,0:T(8,128)S(1)}, f32[40,2560]{1,0:T(8,128)}, u32[]{:S(2)}) %copy-start) | copy-done | bytes 409624
  21.0 0.2 join.2
  21.2 0.0 copy-start.6
  21.2 0.6 copy-done.6
  21.8 0.0 collective-permute-done.4.refs_9_
  21.8 0.0 collective-permute-done.5.refs_10_
  21.8 0.0 copy-start.11
  21.8 0.6 copy-done.10
  22.4 0.0 copy-done.11
  22.4 7.1 %advect.3 = (f32[40,2560]{1,0:T(8,128)}, f32[40,2560]{1,0:T(8,128)}) custom-call(s32[1]{0:T(128)} %bitcast.dev_ref.refs_0_, s32[128]{0:T(128)} %counts_ref.1, s32[2]{0:T(128)} %get-tuple-element.29.refs_2_.state_ref, f32[39,16384]{1,0:T(8,128)} %refs_3_.3, s32[4,16384]{1,0:T(4,128)} %refs_4_.3, s32[4,16384]{1,0:T(4,128)} %refs_5_.1, ...), custom_call_target="tpu_custom_call" | custom-call | tf_op jit(solution)/shard_map/advect/pallas_call | solution.py:360
  29.5 0.2 collective-permute-start.6
  29.7 2.3 %collective-permute-start.3 = (f32[80,2560]{1,0:T(8,128)S(1)}, f32[80,2560]{1,0:T(8,128)S(1)}, u32[]{:S(2)}, u32[]{:S(2)}) collective-permute-start(f32[80,2560]{1,0:T(8,128)S(1)} %get-tuple-element.34.refs_0_), channel_id=1, source_target_pairs={{0,14},{1,15},{2,0},{3,1},{4,2},{5,3},{6,4},{7,5},{8,6},{9,7},{10,... | collective-permute-start | bytes 2457608 | tf_op jit(solution)/shard_map/ppermute | solution.py:666
  32.0 0.4 collective-permute-done.2.refs_1_.refs_2_.other_ref
  32.4 7.5 %collective-permute-done.1.refs_0_.refs_1_.mine_ref = f32[40,2560]{1,0:T(8,128)S(1)} collective-permute-done((f32[40,2560]{1,0:T(8,128)}, f32[40,2560]{1,0:T(8,128)S(1)}, u32[]{:S(2)}, u32[]{:S(2)}) %collective-permute-start.1) | collective-permute-done | bytes 409632 | tf_op jit(solution)/shard_map/ppermute | solution.py:666
  39.9 0.0 collective-permute-done.6.other_ref.refs_3_
  39.9 0.0 copy-done.4
  39.9 1.0 %copy-done.2 = f32[40,2560]{1,0:T(8,128)S(1)} copy-done((f32[40,2560]{1,0:T(8,128)S(1)}, f32[40,2560]{1,0:T(8,128)}, u32[]{:S(2)}) %copy-start.2) | copy-done | bytes 409624
  40.9 0.2 join.3
  41.1 2.8 %collective-permute-start.9 = (f32[80,2560]{1,0:T(8,128)S(1)}, f32[80,2560]{1,0:T(8,128)S(1)}, u32[]{:S(2)}, u32[]{:S(2)}) collective-permute-start(f32[80,2560]{1,0:T(8,128)S(1)} %get-tuple-element.40.refs_0_), channel_id=1, source_target_pairs={{0,14},{1,15},{2,0},{3,1},{4,2},{5,3},{6,4},{7,5},{8,6},{9,7},{10,... | collective-permute-start | bytes 2457608 | tf_op jit(solution)/shard_map/ppermute | solution.py:666
  43.9 0.1 collective-permute-start.8
  44.0 0.0 collective-permute-start.7
  44.1 4.5 %collective-permute-start.13 = (f32[4,5120]{1,0:T(4,128)S(1)}, f32[4,5120]{1,0:T(4,128)S(1)}, u32[]{:S(2)}, u32[]{:S(2)}) collective-permute-start(f32[4,5120]{1,0:T(4,128)S(1)} %far_pack.1), channel_id=1, source_target_pairs={{0,12},{1,13},{2,14},{3,15},{4,0},{5,1},{6,2},{7,3},{8,4},{9,5},{1... | collective-permute-start | bytes 245768 | tf_op jit(solution)/shard_map/ppermute | solution.py:666
  48.6 8.8 %collective-permute-done.8.refs_6_.other_ref.refs_2_ = f32[40,2560]{1,0:T(8,128)S(1)} collective-permute-done((f32[40,2560]{1,0:T(8,128)}, f32[40,2560]{1,0:T(8,128)S(1)}, u32[]{:S(2)}, u32[]{:S(2)}) %collective-permute-start.8) | collective-permute-done | bytes 409632 | tf_op jit(solution)/shard_map/ppermute | solution.py:669
  57.4 0.0 collective-permute-start.12
  57.4 8.8 %collective-permute-done.7.refs_5_.mine_ref.refs_1_ = f32[40,2560]{1,0:T(8,128)S(1)} collective-permute-done((f32[40,2560]{1,0:T(8,128)S(1)}, f32[40,2560]{1,0:T(8,128)S(1)}, u32[]{:S(2)}, u32[]{:S(2)}) %collective-permute-start.7) | collective-permute-done | bytes 409632 | tf_op jit(solution)/shard_map/ppermute | solution.py:666
  66.2 0.0 collective-permute-done.3.refs_3_
  66.2 2.5 %collective-permute-done.9.refs_7_.refs_3_ = f32[80,2560]{1,0:T(8,128)S(1)} collective-permute-done((f32[80,2560]{1,0:T(8,128)S(1)}, f32[80,2560]{1,0:T(8,128)S(1)}, u32[]{:S(2)}, u32[]{:S(2)}) %collective-permute-start.9) | collective-permute-done | bytes 819232 | tf_op jit(solution)/shard_map/ppermute | solution.py:666
  68.8 0.7 moment_windows.1
  69.5 2.9 %collective-permute-done.13.refs_5_.refs_0_ = f32[4,5120]{1,0:T(4,128)S(1)} collective-permute-done((f32[4,5120]{1,0:T(4,128)S(1)}, f32[4,5120]{1,0:T(4,128)S(1)}, u32[]{:S(2)}, u32[]{:S(2)}) %collective-permute-start.13) | collective-permute-done | bytes 81952 | tf_op jit(solution)/shard_map/ppermute | solution.py:666
  72.4 0.6 collective-permute-start.15
  73.0 3.4 %collective-permute-start.11 = (f32[2,5120]{1,0:T(2,128)S(1)}, f32[2,5120]{1,0:T(2,128)S(1)}, u32[]{:S(2)}, u32[]{:S(2)}) collective-permute-start(f32[2,5120]{1,0:T(2,128)S(1)} %get-tuple-element.42), channel_id=1, source_target_pairs={{0,6},{1,7},{2,8},{3,9},{4,10},{5,11},{6,12},{7,13},{8,14},{9,15},... | collective-permute-start | bytes 122888 | tf_op jit(solution)/shard_map/ppermute | solution.py:666
  76.4 1.1 %collective-permute-start.10 = (f32[2,5120]{1,0:T(2,128)S(1)}, f32[2,5120]{1,0:T(2,128)S(1)}, u32[]{:S(2)}, u32[]{:S(2)}) collective-permute-start(f32[2,5120]{1,0:T(2,128)S(1)} %get-tuple-element.41.sum_a.refs_1_), channel_id=1, source_target_pairs={{0,10},{1,11},{2,12},{3,13},{4,14},{5,15},{6,0},{7,1},{8,2},{9,3},... | collective-permute-start | bytes 122888 | tf_op jit(solution)/shard_map/ppermute | solution.py:666
  77.5 0.0 collective-permute-done.12.refs_4_
  77.5 5.1 %collective-permute-done.11.sum_c = f32[2,5120]{1,0:T(2,128)S(1)} collective-permute-done((f32[2,5120]{1,0:T(2,128)S(1)}, f32[2,5120]{1,0:T(2,128)S(1)}, u32[]{:S(2)}, u32[]{:S(2)}) %collective-permute-start.11) | collective-permute-done | bytes 40992 | tf_op jit(solution)/shard_map/ppermute | solution.py:666
  82.6 0.0 collective-permute-done.10.sum_b
  82.7 1.6 %sources.2 = (f32[40,2560]{1,0:T(8,128)S(1)}, f32[40,2560]{1,0:T(8,128)S(1)}) custom-call(s32[1]{0:T(128)} %bitcast.dev_ref.refs_0_, bf16[16,160,816]{2,1,0:T(8,128)(2,1)S(1)} %bitcast.5, f32[40,128]{1,0:T(8,128)S(1)} %copy-done.4, f32[40,128]{1,0:T(8,128)S(1)} %copy-done.5, f32[2,5120]{1,0:T(2,128)S(1)} %get-tuple-element.41.sum_a.refs_1_, ...), custom_call_target="tpu_custom_call" | custom-call | tf_op jit(solution)/shard_map/sources/pallas_call | solution.py:551
  84.3 0.0 copy-start.8
  84.3 3.0 %collective-permute-start.14 = (f32[40,2560]{1,0:T(8,128)S(1)}, f32[40,2560]{1,0:T(8,128)S(1)}, u32[]{:S(2)}, u32[]{:S(2)}) collective-permute-start(f32[40,2560]{1,0:T(8,128)S(1)} %get-tuple-element.44), channel_id=1, source_target_pairs={{0,1},{1,0},{2,3},{3,2},{4,5},{5,4},{6,7},{7,6},{8,9},{9,8},{10,11... | collective-permute-start | bytes 1228808 | tf_op jit(solution)/shard_map/ppermute | solution.py:672
  87.3 0.0 collective-permute-done.15.refs_4_
  87.3 1.6 %sources.3 = (f32[40,2560]{1,0:T(8,128)S(1)}, f32[40,2560]{1,0:T(8,128)S(1)}) custom-call(s32[1]{0:T(128)} %bitcast.dev_ref.refs_0_, bf16[16,160,816]{2,1,0:T(8,128)(2,1)S(1)} %bitcast.5, f32[40,128]{1,0:T(8,128)S(1)} %copy-done.4, f32[40,128]{1,0:T(8,128)S(1)} %copy-done.5, f32[2,5120]{1,0:T(2,128)S(1)} %get-tuple-element.41.sum_a.refs_1_, ...), custom_call_target="tpu_custom_call" | custom-call | tf_op jit(solution)/shard_map/sources/pallas_call | solution.py:551
  88.9 0.1 collective-permute-start.16
  89.0 0.0 collective-permute-done.14.refs_1_
  89.0 1.7 %collective-permute-done.16.refs_3_ = f32[40,2560]{1,0:T(8,128)S(1)} collective-permute-done((f32[40,2560]{1,0:T(8,128)S(1)}, f32[40,2560]{1,0:T(8,128)S(1)}, u32[]{:S(2)}, u32[]{:S(2)}) %collective-permute-start.16) | collective-permute-done | bytes 409632 | tf_op jit(solution)/shard_map/ppermute | solution.py:672
  90.8 0.0 copy-done.9
  90.8 3.8 %expand.1 = f32[39,16384]{1,0:T(8,128)} custom-call(s32[1]{0:T(128)} %bitcast.dev_ref.refs_0_, s32[128]{0:T(128)S(1)} %copy-done.8, s32[2]{0:T(128)S(1)} %copy-done.9, f32[40,2560]{1,0:T(8,128)S(1)} %get-tuple-element.43.refs_0_, f32[40,2560]{1,0:T(8,128)S(1)} %collective-permute-done.14.refs_1_, f32[40,2560]{1,0:T(8,128)S(1)} %get-tuple-element.45.refs_2_, ...), custom_call_target="tpu_custom_call" | custom-call | tf_op jit(solution)/shard_map/expand/pallas_call | solution.py:640
  (15 shorter events, 0.1 us)
Async XLA Ops:
  2.4 10.6 %copy-start.13 = (f32[40,128]{1,0:T(8,128)S(1)}, f32[40,128]{1,0:T(8,128)}, u32[]{:S(2)}) copy-start(f32[40,128]{1,0:T(8,128)} %get-tuple-element.35) | copy-start | bytes 61444
  2.4 10.6 %copy-start.12 = (f32[40,128]{1,0:T(8,128)S(1)}, f32[40,128]{1,0:T(8,128)}, u32[]{:S(2)}) copy-start(f32[40,128]{1,0:T(8,128)} %get-tuple-element.36) | copy-start | bytes 61444
  2.4 17.5 %copy-start.3 = (f32[40,128]{1,0:T(8,128)S(1)}, f32[40,128]{1,0:T(8,128)}, u32[]{:S(2)}) copy-start(f32[40,128]{1,0:T(8,128)} %get-tuple-element.28.refs_7_.tab_a.refs_8_) | copy-start | bytes 61444
  2.4 17.5 %copy-start.5 = (f32[40,128]{1,0:T(8,128)S(1)}, f32[40,128]{1,0:T(8,128)}, u32[]{:S(2)}) copy-start(f32[40,128]{1,0:T(8,128)} %get-tuple-element.30.tab_b.refs_9_) | copy-start | bytes 61444
  2.4 37.5 %copy-start.4 = (f32[40,128]{1,0:T(8,128)S(1)}, f32[40,128]{1,0:T(8,128)}, u32[]{:S(2)}) copy-start(f32[40,128]{1,0:T(8,128)} %get-tuple-element.28.refs_7_.tab_a.refs_8_) | copy-start | bytes 61444
  2.4 80.2 %slice-start = ((s8[4587520]{0:T(1024)(128)(4,1)}), s8[393216]{0:T(1024)(128)(4,1)S(1)}, s32[]{:S(2)}) async-start(s8[4587520]{0:T(1024)(128)(4,1)} %bitcast.4), calls=%async_computation | async-start | bytes 786432
  9.7 10.2 %collective-permute-start = (f32[40,2560]{1,0:T(8,128)}, f32[40,2560]{1,0:T(8,128)S(1)}, u32[]{:S(2)}, u32[]{:S(2)}) collective-permute-start(f32[40,2560]{1,0:T(8,128)} %get-tuple-element.32), channel_id=1, source_target_pairs={{0,1},{1,0},{2,3},{3,2},{4,5},{5,4},{6,7},{7,6},{8,9},{9,8},{10,11... | collective-permute-start | bytes 1228808 | tf_op jit(solution)/shard_map/ppermute | solution.py:672
  13.0 8.7 %collective-permute-start.4 = (f32[40,128]{1,0:T(8,128)S(1)}, f32[40,128]{1,0:T(8,128)S(1)}, u32[]{:S(2)}, u32[]{:S(2)}) collective-permute-start(f32[40,128]{1,0:T(8,128)S(1)} %copy-done.13), channel_id=1, source_target_pairs={{0,16},{16,32},{32,48},{48,64},{64,80},{80,96},{96,112},{112,128},... | collective-permute-start | bytes 61448 | tf_op jit(solution)/shard_map/ppermute | solution.py:675
  13.1 8.7 %collective-permute-start.5 = (f32[40,128]{1,0:T(8,128)S(1)}, f32[40,128]{1,0:T(8,128)S(1)}, u32[]{:S(2)}, u32[]{:S(2)}) collective-permute-start(f32[40,128]{1,0:T(8,128)S(1)} %copy-done.12), channel_id=1, source_target_pairs={{0,240},{16,0},{32,16},{48,32},{64,48},{80,64},{96,80},{112,96},{1... | collective-permute-start | bytes 61448 | tf_op jit(solution)/shard_map/ppermute | solution.py:676
  17.9 14.6 %collective-permute-start.2 = (f32[40,2560]{1,0:T(8,128)}, f32[40,2560]{1,0:T(8,128)S(1)}, u32[]{:S(2)}, u32[]{:S(2)}) collective-permute-start(f32[40,2560]{1,0:T(8,128)} %get-tuple-element.32), channel_id=1, source_target_pairs={{0,3},{1,2},{2,5},{3,4},{4,7},{5,6},{6,9},{7,8},{8,11},{9,10},{10,... | collective-permute-start | bytes 1228808 | tf_op jit(solution)/shard_map/ppermute | solution.py:669
  18.3 21.6 %collective-permute-start.1 = (f32[40,2560]{1,0:T(8,128)}, f32[40,2560]{1,0:T(8,128)S(1)}, u32[]{:S(2)}, u32[]{:S(2)}) collective-permute-start(f32[40,2560]{1,0:T(8,128)} %get-tuple-element.31.mine_ref.refs_0_), channel_id=1, source_target_pairs={{0,2},{1,3},{2,4},{3,5},{4,6},{5,7},{6,8},{7,9},{8,10},{9,11},{10,... | collective-permute-start | bytes 1228808 | tf_op jit(solution)/shard_map/ppermute | solution.py:666
  19.9 1.0 %copy-start = (f32[40,2560]{1,0:T(8,128)S(1)}, f32[40,2560]{1,0:T(8,128)}, u32[]{:S(2)}) copy-start(f32[40,2560]{1,0:T(8,128)} %get-tuple-element.31.mine_ref.refs_0_) | copy-start | bytes 1228804
  21.2 0.6 copy-start.6
  21.8 22.3 %copy-start.1 = (f32[40,2560]{1,0:T(8,128)S(1)}, f32[40,2560]{1,0:T(8,128)}, u32[]{:S(2)}) copy-start(f32[40,2560]{1,0:T(8,128)} %get-tuple-element.31.mine_ref.refs_0_) | copy-start | bytes 1228804
  21.8 0.6 copy-start.10
  21.8 0.6 copy-start.11
  22.4 46.4 %copy-start.7 = (f32[2,2560]{1,0:T(2,128)S(1)}, f32[2,2560]{1,0:T(2,128)}, u32[]{:S(2)}) copy-start(f32[2,2560]{1,0:T(2,128)} %copy-done.6) | copy-start | bytes 61444
  29.5 10.4 %collective-permute-start.6 = (f32[40,2560]{1,0:T(8,128)}, f32[40,2560]{1,0:T(8,128)S(1)}, u32[]{:S(2)}, u32[]{:S(2)}) collective-permute-start(f32[40,2560]{1,0:T(8,128)} %get-tuple-element.38), channel_id=1, source_target_pairs={{0,1},{1,0},{2,3},{3,2},{4,5},{5,4},{6,7},{7,6},{8,9},{9,8},{10,11... | collective-permute-start | bytes 1228808 | tf_op jit(solution)/shard_map/ppermute | solution.py:672
  29.7 36.5 %collective-permute-start.3 = (f32[80,2560]{1,0:T(8,128)S(1)}, f32[80,2560]{1,0:T(8,128)S(1)}, u32[]{:S(2)}, u32[]{:S(2)}) collective-permute-start(f32[80,2560]{1,0:T(8,128)S(1)} %get-tuple-element.34.refs_0_), channel_id=1, source_target_pairs={{0,14},{1,15},{2,0},{3,1},{4,2},{5,3},{6,4},{7,5},{8,6},{9,7},{10,... | collective-permute-start | bytes 2457608 | tf_op jit(solution)/shard_map/ppermute | solution.py:666
  39.9 1.0 %copy-start.2 = (f32[40,2560]{1,0:T(8,128)S(1)}, f32[40,2560]{1,0:T(8,128)}, u32[]{:S(2)}) copy-start(f32[40,2560]{1,0:T(8,128)} %get-tuple-element.37.mine_ref.refs_2_) | copy-start | bytes 1228804
  40.9 41.7 %slice-start.1 = ((s8[4587520]{0:T(1024)(128)(4,1)}), s8[4194304]{0:T(1024)(128)(4,1)S(1)}, s32[]{:S(2)}) async-start(s8[4587520]{0:T(1024)(128)(4,1)} %bitcast.4), calls=%async_computation.1 | async-start | bytes 8388608
  41.1 27.6 %collective-permute-start.9 = (f32[80,2560]{1,0:T(8,128)S(1)}, f32[80,2560]{1,0:T(8,128)S(1)}, u32[]{:S(2)}, u32[]{:S(2)}) collective-permute-start(f32[80,2560]{1,0:T(8,128)S(1)} %get-tuple-element.40.refs_0_), channel_id=1, source_target_pairs={{0,14},{1,15},{2,0},{3,1},{4,2},{5,3},{6,4},{7,5},{8,6},{9,7},{10,... | collective-permute-start | bytes 2457608 | tf_op jit(solution)/shard_map/ppermute | solution.py:666
  43.9 13.4 %collective-permute-start.8 = (f32[40,2560]{1,0:T(8,128)}, f32[40,2560]{1,0:T(8,128)S(1)}, u32[]{:S(2)}, u32[]{:S(2)}) collective-permute-start(f32[40,2560]{1,0:T(8,128)} %get-tuple-element.38), channel_id=1, source_target_pairs={{0,3},{1,2},{2,5},{3,4},{4,7},{5,6},{6,9},{7,8},{8,11},{9,10},{10,... | collective-permute-start | bytes 1228808 | tf_op jit(solution)/shard_map/ppermute | solution.py:669
  44.0 22.2 %collective-permute-start.7 = (f32[40,2560]{1,0:T(8,128)S(1)}, f32[40,2560]{1,0:T(8,128)S(1)}, u32[]{:S(2)}, u32[]{:S(2)}) collective-permute-start(f32[40,2560]{1,0:T(8,128)S(1)} %copy-done.2), channel_id=1, source_target_pairs={{0,2},{1,3},{2,4},{3,5},{4,6},{5,7},{6,8},{7,9},{8,10},{9,11},{10,... | collective-permute-start | bytes 1228808 | tf_op jit(solution)/shard_map/ppermute | solution.py:666
  44.1 28.3 %collective-permute-start.13 = (f32[4,5120]{1,0:T(4,128)S(1)}, f32[4,5120]{1,0:T(4,128)S(1)}, u32[]{:S(2)}, u32[]{:S(2)}) collective-permute-start(f32[4,5120]{1,0:T(4,128)S(1)} %far_pack.1), channel_id=1, source_target_pairs={{0,12},{1,13},{2,14},{3,15},{4,0},{5,1},{6,2},{7,3},{8,4},{9,5},{1... | collective-permute-start | bytes 245768 | tf_op jit(solution)/shard_map/ppermute | solution.py:666
  57.4 20.1 %collective-permute-start.12 = (f32[24,2560]{1,0:T(8,128)S(1)}, f32[24,2560]{1,0:T(8,128)S(1)}, u32[]{:S(2)}, u32[]{:S(2)}) collective-permute-start(f32[24,2560]{1,0:T(8,128)S(1)} %relay_pack.2), channel_id=1, source_target_pairs={{0,2},{1,3},{2,4},{3,5},{4,6},{5,7},{6,8},{7,9},{8,10},{9,11},{10,... | collective-permute-start | bytes 737288 | tf_op jit(solution)/shard_map/ppermute | solution.py:666
  72.4 14.9 %collective-permute-start.15 = (f32[24,2560]{1,0:T(8,128)S(1)}, f32[24,2560]{1,0:T(8,128)S(1)}, u32[]{:S(2)}, u32[]{:S(2)}) collective-permute-start(f32[24,2560]{1,0:T(8,128)S(1)} %relay_pack.3), channel_id=1, source_target_pairs={{0,2},{1,3},{2,4},{3,5},{4,6},{5,7},{6,8},{7,9},{8,10},{9,11},{10,... | collective-permute-start | bytes 737288 | tf_op jit(solution)/shard_map/ppermute | solution.py:666
  73.0 9.6 %collective-permute-start.11 = (f32[2,5120]{1,0:T(2,128)S(1)}, f32[2,5120]{1,0:T(2,128)S(1)}, u32[]{:S(2)}, u32[]{:S(2)}) collective-permute-start(f32[2,5120]{1,0:T(2,128)S(1)} %get-tuple-element.42), channel_id=1, source_target_pairs={{0,6},{1,7},{2,8},{3,9},{4,10},{5,11},{6,12},{7,13},{8,14},{9,15},... | collective-permute-start | bytes 122888 | tf_op jit(solution)/shard_map/ppermute | solution.py:666
  76.4 6.2 %collective-permute-start.10 = (f32[2,5120]{1,0:T(2,128)S(1)}, f32[2,5120]{1,0:T(2,128)S(1)}, u32[]{:S(2)}, u32[]{:S(2)}) collective-permute-start(f32[2,5120]{1,0:T(2,128)S(1)} %get-tuple-element.41.sum_a.refs_1_), channel_id=1, source_target_pairs={{0,10},{1,11},{2,12},{3,13},{4,14},{5,15},{6,0},{7,1},{8,2},{9,3},... | collective-permute-start | bytes 122888 | tf_op jit(solution)/shard_map/ppermute | solution.py:666
  84.3 6.5 %copy-start.8 = (s32[128]{0:T(128)S(1)}, s32[128]{0:T(128)}, u32[]{:S(2)}) copy-start(s32[128]{0:T(128)} %counts_ref.1) | copy-start | bytes 1540
  84.3 6.4 %copy-start.9 = (s32[2]{0:T(128)S(1)}, s32[2]{0:T(128)}, u32[]{:S(2)}) copy-start(s32[2]{0:T(128)} %get-tuple-element.29.refs_2_.state_ref) | copy-start | bytes 28
  84.3 4.7 %collective-permute-start.14 = (f32[40,2560]{1,0:T(8,128)S(1)}, f32[40,2560]{1,0:T(8,128)S(1)}, u32[]{:S(2)}, u32[]{:S(2)}) collective-permute-start(f32[40,2560]{1,0:T(8,128)S(1)} %get-tuple-element.44), channel_id=1, source_target_pairs={{0,1},{1,0},{2,3},{3,2},{4,5},{5,4},{6,7},{7,6},{8,9},{9,8},{10,11... | collective-permute-start | bytes 1228808 | tf_op jit(solution)/shard_map/ppermute | solution.py:672
  88.9 1.8 %collective-permute-start.16 = (f32[40,2560]{1,0:T(8,128)S(1)}, f32[40,2560]{1,0:T(8,128)S(1)}, u32[]{:S(2)}, u32[]{:S(2)}) collective-permute-start(f32[40,2560]{1,0:T(8,128)S(1)} %get-tuple-element.46), channel_id=1, source_target_pairs={{0,1},{1,0},{2,3},{3,2},{4,5},{5,4},{6,7},{7,6},{8,9},{9,8},{10,11... | collective-permute-start | bytes 1228808 | tf_op jit(solution)/shard_map/ppermute | solution.py:672

commit v3 on v2

--- a/solution.py
+++ b/solution.py
@@ -215,10 +215,10 @@
 def advect_kernel(last, base, tiles, *refs):
     if last:
         (dev_ref, counts_ref, state_ref, x_hbm, code_hbm, mask_hbm, wa_ref, wb_ref, tab_ref, lower_ref, upper_ref, order_ref,
-         keep_ref, send_ref, par, dst, x_ref, code_ref, mask_ref, sems) = refs
+         both_ref, send_ref, par, dst, x_ref, code_ref, mask_ref, sems) = refs
     else:
         (dev_ref, counts_ref, x_hbm, code_hbm, mask_hbm, wa_ref, wb_ref, tab_ref, order_ref,
-         keep_ref, send_ref, next_ref, par, dst, x_ref, code_ref, mask_ref, sems) = refs
+         both_ref, send_ref, next_ref, par, dst, x_ref, code_ref, mask_ref, sems) = refs
 
     def copies(seg):
         at = pl.ds(pl.multiple_of(seg * (SEG_TILES * TILE), SEG_TILES * TILE), SEG_TILES * TILE)
@@ -334,13 +334,17 @@
     core = dev_ref[0] & 1
 
     def emit(j, _):
-        keep_ref[:ROWS, lanes(j)] = dst[MARGIN + core * half + j]
-        send_ref[:ROWS, lanes(j)] = dst[MARGIN + (1 - core) * half + j]
+        other = dst[MARGIN + (1 - core) * half + j]
+        both_ref[:ROWS, lanes(j)] = dst[MARGIN + core * half + j]
+        both_ref[PAD : PAD + ROWS, lanes(j)] = other
+        send_ref[:ROWS, lanes(j)] = other
         return 0
 
     lax.fori_loop(0, half, emit, 0, unroll=2)
-    for out in (keep_ref, send_ref):
-        out[ROWS:PAD, :] = jnp.zeros((PAD - ROWS, out.shape[1]), jnp.float32)
+    none = jnp.zeros((PAD - ROWS, send_ref.shape[1]), jnp.float32)
+    both_ref[ROWS:PAD, :] = none
+    both_ref[PAD + ROWS :, :] = none
+    send_ref[ROWS:, :] = none
 
 
 def advect(last, base, tiles, dev, counts, state, spectrum, codes, mask, wa, wb, tab, extra):
@@ -352,8 +356,8 @@
     specs = [SMEM] + ([SMEM] if last else [])
     specs += [hbm, hbm, hbm, whole((NT, TILE)), whole((NT, TILE)), tab_spec]
     specs += ([whole((PAD, TILE))] * 2 if last else []) + [pl.BlockSpec(memory_space=pl.ANY)]
-    outs = [jax.ShapeDtypeStruct((PAD, half), jnp.float32)] * 2
-    out_specs = [whole((PAD, half))] * 2
+    outs = [jax.ShapeDtypeStruct((rows, half), jnp.float32) for rows in (2 * PAD, PAD)]
+    out_specs = [whole((rows, half)) for rows in (2 * PAD, PAD)]
     if not last:
         outs = outs + [jax.ShapeDtypeStruct((2,), jnp.int32)]
         out_specs = out_specs + [SMEM]
@@ -380,27 +384,29 @@
     )(dev, *args)
 
 
-def join_kernel(mine_ref, other_ref, tab_a, tab_b, *refs):
-    both_ref, out_ref = refs[-2:]
+def head(x):
+    return pl.BlockSpec((PAD, x.shape[1]), lambda *i: (0, 0))
+
+
+def moments_kernel(mine_ref, other_ref, tab_a, tab_b, out_ref):
     mine, other = mine_ref[...], other_ref[...]
-    both_ref[:PAD] = mine
-    both_ref[PAD:] = other
     fa, fb = tab_a[:, 7:8], tab_b[:, 7:8]
     out_ref[0:1, :] = jnp.sum(mine, axis=0, keepdims=True) + jnp.sum(other, axis=0, keepdims=True)
     out_ref[1:2, :] = jnp.sum(fa * mine, axis=0, keepdims=True) + jnp.sum(fb * other, axis=0, keepdims=True)
 
 
-def join(mine, other, tabs, after=()):
+def moments(mine, other, tabs):
     n = mine.shape[1]
     return pl.pallas_call(
-        join_kernel,
-        in_specs=[VMEM] * 4 + [pl.BlockSpec(memory_space=pl.ANY)] * len(after),
-        out_specs=[VMEM] * 2,
-        out_shape=[jax.ShapeDtypeStruct((2 * PAD, n), jnp.float32), jax.ShapeDtypeStruct((2, n), jnp.float32)],
+        moments_kernel,
+        grid=(1,),
+        in_specs=[head(mine), head(other)] + [pl.BlockSpec((PAD, TILE), lambda i: (0, 0))] * 2,
+        out_specs=pl.BlockSpec((2, n), lambda i: (0, 0)),
+        out_shape=jax.ShapeDtypeStruct((2, n), jnp.float32),
         compiler_params=SMALL,
         cost_estimate=cost(0),
-        name="join",
-    )(mine, other, *tabs, *after)
+        name="moments",
+    )(mine, other, *tabs)
 
 
 def windows_kernel(*refs):
@@ -414,11 +420,11 @@
         )
 
     at = 0
-    for j in range(0, len(refs) - 4, 4):
-        own, um, uo, down = refs[j : j + 4]
+    for j in range(0, len(refs) - 4, 5):
+        own, um, uo, dm, do = refs[j : j + 5]
         n = own.shape[1]
         below = sums(um[...], uo[...], 8)
-        above = sums(down[:PAD], down[PAD:], 9)
+        above = sums(dm[...], do[...], 9)
         for i in range(2):
             two = own[i : i + 1, :] + above[i]
             two_ref[i : i + 1, at : at + n] = two
@@ -427,12 +433,14 @@
 
 
 def moment_windows(chunks, tabs):
-    args = [x for own, up, down in chunks for x in (own, *up, down)]
+    args = [x for own, up, down in chunks for x in (own, *up, *down)]
     total = sum(own.shape[1] for own, _, _ in chunks)
     return pl.pallas_call(
         windows_kernel,
-        in_specs=[VMEM] * (len(args) + 2),
-        out_specs=[VMEM] * 2,
+        grid=(1,),
+        in_specs=[head(x) if x.shape[0] > 2 else pl.BlockSpec(x.shape, lambda i: (0, 0)) for x in args]
+        + [pl.BlockSpec((PAD, TILE), lambda i: (0, 0))] * 2,
+        out_specs=[pl.BlockSpec((2, total), lambda i: (0, 0))] * 2,
         out_shape=[jax.ShapeDtypeStruct((2, total), jnp.float32)] * 2,
         compiler_params=SMALL,
         cost_estimate=cost(0),
@@ -506,7 +514,7 @@
         grid_spec=pltpu.PrefetchScalarGridSpec(
             num_scalar_prefetch=1,
             grid=(1,),
-            in_specs=[pl.BlockSpec(x.shape, lambda i, d: (0, 0)) for x in up]
+            in_specs=[head(x) for x in up]
             + [pl.BlockSpec(memory_space=pl.ANY)] * len(after),
             out_specs=pl.BlockSpec((RELAY, n), lambda i, d: (0, 0)),
         ),
@@ -556,7 +564,7 @@
             in_specs=[pl.BlockSpec((1, 4 * PAD, 3 * PIECES), lambda i, d: (d[0], 0, 0))]
             + [pl.BlockSpec((PAD, TILE), lambda i, d: (0, 0))] * 2
             + [wide(2)] * 3
-            + [spec(p.shape[0]) for p in pieces]
+            + [spec(min(p.shape[0], PAD)) for p in pieces]
             + [wide(FAR)],
             out_specs=[spec(PAD)] * 2,
         ),
@@ -675,28 +683,28 @@
     lower = lax.ppermute(to_upper, "space", [(s, (s + 1) % N_SPACE) for s in range(N_SPACE)])
     upper = lax.ppermute(to_lower, "space", [(s, (s - 1) % N_SPACE) for s in range(N_SPACE)])
 
-    mine, send, state = advect(
+    def spread(both):
+        up, down = shift(both, 2), shift(both, -2)
+        return (up, swap(up[PAD:])), (down, swap(down[PAD:]))
+
+    both1, send, state = advect(
         False, 0, CHUNKS[0], dev, counts, None, spectrum, neighbors, neighbor_mask, wa, wb, tabs[0], [wa]
     )
-    up1 = shift(mine, 2), cross(send, 2)
-    own1 = mine, swap(send)
-    both1, sums1 = join(*own1, tabs)
-    down1 = shift(both1, -2)
-    mine, send = advect(
+    up1, down1 = spread(both1)
+    own1 = both1, swap(send)
+    both2, send = advect(
         True, CHUNKS[0], CHUNKS[1], dev, counts, state, spectrum, neighbors, neighbor_mask, wa, wb, tabs[0],
-        [lower, upper, sums1],
+        [lower, upper, wa],
     )
-    up2 = shift(mine, 2), cross(send, 2)
-    own2 = mine, swap(send)
-    both2, sums2 = join(*own2, tabs, up1)
-    down2 = shift(both2, -2)
+    up2, down2 = spread(both2)
+    own2 = both2, swap(send)
     far = shift(far_pack(dev, own1, own2), -4)
-    three, two = moment_windows([(sums1, up1, down1), (sums2, up2, down2)], tabs)
+    three, two = moment_windows([(moments(*own1, tabs), up1, down1), (moments(*own2, tabs), up2, down2)], tabs)
     sums = three, shift(three, -6), shift(two, 6)
     relay1 = shift(relay_pack(dev, up1), 2)
-    relay2 = shift(relay_pack(dev, up2, [far, three]), 2)
+    relay2 = shift(relay_pack(dev, up2, [three]), 2)
     results, start = [], 0
-    for pieces in ([both1, *up1, down1, relay1], [both2, *up2, down2, relay2]):
+    for pieces in ([*own1, *up1, *down1, relay1], [*own2, *up2, *down2, relay2]):
         mine, other = sources(dev, weights, tabs, sums, pieces, far, start)
         start += mine.shape[1]
         results += [mine, swap(other)]

time: 94.8 us -> 86.5 us (0.912)
  waiting for transfers between devices: 37.9 us -> 22.4 us
  starting transfers between devices: 28.2 us -> 37.2 us
  local copies, waits for them, and re-layouts: 3.24 us -> 0.74 us
    ppermute x2 -> x0, waiting for transfers between devices: 9.22 us -> none  [cross(): lax.ppermute(x, 'spec', [(s, (s + hops) % N_SPEC ^ 1) for s in range(N_SP...]
    ppermute x4 -> x8, starting transfers between devices: 6.61 us -> 15.3 us  [swap(): return lax.ppermute(x, 'spec', [(s, s ^ 1) for s in range(N_SPEC)])]
    ppermute x9, waiting for transfers between devices: 26.9 us -> 19.5 us  [shift(): lax.ppermute(x, 'spec', [(s, (s + hops) % N_SPEC) for s in range(N_SPEC)])]
    unnamed x32 -> x22, local copies, waits for them, and re-layouts: 3.24 us -> 0.64 us
    ppermute x1, starting transfers between devices: 0.01 us -> 2.2 us  [per_device(): lax.ppermute(to_upper, 'space', [(s, (s + 1) % N_SPACE) for s in range(N_...]
    ppermute x4 -> x8, waiting for transfers between devices: 1.73 us -> 2.87 us  [swap(): return lax.ppermute(x, 'spec', [(s, s ^ 1) for s in range(N_SPEC)])]
    ppermute x1, starting transfers between devices: 4.8 us -> 3.72 us  [per_device(): lax.ppermute(to_lower, 'space', [(s, (s - 1) % N_SPACE) for s in range(N_...]
  transfers between devices with their start and end apart: 17 -> 19, of which waited for: 8 -> 7; matrix products, arithmetic and copies ran while one was open for 0% -> 0% of each run, Pallas kernels for 12% -> 22%
where the time goes in v3:
time: 86.5 us; the launch traced here: 85.6 us
  starting transfers between devices  37.2 us (43%)
  Pallas kernels  24.9 us (29%)
  waiting for transfers between devices  22.4 us (26%)
    ppermute x9, waiting for transfers between devices, shift(): lax.ppermute(x, 'spec', [(s, (s + hops) % N_SPEC) for s in range(N_SPEC)])  19.5 us
    ppermute x9, starting transfers between devices, shift(): lax.ppermute(x, 'spec', [(s, (s + hops) % N_SPEC) for s in range(N_SPEC)])  15.9 us
    ppermute x8, starting transfers between devices, swap(): return lax.ppermute(x, 'spec', [(s, s ^ 1) for s in range(N_SPEC)])  15.3 us
    pallas_call x2, Pallas kernels, advect(): pl.pallas_call(partial(advect_kernel, last, base, tiles), grid_spec=pltpu...  14.3 us
    pallas_call x1, Pallas kernels, expand(): pl.pallas_call(expand_kernel, grid_spec=pltpu.PrefetchScalarGridSpec(num_...  3.75 us
    ppermute x1, starting transfers between devices, per_device(): lax.ppermute(to_lower, 'space', [(s, (s - 1) % N_SPACE) for s in range(N_...  3.72 us
    pallas_call x2, Pallas kernels, sources(): pl.pallas_call(sources_kernel, grid_spec=pltpu.PrefetchScalarGridSpec(num...  3.29 us
    ppermute x8, waiting for transfers between devices, swap(): return lax.ppermute(x, 'spec', [(s, s ^ 1) for s in range(N_SPEC)])  2.87 us
  transfers between devices with their start and end apart: 19, of which 7 were waited for; matrix products, arithmetic and copies ran while one was open for 0% of the time, Pallas kernels for 22%

profile of v3, /device:TPU:1, one launch (start us, length us, event | category | flops | bytes accessed | tf_op | source)
XLA Modules:
  0.0 85.6 jit_solution(3238184724940349748)
XLA Ops:
  0.0 2.4 %edges.1 = (f32[40,128]{1,0:T(8,128)}, f32[40,128]{1,0:T(8,128)}, f32[128,128]{1,0:T(8,128)}, f32[128,128]{1,0:T(8,128)}, f32[40,128]{1,0:T(8,128)}, /*index=5*/f32[40,128]{1,0:T(8,128)}) custom-call(s32[1]{0:T(128)} %bitcast.dev_ref.refs_0_, f32[39,16384]{1,0:T(8,128)} %refs_3_.3, f32[39,16384]{1,0:T(8,128)} %refs_3_.3, s32[2,128]{1,0:T(2,128)} %bitcast.8, ...), custom_call_target="tpu_custom_call" | custom-call | tf_op jit(solution)/shard_map/edges/pallas_call | solution.py:185
  2.4 2.2 %collective-permute-start.5 = (f32[40,128]{1,0:T(8,128)}, f32[40,128]{1,0:T(8,128)S(1)}, u32[]{:S(2)}, u32[]{:S(2)}) collective-permute-start(f32[40,128]{1,0:T(8,128)} %get-tuple-element.29), channel_id=1, source_target_pairs={{0,16},{16,32},{32,48},{48,64},{64,80},{80,96},{96,112},{112,128},... | collective-permute-start | bytes 61448 | tf_op jit(solution)/shard_map/ppermute | solution.py:683
  4.6 3.7 %collective-permute-start.6 = (f32[40,128]{1,0:T(8,128)}, f32[40,128]{1,0:T(8,128)S(1)}, u32[]{:S(2)}, u32[]{:S(2)}) collective-permute-start(f32[40,128]{1,0:T(8,128)} %get-tuple-element.30), channel_id=1, source_target_pairs={{0,240},{16,0},{32,16},{48,32},{64,48},{80,64},{96,80},{112,96},{1... | collective-permute-start | bytes 61448 | tf_op jit(solution)/shard_map/ppermute | solution.py:684
  8.3 6.9 %advect.2 = (f32[80,2560]{1,0:T(8,128)}, f32[40,2560]{1,0:T(8,128)}, s32[2]{0:T(128)}) custom-call(s32[1]{0:T(128)} %bitcast.dev_ref.refs_0_, s32[128]{0:T(128)} %counts_ref.1, f32[39,16384]{1,0:T(8,128)} %refs_3_.3, s32[4,16384]{1,0:T(4,128)} %refs_4_.3, s32[4,16384]{1,0:T(4,128)} %refs_5_.1, f32[128,128]{1,0:T(8,128)} %get-tuple-element.22.refs_5_.refs_8_.refs_6_.refs_11_, ...), custom_call_target="tpu_custom_call" | custom-call | tf_op jit(solution)/shard_map/advect/pallas_call | solution.py:364
  15.3 0.0 copy-start.8
  15.3 5.7 %collective-permute-start.3 = (f32[80,2560]{1,0:T(8,128)}, f32[80,2560]{1,0:T(8,128)S(1)}, u32[]{:S(2)}, u32[]{:S(2)}) collective-permute-start(f32[80,2560]{1,0:T(8,128)} %get-tuple-element.27.mine_ref.refs_0_), channel_id=1, source_target_pairs={{0,14},{1,15},{2,0},{3,1},{4,2},{5,3},{6,4},{7,5},{8,6},{9,7},{10,... | collective-permute-start | bytes 2457608 | tf_op jit(solution)/shard_map/ppermute | solution.py:674
  20.9 0.0 collective-permute-start.1
  20.9 0.0 collective-permute-done.5.refs_9_
  20.9 0.0 collective-permute-done.6.refs_10_
  21.0 0.0 copy-start.7
  21.0 0.6 copy-done.6
  21.5 0.0 copy-done.7
  21.6 7.3 %advect.3 = (f32[80,2560]{1,0:T(8,128)}, f32[40,2560]{1,0:T(8,128)}) custom-call(s32[1]{0:T(128)} %bitcast.dev_ref.refs_0_, s32[128]{0:T(128)} %counts_ref.1, s32[2]{0:T(128)} %get-tuple-element.25.refs_2_.state_ref, f32[39,16384]{1,0:T(8,128)} %refs_3_.3, s32[4,16384]{1,0:T(4,128)} %refs_4_.3, s32[4,16384]{1,0:T(4,128)} %refs_5_.1, ...), custom_call_target="tpu_custom_call" | custom-call | tf_op jit(solution)/shard_map/advect/pallas_call | solution.py:364
  28.9 0.0 copy-start
  28.9 2.7 %collective-permute-start.10 = (f32[80,2560]{1,0:T(8,128)}, f32[80,2560]{1,0:T(8,128)S(1)}, u32[]{:S(2)}, u32[]{:S(2)}) collective-permute-start(f32[80,2560]{1,0:T(8,128)} %get-tuple-element.31.mine_ref.refs_2_.refs_0_), channel_id=1, source_target_pairs={{0,14},{1,15},{2,0},{3,1},{4,2},{5,3},{6,4},{7,5},{8,6},{9,7},{10,... | collective-permute-start | bytes 2457608 | tf_op jit(solution)/shard_map/ppermute | solution.py:674
  31.7 0.0 collective-permute-start.8
  31.7 0.0 copy-done.8
  31.7 1.8 %collective-permute-start = (f32[40,2560]{1,0:T(8,128)S(1)}, f32[40,2560]{1,0:T(8,128)S(1)}, u32[]{:S(2)}, u32[]{:S(2)}) collective-permute-start(f32[40,2560]{1,0:T(8,128)S(1)} %copy-done.8), channel_id=1, source_target_pairs={{0,1},{1,0},{2,3},{3,2},{4,5},{5,4},{6,7},{7,6},{8,9},{9,8},{10,11... | collective-permute-start | bytes 1228808 | tf_op jit(solution)/shard_map/ppermute | solution.py:680
  33.5 4.3 %collective-permute-done.3.refs_3_.refs_4_ = f32[80,2560]{1,0:T(8,128)S(1)} collective-permute-done((f32[80,2560]{1,0:T(8,128)}, f32[80,2560]{1,0:T(8,128)S(1)}, u32[]{:S(2)}, u32[]{:S(2)}) %collective-permute-start.3) | collective-permute-done | bytes 819232 | tf_op jit(solution)/shard_map/ppermute | solution.py:674
  37.8 3.4 %collective-permute-start.7 = (f32[40,2560]{1,0:T(8,128)}, f32[40,2560]{1,0:T(8,128)S(1)}, u32[]{:S(2)}, u32[]{:S(2)}) collective-permute-start(f32[40,2560]{1,0:T(8,128)} %get-tuple-element.32), channel_id=1, source_target_pairs={{0,1},{1,0},{2,3},{3,2},{4,5},{5,4},{6,7},{7,6},{8,9},{9,8},{10,11... | collective-permute-start | bytes 1228808 | tf_op jit(solution)/shard_map/ppermute | solution.py:680
  41.3 0.0 collective-permute-done.1.refs_1_.mine_ref.refs_2_
  41.3 3.6 %collective-permute-start.4 = (f32[40,2560]{1,0:T(8,128)S(1)}, f32[40,2560]{1,0:T(8,128)S(1)}, u32[]{:S(2)}, u32[]{:S(2)}) collective-permute-start(f32[40,2560]{1,0:T(8,128)S(1)} %slice.17), channel_id=1, source_target_pairs={{0,1},{1,0},{2,3},{3,2},{4,5},{5,4},{6,7},{7,6},{8,9},{9,8},{10,11... | collective-permute-start | bytes 1228808 | tf_op jit(solution)/shard_map/ppermute | solution.py:680
  44.9 10.5 %collective-permute-done.10.refs_8_.refs_4_ = f32[80,2560]{1,0:T(8,128)S(1)} collective-permute-done((f32[80,2560]{1,0:T(8,128)}, f32[80,2560]{1,0:T(8,128)S(1)}, u32[]{:S(2)}, u32[]{:S(2)}) %collective-permute-start.10) | collective-permute-done | bytes 819232 | tf_op jit(solution)/shard_map/ppermute | solution.py:674
  55.3 1.9 %collective-permute-start.2 = (f32[40,2560]{1,0:T(8,128)S(1)}, f32[40,2560]{1,0:T(8,128)S(1)}, u32[]{:S(2)}, u32[]{:S(2)}) collective-permute-start(f32[40,2560]{1,0:T(8,128)S(1)} %slice.16), channel_id=1, source_target_pairs={{0,1},{1,0},{2,3},{3,2},{4,5},{5,4},{6,7},{7,6},{8,9},{9,8},{10,11... | collective-permute-start | bytes 1228808 | tf_op jit(solution)/shard_map/ppermute | solution.py:680
  57.3 1.1 %collective-permute-done.8.refs_6_.mine_ref.refs_2_ = f32[80,2560]{1,0:T(8,128)S(1)} collective-permute-done((f32[80,2560]{1,0:T(8,128)}, f32[80,2560]{1,0:T(8,128)S(1)}, u32[]{:S(2)}, u32[]{:S(2)}) %collective-permute-start.8) | collective-permute-done | bytes 819232 | tf_op jit(solution)/shard_map/ppermute | solution.py:674
  58.4 2.2 %collective-permute-start.11 = (f32[40,2560]{1,0:T(8,128)S(1)}, f32[40,2560]{1,0:T(8,128)S(1)}, u32[]{:S(2)}, u32[]{:S(2)}) collective-permute-start(f32[40,2560]{1,0:T(8,128)S(1)} %slice.19), channel_id=1, source_target_pairs={{0,1},{1,0},{2,3},{3,2},{4,5},{5,4},{6,7},{7,6},{8,9},{9,8},{10,11... | collective-permute-start | bytes 1228808 | tf_op jit(solution)/shard_map/ppermute | solution.py:680
  60.6 0.0 collective-permute-done.other_ref.refs_1_
  60.6 0.1 collective-permute-start.9
  60.7 0.0 copy-done.1
  60.7 0.0 copy-done.2
  60.7 0.0 copy-done.3
  60.7 0.2 moments.2.refs_0_
  60.9 0.0 collective-permute-done.7.other_ref.refs_3_.refs_1_
  60.9 0.0 copy-done
  60.9 0.2 moments.3.refs_5_
  61.1 0.0 collective-permute-done.2.refs_2_.other_ref.refs_3_
  61.1 0.0 slice-start
  61.2 0.0 slice-start.1
  61.2 0.1 collective-permute-start.14
  61.3 0.0 collective-permute-done.4.refs_4_.refs_5_
  61.3 0.6 collective-permute-done.11.refs_9_.refs_5_
  61.9 0.6 collective-permute-done.9.refs_7_.other_ref.refs_3_
  62.5 0.7 moment_windows.1
  63.3 0.3 collective-permute-start.17
  63.6 2.7 %collective-permute-start.15 = (f32[4,5120]{1,0:T(4,128)S(1)}, f32[4,5120]{1,0:T(4,128)S(1)}, u32[]{:S(2)}, u32[]{:S(2)}) collective-permute-start(f32[4,5120]{1,0:T(4,128)S(1)} %far_pack.1), channel_id=1, source_target_pairs={{0,12},{1,13},{2,14},{3,15},{4,0},{5,1},{6,2},{7,3},{8,4},{9,5},{1... | collective-permute-start | bytes 245768 | tf_op jit(solution)/shard_map/ppermute | solution.py:674
  66.3 0.0 collective-permute-start.13
  66.3 4.5 %collective-permute-start.12 = (f32[2,5120]{1,0:T(2,128)S(1)}, f32[2,5120]{1,0:T(2,128)S(1)}, u32[]{:S(2)}, u32[]{:S(2)}) collective-permute-start(f32[2,5120]{1,0:T(2,128)S(1)} %get-tuple-element.33.sum_a.refs_0_), channel_id=1, source_target_pairs={{0,10},{1,11},{2,12},{3,13},{4,14},{5,15},{6,0},{7,1},{8,2},{9,3},... | collective-permute-start | bytes 122888 | tf_op jit(solution)/shard_map/ppermute | solution.py:674
  70.8 0.0 collective-permute-done.15.refs_7_
  70.8 3.6 %collective-permute-done.13.sum_c = f32[2,5120]{1,0:T(2,128)S(1)} collective-permute-done((f32[2,5120]{1,0:T(2,128)S(1)}, f32[2,5120]{1,0:T(2,128)S(1)}, u32[]{:S(2)}, u32[]{:S(2)}) %collective-permute-start.13) | collective-permute-done | bytes 40992 | tf_op jit(solution)/shard_map/ppermute | solution.py:674
  74.4 0.0 collective-permute-done.12.sum_b
  74.4 0.0 collective-permute-done.14.refs_6_
  74.4 0.0 slice-done
  74.4 0.0 slice-done.1
  74.5 1.7 %sources.2 = (f32[40,2560]{1,0:T(8,128)S(1)}, f32[40,2560]{1,0:T(8,128)S(1)}) custom-call(s32[1]{0:T(128)} %bitcast.dev_ref.refs_0_, bf16[16,160,816]{2,1,0:T(8,128)(2,1)S(1)} %bitcast.5, f32[40,128]{1,0:T(8,128)S(1)} %copy-done.2, f32[40,128]{1,0:T(8,128)S(1)} %copy-done.3, f32[2,5120]{1,0:T(2,128)S(1)} %get-tuple-element.33.sum_a.refs_0_, ...), custom_call_target="tpu_custom_call" | custom-call | tf_op jit(solution)/shard_map/sources/pallas_call | solution.py:559
  76.1 0.0 copy-start.4
  76.1 0.0 copy-start.5
  76.1 2.1 %collective-permute-start.16 = (f32[40,2560]{1,0:T(8,128)S(1)}, f32[40,2560]{1,0:T(8,128)S(1)}, u32[]{:S(2)}, u32[]{:S(2)}) collective-permute-start(f32[40,2560]{1,0:T(8,128)S(1)} %get-tuple-element.36), channel_id=1, source_target_pairs={{0,1},{1,0},{2,3},{3,2},{4,5},{5,4},{6,7},{7,6},{8,9},{9,8},{10,11... | collective-permute-start | bytes 1228808 | tf_op jit(solution)/shard_map/ppermute | solution.py:680
  78.2 0.0 collective-permute-done.17.refs_6_
  78.2 1.6 %sources.3 = (f32[40,2560]{1,0:T(8,128)S(1)}, f32[40,2560]{1,0:T(8,128)S(1)}) custom-call(s32[1]{0:T(128)} %bitcast.dev_ref.refs_0_, bf16[16,160,816]{2,1,0:T(8,128)(2,1)S(1)} %bitcast.5, f32[40,128]{1,0:T(8,128)S(1)} %copy-done.2, f32[40,128]{1,0:T(8,128)S(1)} %copy-done.3, f32[2,5120]{1,0:T(2,128)S(1)} %get-tuple-element.33.sum_a.refs_0_, ...), custom_call_target="tpu_custom_call" | custom-call | tf_op jit(solution)/shard_map/sources/pallas_call | solution.py:559
  79.9 0.2 collective-permute-start.18
  80.1 0.0 collective-permute-done.16.refs_1_
  80.1 1.6 %collective-permute-done.18.refs_3_ = f32[40,2560]{1,0:T(8,128)S(1)} collective-permute-done((f32[40,2560]{1,0:T(8,128)S(1)}, f32[40,2560]{1,0:T(8,128)S(1)}, u32[]{:S(2)}, u32[]{:S(2)}) %collective-permute-start.18) | collective-permute-done | bytes 409632 | tf_op jit(solution)/shard_map/ppermute | solution.py:680
  81.7 0.0 copy-done.4
  81.7 3.8 %expand.1 = f32[39,16384]{1,0:T(8,128)} custom-call(s32[1]{0:T(128)} %bitcast.dev_ref.refs_0_, s32[128]{0:T(128)S(1)} %copy-done.4, s32[2]{0:T(128)S(1)} %copy-done.5, f32[40,2560]{1,0:T(8,128)S(1)} %get-tuple-element.35.refs_0_, f32[40,2560]{1,0:T(8,128)S(1)} %collective-permute-done.16.refs_1_, f32[40,2560]{1,0:T(8,128)S(1)} %get-tuple-element.37.refs_2_, ...), custom_call_target="tpu_custom_call" | custom-call | tf_op jit(solution)/shard_map/expand/pallas_call | solution.py:648
  (13 shorter events, 0.2 us)
Async XLA Ops:
  2.4 18.5 %collective-permute-start.5 = (f32[40,128]{1,0:T(8,128)}, f32[40,128]{1,0:T(8,128)S(1)}, u32[]{:S(2)}, u32[]{:S(2)}) collective-permute-start(f32[40,128]{1,0:T(8,128)} %get-tuple-element.29), channel_id=1, source_target_pairs={{0,16},{16,32},{32,48},{48,64},{64,80},{80,96},{96,112},{112,128},... | collective-permute-start | bytes 61448 | tf_op jit(solution)/shard_map/ppermute | solution.py:683
  4.6 16.3 %collective-permute-start.6 = (f32[40,128]{1,0:T(8,128)}, f32[40,128]{1,0:T(8,128)S(1)}, u32[]{:S(2)}, u32[]{:S(2)}) collective-permute-start(f32[40,128]{1,0:T(8,128)} %get-tuple-element.30), channel_id=1, source_target_pairs={{0,240},{16,0},{32,16},{48,32},{64,48},{80,64},{96,80},{112,96},{1... | collective-permute-start | bytes 61448 | tf_op jit(solution)/shard_map/ppermute | solution.py:684
  15.3 16.4 %copy-start.8 = (f32[40,2560]{1,0:T(8,128)S(1)}, f32[40,2560]{1,0:T(8,128)}, u32[]{:S(2)}) copy-start(f32[40,2560]{1,0:T(8,128)} %get-tuple-element.28) | copy-start | bytes 1228804
  15.3 22.5 %collective-permute-start.3 = (f32[80,2560]{1,0:T(8,128)}, f32[80,2560]{1,0:T(8,128)S(1)}, u32[]{:S(2)}, u32[]{:S(2)}) collective-permute-start(f32[80,2560]{1,0:T(8,128)} %get-tuple-element.27.mine_ref.refs_0_), channel_id=1, source_target_pairs={{0,14},{1,15},{2,0},{3,1},{4,2},{5,3},{6,4},{7,5},{8,6},{9,7},{10,... | collective-permute-start | bytes 2457608 | tf_op jit(solution)/shard_map/ppermute | solution.py:674
  20.9 20.3 %collective-permute-start.1 = (f32[80,2560]{1,0:T(8,128)}, f32[80,2560]{1,0:T(8,128)S(1)}, u32[]{:S(2)}, u32[]{:S(2)}) collective-permute-start(f32[80,2560]{1,0:T(8,128)} %get-tuple-element.27.mine_ref.refs_0_), channel_id=1, source_target_pairs={{0,2},{1,3},{2,4},{3,5},{4,6},{5,7},{6,8},{7,9},{8,10},{9,11},{10,... | collective-permute-start | bytes 2457608 | tf_op jit(solution)/shard_map/ppermute | solution.py:674
  20.9 0.6 copy-start.6
  21.0 0.6 copy-start.7
  21.6 39.2 %copy-start.1 = (f32[80,2560]{1,0:T(8,128)S(1)}, f32[80,2560]{1,0:T(8,128)}, u32[]{:S(2)}) copy-start(f32[80,2560]{1,0:T(8,128)} %get-tuple-element.27.mine_ref.refs_0_) | copy-start | bytes 2457604
  21.6 39.2 %copy-start.2 = (f32[40,128]{1,0:T(8,128)S(1)}, f32[40,128]{1,0:T(8,128)}, u32[]{:S(2)}) copy-start(f32[40,128]{1,0:T(8,128)} %get-tuple-element.24.refs_7_.tab_a.refs_8_.refs_10_) | copy-start | bytes 61444
  21.6 39.2 %copy-start.3 = (f32[40,128]{1,0:T(8,128)S(1)}, f32[40,128]{1,0:T(8,128)}, u32[]{:S(2)}) copy-start(f32[40,128]{1,0:T(8,128)} %get-tuple-element.26.tab_b.refs_11_) | copy-start | bytes 61444
  28.9 32.0 %copy-start = (f32[80,2560]{1,0:T(8,128)S(1)}, f32[80,2560]{1,0:T(8,128)}, u32[]{:S(2)}) copy-start(f32[80,2560]{1,0:T(8,128)} %get-tuple-element.31.mine_ref.refs_2_.refs_0_) | copy-start | bytes 2457604
  28.9 26.4 %collective-permute-start.10 = (f32[80,2560]{1,0:T(8,128)}, f32[80,2560]{1,0:T(8,128)S(1)}, u32[]{:S(2)}, u32[]{:S(2)}) collective-permute-start(f32[80,2560]{1,0:T(8,128)} %get-tuple-element.31.mine_ref.refs_2_.refs_0_), channel_id=1, source_target_pairs={{0,14},{1,15},{2,0},{3,1},{4,2},{5,3},{6,4},{7,5},{8,6},{9,7},{10,... | collective-permute-start | bytes 2457608 | tf_op jit(solution)/shard_map/ppermute | solution.py:674
  31.7 26.7 %collective-permute-start.8 = (f32[80,2560]{1,0:T(8,128)}, f32[80,2560]{1,0:T(8,128)S(1)}, u32[]{:S(2)}, u32[]{:S(2)}) collective-permute-start(f32[80,2560]{1,0:T(8,128)} %get-tuple-element.31.mine_ref.refs_2_.refs_0_), channel_id=1, source_target_pairs={{0,2},{1,3},{2,4},{3,5},{4,6},{5,7},{6,8},{7,9},{8,10},{9,11},{10,... | collective-permute-start | bytes 2457608 | tf_op jit(solution)/shard_map/ppermute | solution.py:674
  31.7 28.9 %collective-permute-start = (f32[40,2560]{1,0:T(8,128)S(1)}, f32[40,2560]{1,0:T(8,128)S(1)}, u32[]{:S(2)}, u32[]{:S(2)}) collective-permute-start(f32[40,2560]{1,0:T(8,128)S(1)} %copy-done.8), channel_id=1, source_target_pairs={{0,1},{1,0},{2,3},{3,2},{4,5},{5,4},{6,7},{7,6},{8,9},{9,8},{10,11... | collective-permute-start | bytes 1228808 | tf_op jit(solution)/shard_map/ppermute | solution.py:680
  37.8 23.1 %collective-permute-start.7 = (f32[40,2560]{1,0:T(8,128)}, f32[40,2560]{1,0:T(8,128)S(1)}, u32[]{:S(2)}, u32[]{:S(2)}) collective-permute-start(f32[40,2560]{1,0:T(8,128)} %get-tuple-element.32), channel_id=1, source_target_pairs={{0,1},{1,0},{2,3},{3,2},{4,5},{5,4},{6,7},{7,6},{8,9},{9,8},{10,11... | collective-permute-start | bytes 1228808 | tf_op jit(solution)/shard_map/ppermute | solution.py:680
  41.3 20.0 %collective-permute-start.4 = (f32[40,2560]{1,0:T(8,128)S(1)}, f32[40,2560]{1,0:T(8,128)S(1)}, u32[]{:S(2)}, u32[]{:S(2)}) collective-permute-start(f32[40,2560]{1,0:T(8,128)S(1)} %slice.17), channel_id=1, source_target_pairs={{0,1},{1,0},{2,3},{3,2},{4,5},{5,4},{6,7},{7,6},{8,9},{9,8},{10,11... | collective-permute-start | bytes 1228808 | tf_op jit(solution)/shard_map/ppermute | solution.py:680
  55.3 5.8 %collective-permute-start.2 = (f32[40,2560]{1,0:T(8,128)S(1)}, f32[40,2560]{1,0:T(8,128)S(1)}, u32[]{:S(2)}, u32[]{:S(2)}) collective-permute-start(f32[40,2560]{1,0:T(8,128)S(1)} %slice.16), channel_id=1, source_target_pairs={{0,1},{1,0},{2,3},{3,2},{4,5},{5,4},{6,7},{7,6},{8,9},{9,8},{10,11... | collective-permute-start | bytes 1228808 | tf_op jit(solution)/shard_map/ppermute | solution.py:680
  58.4 3.6 %collective-permute-start.11 = (f32[40,2560]{1,0:T(8,128)S(1)}, f32[40,2560]{1,0:T(8,128)S(1)}, u32[]{:S(2)}, u32[]{:S(2)}) collective-permute-start(f32[40,2560]{1,0:T(8,128)S(1)} %slice.19), channel_id=1, source_target_pairs={{0,1},{1,0},{2,3},{3,2},{4,5},{5,4},{6,7},{7,6},{8,9},{9,8},{10,11... | collective-permute-start | bytes 1228808 | tf_op jit(solution)/shard_map/ppermute | solution.py:680
  60.6 1.9 %collective-permute-start.9 = (f32[40,2560]{1,0:T(8,128)S(1)}, f32[40,2560]{1,0:T(8,128)S(1)}, u32[]{:S(2)}, u32[]{:S(2)}) collective-permute-start(f32[40,2560]{1,0:T(8,128)S(1)} %slice.18), channel_id=1, source_target_pairs={{0,1},{1,0},{2,3},{3,2},{4,5},{5,4},{6,7},{7,6},{8,9},{9,8},{10,11... | collective-permute-start | bytes 1228808 | tf_op jit(solution)/shard_map/ppermute | solution.py:680
  61.1 13.3 %slice-start = ((s8[4587520]{0:T(1024)(128)(4,1)}), s8[4194304]{0:T(1024)(128)(4,1)S(1)}, s32[]{:S(2)}) async-start(s8[4587520]{0:T(1024)(128)(4,1)} %bitcast.4), calls=%async_computation | async-start | bytes 8388608
  61.2 13.2 %slice-start.1 = ((s8[4587520]{0:T(1024)(128)(4,1)}), s8[393216]{0:T(1024)(128)(4,1)S(1)}, s32[]{:S(2)}) async-start(s8[4587520]{0:T(1024)(128)(4,1)} %bitcast.4), calls=%async_computation.1 | async-start | bytes 786432
  61.2 13.2 %collective-permute-start.14 = (f32[24,2560]{1,0:T(8,128)S(1)}, f32[24,2560]{1,0:T(8,128)S(1)}, u32[]{:S(2)}, u32[]{:S(2)}) collective-permute-start(f32[24,2560]{1,0:T(8,128)S(1)} %relay_pack.2), channel_id=1, source_target_pairs={{0,2},{1,3},{2,4},{3,5},{4,6},{5,7},{6,8},{7,9},{8,10},{9,11},{10,... | collective-permute-start | bytes 737288 | tf_op jit(solution)/shard_map/ppermute | solution.py:674
  63.3 14.9 %collective-permute-start.17 = (f32[24,2560]{1,0:T(8,128)S(1)}, f32[24,2560]{1,0:T(8,128)S(1)}, u32[]{:S(2)}, u32[]{:S(2)}) collective-permute-start(f32[24,2560]{1,0:T(8,128)S(1)} %relay_pack.3), channel_id=1, source_target_pairs={{0,2},{1,3},{2,4},{3,5},{4,6},{5,7},{6,8},{7,9},{8,10},{9,11},{10,... | collective-permute-start | bytes 737288 | tf_op jit(solution)/shard_map/ppermute | solution.py:674
  63.6 7.2 %collective-permute-start.15 = (f32[4,5120]{1,0:T(4,128)S(1)}, f32[4,5120]{1,0:T(4,128)S(1)}, u32[]{:S(2)}, u32[]{:S(2)}) collective-permute-start(f32[4,5120]{1,0:T(4,128)S(1)} %far_pack.1), channel_id=1, source_target_pairs={{0,12},{1,13},{2,14},{3,15},{4,0},{5,1},{6,2},{7,3},{8,4},{9,5},{1... | collective-permute-start | bytes 245768 | tf_op jit(solution)/shard_map/ppermute | solution.py:674
  66.3 8.1 %collective-permute-start.13 = (f32[2,5120]{1,0:T(2,128)S(1)}, f32[2,5120]{1,0:T(2,128)S(1)}, u32[]{:S(2)}, u32[]{:S(2)}) collective-permute-start(f32[2,5120]{1,0:T(2,128)S(1)} %get-tuple-element.34), channel_id=1, source_target_pairs={{0,6},{1,7},{2,8},{3,9},{4,10},{5,11},{6,12},{7,13},{8,14},{9,15},... | collective-permute-start | bytes 122888 | tf_op jit(solution)/shard_map/ppermute | solution.py:674
  66.3 8.1 %collective-permute-start.12 = (f32[2,5120]{1,0:T(2,128)S(1)}, f32[2,5120]{1,0:T(2,128)S(1)}, u32[]{:S(2)}, u32[]{:S(2)}) collective-permute-start(f32[2,5120]{1,0:T(2,128)S(1)} %get-tuple-element.33.sum_a.refs_0_), channel_id=1, source_target_pairs={{0,10},{1,11},{2,12},{3,13},{4,14},{5,15},{6,0},{7,1},{8,2},{9,3},... | collective-permute-start | bytes 122888 | tf_op jit(solution)/shard_map/ppermute | solution.py:674
  76.1 5.6 %copy-start.4 = (s32[128]{0:T(128)S(1)}, s32[128]{0:T(128)}, u32[]{:S(2)}) copy-start(s32[128]{0:T(128)} %counts_ref.1) | copy-start | bytes 1540
  76.1 5.6 %copy-start.5 = (s32[2]{0:T(128)S(1)}, s32[2]{0:T(128)}, u32[]{:S(2)}) copy-start(s32[2]{0:T(128)} %get-tuple-element.25.refs_2_.state_ref) | copy-start | bytes 28
  76.1 3.9 %collective-permute-start.16 = (f32[40,2560]{1,0:T(8,128)S(1)}, f32[40,2560]{1,0:T(8,128)S(1)}, u32[]{:S(2)}, u32[]{:S(2)}) collective-permute-start(f32[40,2560]{1,0:T(8,128)S(1)} %get-tuple-element.36), channel_id=1, source_target_pairs={{0,1},{1,0},{2,3},{3,2},{4,5},{5,4},{6,7},{7,6},{8,9},{9,8},{10,11... | collective-permute-start | bytes 1228808 | tf_op jit(solution)/shard_map/ppermute | solution.py:680
  79.9 1.8 %collective-permute-start.18 = (f32[40,2560]{1,0:T(8,128)S(1)}, f32[40,2560]{1,0:T(8,128)S(1)}, u32[]{:S(2)}, u32[]{:S(2)}) collective-permute-start(f32[40,2560]{1,0:T(8,128)S(1)} %get-tuple-element.38), channel_id=1, source_target_pairs={{0,1},{1,0},{2,3},{3,2},{4,5},{5,4},{6,7},{7,6},{8,9},{9,8},{10,11... | collective-permute-start | bytes 1228808 | tf_op jit(solution)/shard_map/ppermute | solution.py:680

commit v4 on v3

--- a/solution.py
+++ b/solution.py
@@ -488,41 +488,45 @@
     )(dev, *[x for pair in pairs for x in pair])
 
 
-def relay_kernel(dev_ref, mine_ref, other_ref, *refs):
+def relay_kernel(dev_ref, *refs):
     out_ref = refs[-1]
     core = dev_ref[0] & 1
     turn = ((dev_ref[0] >> 1) + 1) & 3
 
-    def fill(rows):
-        row = lambda i: rows[i : i + 1, :]
-        out_ref[...] = rows[16:40, :]
-        out_ref[0:1, :] = jnp.where(turn == 1, row(15), jnp.where(turn == 2, row(9), row(3)))
+    def fill(parts):
+        at = 0
+        for rows in parts:
+            n = rows.shape[1]
+            row = lambda i: rows[i : i + 1, :]
+            out_ref[:, at : at + n] = rows[16:40, :]
+            out_ref[0:1, at : at + n] = jnp.where(turn == 1, row(15), jnp.where(turn == 2, row(9), row(3)))
+            at += n
 
     @pl.when(core == 1)
     def _():
-        fill(mine_ref)
+        fill(refs[0 : 2 * len(CHUNKS) : 2])
 
     @pl.when(core == 0)
     def _():
-        fill(other_ref)
-
-
-def relay_pack(dev, up, after=()):
-    n = up[0].shape[1]
+        fill(refs[1 : 2 * len(CHUNKS) : 2])
+
+
+def relay_pack(dev, ups, after):
+    args = [x for up in ups for x in up]
+    total = sum(up[0].shape[1] for up in ups)
     return pl.pallas_call(
         relay_kernel,
         grid_spec=pltpu.PrefetchScalarGridSpec(
             num_scalar_prefetch=1,
             grid=(1,),
-            in_specs=[head(x) for x in up]
-            + [pl.BlockSpec(memory_space=pl.ANY)] * len(after),
-            out_specs=pl.BlockSpec((RELAY, n), lambda i, d: (0, 0)),
+            in_specs=[head(x) for x in args] + [pl.BlockSpec(memory_space=pl.ANY)] * len(after),
+            out_specs=pl.BlockSpec((RELAY, total), lambda i, d: (0, 0)),
         ),
-        out_shape=jax.ShapeDtypeStruct((RELAY, n), jnp.float32),
+        out_shape=jax.ShapeDtypeStruct((RELAY, total), jnp.float32),
         compiler_params=SMALL,
         cost_estimate=cost(0),
         name="relay_pack",
-    )(dev, *up, *after)
+    )(dev, *args, *after)
 
 
 def sources_kernel(dev_ref, w_ref, tab_a, tab_b, sum_a, sum_b, sum_c, *refs):
@@ -550,7 +554,7 @@
         out[...] = g * (jnp.exp(freq * fade) + (freq * gain) * (g * (upper + lower) - cross * (upper * lower)))
 
 
-def sources(dev, weights, tabs, sums, pieces, far, start):
+def sources(dev, weights, tabs, sums, pieces, relay, far, start):
     n = pieces[0].shape[1]
     block = BLOCK
     skip = start // block
@@ -565,14 +569,14 @@
             + [pl.BlockSpec((PAD, TILE), lambda i, d: (0, 0))] * 2
             + [wide(2)] * 3
             + [spec(min(p.shape[0], PAD)) for p in pieces]
-            + [wide(FAR)],
+            + [wide(RELAY), wide(FAR)],
             out_specs=[spec(PAD)] * 2,
         ),
         out_shape=[jax.ShapeDtypeStruct((PAD, n), jnp.float32)] * 2,
         compiler_params=SMALL,
         cost_estimate=cost(0),
         name="sources",
-    )(dev, weights, *tabs, *sums, *pieces, far)
+    )(dev, weights, *tabs, *sums, *pieces, relay, far)
 
 
 def expand_kernel(dev_ref, counts_ref, state_ref, *refs):
@@ -701,11 +705,10 @@
     far = shift(far_pack(dev, own1, own2), -4)
     three, two = moment_windows([(moments(*own1, tabs), up1, down1), (moments(*own2, tabs), up2, down2)], tabs)
     sums = three, shift(three, -6), shift(two, 6)
-    relay1 = shift(relay_pack(dev, up1), 2)
-    relay2 = shift(relay_pack(dev, up2, [three]), 2)
+    relay = shift(relay_pack(dev, [up1, up2], [three]), 2)
     results, start = [], 0
-    for pieces in ([*own1, *up1, *down1, relay1], [*own2, *up2, *down2, relay2]):
-        mine, other = sources(dev, weights, tabs, sums, pieces, far, start)
+    for pieces in ([*own1, *up1, *down1], [*own2, *up2, *down2]):
+        mine, other = sources(dev, weights, tabs, sums, pieces, relay, far, start)
         start += mine.shape[1]
         results += [mine, swap(other)]
     return expand(dev, counts, state, results)

time: 86.5 us -> 90.1 us (1.042)
  waiting for transfers between devices: 22.4 us -> 26.8 us
    ppermute x9 -> x8, waiting for transfers between devices: 19.5 us -> 23.7 us  [shift(): lax.ppermute(x, 'spec', [(s, (s + hops) % N_SPEC) for s in range(N_SPEC)])]
    ppermute x9 -> x8, starting transfers between devices: 15.9 us -> 15 us  [shift(): lax.ppermute(x, 'spec', [(s, (s + hops) % N_SPEC) for s in range(N_SPEC)])]
  transfers between devices with their start and end apart: 19 -> 18, of which waited for: 7 -> 8; matrix products, arithmetic and copies ran while one was open for 0% -> 0% of each run, Pallas kernels for 22% -> 18%
where the time goes in v4:
time: 90.1 us; the launch traced here: 89.6 us
  starting transfers between devices  36.8 us (41%)
  waiting for transfers between devices  26.8 us (30%)
  Pallas kernels  24.9 us (28%)
    ppermute x8, waiting for transfers between devices, shift(): lax.ppermute(x, 'spec', [(s, (s + hops) % N_SPEC) for s in range(N_SPEC)])  23.7 us
    ppermute x8, starting transfers between devices, swap(): return lax.ppermute(x, 'spec', [(s, s ^ 1) for s in range(N_SPEC)])  15.9 us
    ppermute x8, starting transfers between devices, shift(): lax.ppermute(x, 'spec', [(s, (s + hops) % N_SPEC) for s in range(N_SPEC)])  15 us
    pallas_call x2, Pallas kernels, advect(): pl.pallas_call(partial(advect_kernel, last, base, tiles), grid_spec=pltpu...  14.3 us
    pallas_call x1, Pallas kernels, expand(): pl.pallas_call(expand_kernel, grid_spec=pltpu.PrefetchScalarGridSpec(num_...  3.75 us
    ppermute x1, starting transfers between devices, per_device(): lax.ppermute(to_lower, 'space', [(s, (s - 1) % N_SPACE) for s in range(N_...  3.72 us
    pallas_call x2, Pallas kernels, sources(): pl.pallas_call(sources_kernel, grid_spec=pltpu.PrefetchScalarGridSpec(num...  3.28 us
    ppermute x8, waiting for transfers between devices, swap(): return lax.ppermute(x, 'spec', [(s, s ^ 1) for s in range(N_SPEC)])  3.07 us
  transfers between devices with their start and end apart: 18, of which 8 were waited for; matrix products, arithmetic and copies ran while one was open for 0% of the time, Pallas kernels for 18%

profile of v4, /device:TPU:1, one launch (start us, length us, event | category | flops | bytes accessed | tf_op | source)
XLA Modules:
  0.0 89.6 jit_solution(8598261890952274002)
XLA Ops:
  0.0 2.4 %edges.1 = (f32[40,128]{1,0:T(8,128)}, f32[40,128]{1,0:T(8,128)}, f32[128,128]{1,0:T(8,128)}, f32[128,128]{1,0:T(8,128)}, f32[40,128]{1,0:T(8,128)}, /*index=5*/f32[40,128]{1,0:T(8,128)}) custom-call(s32[1]{0:T(128)} %bitcast.dev_ref.refs_0_, f32[39,16384]{1,0:T(8,128)} %refs_3_.3, f32[39,16384]{1,0:T(8,128)} %refs_3_.3, s32[2,128]{1,0:T(2,128)} %bitcast.8, ...), custom_call_target="tpu_custom_call" | custom-call | tf_op jit(solution)/shard_map/edges/pallas_call | solution.py:185
  2.4 2.2 %collective-permute-start.5 = (f32[40,128]{1,0:T(8,128)}, f32[40,128]{1,0:T(8,128)S(1)}, u32[]{:S(2)}, u32[]{:S(2)}) collective-permute-start(f32[40,128]{1,0:T(8,128)} %get-tuple-element.29), channel_id=1, source_target_pairs={{0,16},{16,32},{32,48},{48,64},{64,80},{80,96},{96,112},{112,128},... | collective-permute-start | bytes 61448 | tf_op jit(solution)/shard_map/ppermute | solution.py:687
  4.6 3.7 %collective-permute-start.6 = (f32[40,128]{1,0:T(8,128)}, f32[40,128]{1,0:T(8,128)S(1)}, u32[]{:S(2)}, u32[]{:S(2)}) collective-permute-start(f32[40,128]{1,0:T(8,128)} %get-tuple-element.30), channel_id=1, source_target_pairs={{0,240},{16,0},{32,16},{48,32},{64,48},{80,64},{96,80},{112,96},{1... | collective-permute-start | bytes 61448 | tf_op jit(solution)/shard_map/ppermute | solution.py:688
  8.3 6.9 %advect.2 = (f32[80,2560]{1,0:T(8,128)}, f32[40,2560]{1,0:T(8,128)}, s32[2]{0:T(128)}) custom-call(s32[1]{0:T(128)} %bitcast.dev_ref.refs_0_, s32[128]{0:T(128)} %counts_ref.1, f32[39,16384]{1,0:T(8,128)} %refs_3_.3, s32[4,16384]{1,0:T(4,128)} %refs_4_.3, s32[4,16384]{1,0:T(4,128)} %refs_5_.1, f32[128,128]{1,0:T(8,128)} %get-tuple-element.22.refs_5_.refs_8_.refs_6_.refs_11_, ...), custom_call_target="tpu_custom_call" | custom-call | tf_op jit(solution)/shard_map/advect/pallas_call | solution.py:364
  15.3 0.0 copy-start.8
  15.3 5.7 %collective-permute-start.3 = (f32[80,2560]{1,0:T(8,128)}, f32[80,2560]{1,0:T(8,128)S(1)}, u32[]{:S(2)}, u32[]{:S(2)}) collective-permute-start(f32[80,2560]{1,0:T(8,128)} %get-tuple-element.27.mine_ref.refs_0_), channel_id=1, source_target_pairs={{0,14},{1,15},{2,0},{3,1},{4,2},{5,3},{6,4},{7,5},{8,6},{9,7},{10,... | collective-permute-start | bytes 2457608 | tf_op jit(solution)/shard_map/ppermute | solution.py:678
  20.9 0.0 collective-permute-start.1
  20.9 0.0 collective-permute-done.5.refs_9_
  20.9 0.0 collective-permute-done.6.refs_10_
  21.0 0.0 copy-start.7
  21.0 0.6 copy-done.6
  21.5 0.0 copy-done.7
  21.6 7.3 %advect.3 = (f32[80,2560]{1,0:T(8,128)}, f32[40,2560]{1,0:T(8,128)}) custom-call(s32[1]{0:T(128)} %bitcast.dev_ref.refs_0_, s32[128]{0:T(128)} %counts_ref.1, s32[2]{0:T(128)} %get-tuple-element.25.refs_2_.state_ref, f32[39,16384]{1,0:T(8,128)} %refs_3_.3, s32[4,16384]{1,0:T(4,128)} %refs_4_.3, s32[4,16384]{1,0:T(4,128)} %refs_5_.1, ...), custom_call_target="tpu_custom_call" | custom-call | tf_op jit(solution)/shard_map/advect/pallas_call | solution.py:364
  28.9 0.0 copy-start.1
  28.9 2.7 %collective-permute-start.10 = (f32[80,2560]{1,0:T(8,128)}, f32[80,2560]{1,0:T(8,128)S(1)}, u32[]{:S(2)}, u32[]{:S(2)}) collective-permute-start(f32[80,2560]{1,0:T(8,128)} %get-tuple-element.31.mine_ref.refs_2_.refs_0_), channel_id=1, source_target_pairs={{0,14},{1,15},{2,0},{3,1},{4,2},{5,3},{6,4},{7,5},{8,6},{9,7},{10,... | collective-permute-start | bytes 2457608 | tf_op jit(solution)/shard_map/ppermute | solution.py:678
  31.7 0.0 collective-permute-start.8
  31.7 0.0 copy-done.8
  31.7 1.8 %collective-permute-start = (f32[40,2560]{1,0:T(8,128)S(1)}, f32[40,2560]{1,0:T(8,128)S(1)}, u32[]{:S(2)}, u32[]{:S(2)}) collective-permute-start(f32[40,2560]{1,0:T(8,128)S(1)} %copy-done.8), channel_id=1, source_target_pairs={{0,1},{1,0},{2,3},{3,2},{4,5},{5,4},{6,7},{7,6},{8,9},{9,8},{10,11... | collective-permute-start | bytes 1228808 | tf_op jit(solution)/shard_map/ppermute | solution.py:684
  33.5 4.2 %collective-permute-done.3.refs_3_.refs_4_ = f32[80,2560]{1,0:T(8,128)S(1)} collective-permute-done((f32[80,2560]{1,0:T(8,128)}, f32[80,2560]{1,0:T(8,128)S(1)}, u32[]{:S(2)}, u32[]{:S(2)}) %collective-permute-start.3) | collective-permute-done | bytes 819232 | tf_op jit(solution)/shard_map/ppermute | solution.py:678
  37.8 3.4 %collective-permute-start.7 = (f32[40,2560]{1,0:T(8,128)}, f32[40,2560]{1,0:T(8,128)S(1)}, u32[]{:S(2)}, u32[]{:S(2)}) collective-permute-start(f32[40,2560]{1,0:T(8,128)} %get-tuple-element.32), channel_id=1, source_target_pairs={{0,1},{1,0},{2,3},{3,2},{4,5},{5,4},{6,7},{7,6},{8,9},{9,8},{10,11... | collective-permute-start | bytes 1228808 | tf_op jit(solution)/shard_map/ppermute | solution.py:684
  41.3 0.0 collective-permute-done.1.refs_1_.refs_0_.refs_2_
  41.3 3.6 %collective-permute-start.4 = (f32[40,2560]{1,0:T(8,128)S(1)}, f32[40,2560]{1,0:T(8,128)S(1)}, u32[]{:S(2)}, u32[]{:S(2)}) collective-permute-start(f32[40,2560]{1,0:T(8,128)S(1)} %slice.17), channel_id=1, source_target_pairs={{0,1},{1,0},{2,3},{3,2},{4,5},{5,4},{6,7},{7,6},{8,9},{9,8},{10,11... | collective-permute-start | bytes 1228808 | tf_op jit(solution)/shard_map/ppermute | solution.py:684
  44.8 10.5 %collective-permute-done.10.refs_8_.refs_4_ = f32[80,2560]{1,0:T(8,128)S(1)} collective-permute-done((f32[80,2560]{1,0:T(8,128)}, f32[80,2560]{1,0:T(8,128)S(1)}, u32[]{:S(2)}, u32[]{:S(2)}) %collective-permute-start.10) | collective-permute-done | bytes 819232 | tf_op jit(solution)/shard_map/ppermute | solution.py:678
  55.3 1.9 %collective-permute-start.2 = (f32[40,2560]{1,0:T(8,128)S(1)}, f32[40,2560]{1,0:T(8,128)S(1)}, u32[]{:S(2)}, u32[]{:S(2)}) collective-permute-start(f32[40,2560]{1,0:T(8,128)S(1)} %slice.16), channel_id=1, source_target_pairs={{0,1},{1,0},{2,3},{3,2},{4,5},{5,4},{6,7},{7,6},{8,9},{9,8},{10,11... | collective-permute-start | bytes 1228808 | tf_op jit(solution)/shard_map/ppermute | solution.py:684
  57.3 1.1 %collective-permute-done.8.refs_6_.refs_2_ = f32[80,2560]{1,0:T(8,128)S(1)} collective-permute-done((f32[80,2560]{1,0:T(8,128)}, f32[80,2560]{1,0:T(8,128)S(1)}, u32[]{:S(2)}, u32[]{:S(2)}) %collective-permute-start.8) | collective-permute-done | bytes 819232 | tf_op jit(solution)/shard_map/ppermute | solution.py:678
  58.4 2.2 %collective-permute-start.11 = (f32[40,2560]{1,0:T(8,128)S(1)}, f32[40,2560]{1,0:T(8,128)S(1)}, u32[]{:S(2)}, u32[]{:S(2)}) collective-permute-start(f32[40,2560]{1,0:T(8,128)S(1)} %slice.19), channel_id=1, source_target_pairs={{0,1},{1,0},{2,3},{3,2},{4,5},{5,4},{6,7},{7,6},{8,9},{9,8},{10,11... | collective-permute-start | bytes 1228808 | tf_op jit(solution)/shard_map/ppermute | solution.py:684
  60.6 0.0 collective-permute-done.other_ref.refs_1_
  60.6 0.1 collective-permute-start.9
  60.7 0.0 copy-done
  60.7 0.0 copy-done.2
  60.7 0.0 copy-done.3
  60.7 0.2 moments.2.refs_0_
  60.9 0.0 collective-permute-done.7.other_ref.refs_3_.refs_1_
  60.9 0.0 copy-done.1
  60.9 0.0 slice-start
  61.0 0.2 moments.3.refs_5_
  61.1 0.0 slice-start.1
  61.2 0.0 collective-permute-done.4.refs_4_.refs_5_
  61.2 0.0 collective-permute-done.2.refs_2_.refs_1_.refs_3_
  61.2 0.8 collective-permute-done.11.refs_9_.refs_5_
  61.9 0.6 collective-permute-done.9.refs_7_.refs_3_
  62.5 0.7 moment_windows.1
  63.3 0.1 relay_pack.1
  63.3 0.1 collective-permute-start.14
  63.5 2.0 %collective-permute-start.15 = (f32[4,5120]{1,0:T(4,128)S(1)}, f32[4,5120]{1,0:T(4,128)S(1)}, u32[]{:S(2)}, u32[]{:S(2)}) collective-permute-start(f32[4,5120]{1,0:T(4,128)S(1)} %far_pack.1), channel_id=1, source_target_pairs={{0,12},{1,13},{2,14},{3,15},{4,0},{5,1},{6,2},{7,3},{8,4},{9,5},{1... | collective-permute-start | bytes 245768 | tf_op jit(solution)/shard_map/ppermute | solution.py:678
  65.5 0.0 collective-permute-start.13
  65.5 4.4 %collective-permute-start.12 = (f32[2,5120]{1,0:T(2,128)S(1)}, f32[2,5120]{1,0:T(2,128)S(1)}, u32[]{:S(2)}, u32[]{:S(2)}) collective-permute-start(f32[2,5120]{1,0:T(2,128)S(1)} %get-tuple-element.33.refs_4_.sum_a), channel_id=1, source_target_pairs={{0,10},{1,11},{2,12},{3,13},{4,14},{5,15},{6,0},{7,1},{8,2},{9,3},... | collective-permute-start | bytes 122888 | tf_op jit(solution)/shard_map/ppermute | solution.py:678
  69.9 0.0 collective-permute-done.15.refs_7_
  70.0 6.6 %collective-permute-done.13.sum_c = f32[2,5120]{1,0:T(2,128)S(1)} collective-permute-done((f32[2,5120]{1,0:T(2,128)S(1)}, f32[2,5120]{1,0:T(2,128)S(1)}, u32[]{:S(2)}, u32[]{:S(2)}) %collective-permute-start.13) | collective-permute-done | bytes 40992 | tf_op jit(solution)/shard_map/ppermute | solution.py:678
  76.5 0.0 collective-permute-done.12.sum_b
  76.5 1.3 %collective-permute-done.14.refs_6_ = f32[24,5120]{1,0:T(8,128)S(1)} collective-permute-done((f32[24,5120]{1,0:T(8,128)S(1)}, f32[24,5120]{1,0:T(8,128)S(1)}, u32[]{:S(2)}, u32[]{:S(2)}) %collective-permute-start.14) | collective-permute-done | bytes 491552 | tf_op jit(solution)/shard_map/ppermute | solution.py:678
  77.8 0.0 slice-done
  77.8 0.0 slice-done.1
  77.8 1.6 %sources.3 = (f32[40,2560]{1,0:T(8,128)S(1)}, f32[40,2560]{1,0:T(8,128)S(1)}) custom-call(s32[1]{0:T(128)} %bitcast.dev_ref.refs_0_, bf16[16,160,816]{2,1,0:T(8,128)(2,1)S(1)} %bitcast.5, f32[40,128]{1,0:T(8,128)S(1)} %copy-done.2, f32[40,128]{1,0:T(8,128)S(1)} %copy-done.3, f32[2,5120]{1,0:T(2,128)S(1)} %get-tuple-element.33.refs_4_.sum_a, ...), custom_call_target="tpu_custom_call" | custom-call | tf_op jit(solution)/shard_map/sources/pallas_call | solution.py:563
  79.5 0.0 copy-start.4
  79.5 0.0 copy-start.5
  79.5 2.7 %collective-permute-start.17 = (f32[40,2560]{1,0:T(8,128)S(1)}, f32[40,2560]{1,0:T(8,128)S(1)}, u32[]{:S(2)}, u32[]{:S(2)}) collective-permute-start(f32[40,2560]{1,0:T(8,128)S(1)} %get-tuple-element.38), channel_id=1, source_target_pairs={{0,1},{1,0},{2,3},{3,2},{4,5},{5,4},{6,7},{7,6},{8,9},{9,8},{10,11... | collective-permute-start | bytes 1228808 | tf_op jit(solution)/shard_map/ppermute | solution.py:684
  82.2 1.6 %sources.2 = (f32[40,2560]{1,0:T(8,128)S(1)}, f32[40,2560]{1,0:T(8,128)S(1)}) custom-call(s32[1]{0:T(128)} %bitcast.dev_ref.refs_0_, bf16[16,160,816]{2,1,0:T(8,128)(2,1)S(1)} %bitcast.5, f32[40,128]{1,0:T(8,128)S(1)} %copy-done.2, f32[40,128]{1,0:T(8,128)S(1)} %copy-done.3, f32[2,5120]{1,0:T(2,128)S(1)} %get-tuple-element.33.refs_4_.sum_a, ...), custom_call_target="tpu_custom_call" | custom-call | tf_op jit(solution)/shard_map/sources/pallas_call | solution.py:563
  83.9 0.1 collective-permute-start.16
  84.0 0.0 collective-permute-done.17.refs_3_
  84.0 1.7 %collective-permute-done.16.refs_1_ = f32[40,2560]{1,0:T(8,128)S(1)} collective-permute-done((f32[40,2560]{1,0:T(8,128)S(1)}, f32[40,2560]{1,0:T(8,128)S(1)}, u32[]{:S(2)}, u32[]{:S(2)}) %collective-permute-start.16) | collective-permute-done | bytes 409632 | tf_op jit(solution)/shard_map/ppermute | solution.py:684
  85.7 0.0 copy-done.4
  85.7 0.0 copy-done.5
  85.7 3.8 %expand.1 = f32[39,16384]{1,0:T(8,128)} custom-call(s32[1]{0:T(128)} %bitcast.dev_ref.refs_0_, s32[128]{0:T(128)S(1)} %copy-done.4, s32[2]{0:T(128)S(1)} %copy-done.5, f32[40,2560]{1,0:T(8,128)S(1)} %get-tuple-element.35.refs_0_, f32[40,2560]{1,0:T(8,128)S(1)} %collective-permute-done.16.refs_1_, f32[40,2560]{1,0:T(8,128)S(1)} %get-tuple-element.37.refs_2_, ...), custom_call_target="tpu_custom_call" | custom-call | tf_op jit(solution)/shard_map/expand/pallas_call | solution.py:652
  (10 shorter events, 0.2 us)
Async XLA Ops:
  2.4 18.5 %collective-permute-start.5 = (f32[40,128]{1,0:T(8,128)}, f32[40,128]{1,0:T(8,128)S(1)}, u32[]{:S(2)}, u32[]{:S(2)}) collective-permute-start(f32[40,128]{1,0:T(8,128)} %get-tuple-element.29), channel_id=1, source_target_pairs={{0,16},{16,32},{32,48},{48,64},{64,80},{80,96},{96,112},{112,128},... | collective-permute-start | bytes 61448 | tf_op jit(solution)/shard_map/ppermute | solution.py:687
  4.6 16.3 %collective-permute-start.6 = (f32[40,128]{1,0:T(8,128)}, f32[40,128]{1,0:T(8,128)S(1)}, u32[]{:S(2)}, u32[]{:S(2)}) collective-permute-start(f32[40,128]{1,0:T(8,128)} %get-tuple-element.30), channel_id=1, source_target_pairs={{0,240},{16,0},{32,16},{48,32},{64,48},{80,64},{96,80},{112,96},{1... | collective-permute-start | bytes 61448 | tf_op jit(solution)/shard_map/ppermute | solution.py:688
  15.3 16.4 %copy-start.8 = (f32[40,2560]{1,0:T(8,128)S(1)}, f32[40,2560]{1,0:T(8,128)}, u32[]{:S(2)}) copy-start(f32[40,2560]{1,0:T(8,128)} %get-tuple-element.28) | copy-start | bytes 1228804
  15.3 22.5 %collective-permute-start.3 = (f32[80,2560]{1,0:T(8,128)}, f32[80,2560]{1,0:T(8,128)S(1)}, u32[]{:S(2)}, u32[]{:S(2)}) collective-permute-start(f32[80,2560]{1,0:T(8,128)} %get-tuple-element.27.mine_ref.refs_0_), channel_id=1, source_target_pairs={{0,14},{1,15},{2,0},{3,1},{4,2},{5,3},{6,4},{7,5},{8,6},{9,7},{10,... | collective-permute-start | bytes 2457608 | tf_op jit(solution)/shard_map/ppermute | solution.py:678
  20.9 20.3 %collective-permute-start.1 = (f32[80,2560]{1,0:T(8,128)}, f32[80,2560]{1,0:T(8,128)S(1)}, u32[]{:S(2)}, u32[]{:S(2)}) collective-permute-start(f32[80,2560]{1,0:T(8,128)} %get-tuple-element.27.mine_ref.refs_0_), channel_id=1, source_target_pairs={{0,2},{1,3},{2,4},{3,5},{4,6},{5,7},{6,8},{7,9},{8,10},{9,11},{10,... | collective-permute-start | bytes 2457608 | tf_op jit(solution)/shard_map/ppermute | solution.py:678
  20.9 0.6 copy-start.6
  21.0 0.6 copy-start.7
  21.6 39.1 %copy-start = (f32[80,2560]{1,0:T(8,128)S(1)}, f32[80,2560]{1,0:T(8,128)}, u32[]{:S(2)}) copy-start(f32[80,2560]{1,0:T(8,128)} %get-tuple-element.27.mine_ref.refs_0_) | copy-start | bytes 2457604
  21.6 39.1 %copy-start.2 = (f32[40,128]{1,0:T(8,128)S(1)}, f32[40,128]{1,0:T(8,128)}, u32[]{:S(2)}) copy-start(f32[40,128]{1,0:T(8,128)} %get-tuple-element.24.refs_7_.tab_a.refs_8_.refs_10_) | copy-start | bytes 61444
  21.6 39.2 %copy-start.3 = (f32[40,128]{1,0:T(8,128)S(1)}, f32[40,128]{1,0:T(8,128)}, u32[]{:S(2)}) copy-start(f32[40,128]{1,0:T(8,128)} %get-tuple-element.26.tab_b.refs_11_) | copy-start | bytes 61444
  28.9 32.0 %copy-start.1 = (f32[80,2560]{1,0:T(8,128)S(1)}, f32[80,2560]{1,0:T(8,128)}, u32[]{:S(2)}) copy-start(f32[80,2560]{1,0:T(8,128)} %get-tuple-element.31.mine_ref.refs_2_.refs_0_) | copy-start | bytes 2457604
  28.9 26.4 %collective-permute-start.10 = (f32[80,2560]{1,0:T(8,128)}, f32[80,2560]{1,0:T(8,128)S(1)}, u32[]{:S(2)}, u32[]{:S(2)}) collective-permute-start(f32[80,2560]{1,0:T(8,128)} %get-tuple-element.31.mine_ref.refs_2_.refs_0_), channel_id=1, source_target_pairs={{0,14},{1,15},{2,0},{3,1},{4,2},{5,3},{6,4},{7,5},{8,6},{9,7},{10,... | collective-permute-start | bytes 2457608 | tf_op jit(solution)/shard_map/ppermute | solution.py:678
  31.7 26.7 %collective-permute-start.8 = (f32[80,2560]{1,0:T(8,128)}, f32[80,2560]{1,0:T(8,128)S(1)}, u32[]{:S(2)}, u32[]{:S(2)}) collective-permute-start(f32[80,2560]{1,0:T(8,128)} %get-tuple-element.31.mine_ref.refs_2_.refs_0_), channel_id=1, source_target_pairs={{0,2},{1,3},{2,4},{3,5},{4,6},{5,7},{6,8},{7,9},{8,10},{9,11},{10,... | collective-permute-start | bytes 2457608 | tf_op jit(solution)/shard_map/ppermute | solution.py:678
  31.7 28.9 %collective-permute-start = (f32[40,2560]{1,0:T(8,128)S(1)}, f32[40,2560]{1,0:T(8,128)S(1)}, u32[]{:S(2)}, u32[]{:S(2)}) collective-permute-start(f32[40,2560]{1,0:T(8,128)S(1)} %copy-done.8), channel_id=1, source_target_pairs={{0,1},{1,0},{2,3},{3,2},{4,5},{5,4},{6,7},{7,6},{8,9},{9,8},{10,11... | collective-permute-start | bytes 1228808 | tf_op jit(solution)/shard_map/ppermute | solution.py:684
  37.8 23.1 %collective-permute-start.7 = (f32[40,2560]{1,0:T(8,128)}, f32[40,2560]{1,0:T(8,128)S(1)}, u32[]{:S(2)}, u32[]{:S(2)}) collective-permute-start(f32[40,2560]{1,0:T(8,128)} %get-tuple-element.32), channel_id=1, source_target_pairs={{0,1},{1,0},{2,3},{3,2},{4,5},{5,4},{6,7},{7,6},{8,9},{9,8},{10,11... | collective-permute-start | bytes 1228808 | tf_op jit(solution)/shard_map/ppermute | solution.py:684
  41.3 19.9 %collective-permute-start.4 = (f32[40,2560]{1,0:T(8,128)S(1)}, f32[40,2560]{1,0:T(8,128)S(1)}, u32[]{:S(2)}, u32[]{:S(2)}) collective-permute-start(f32[40,2560]{1,0:T(8,128)S(1)} %slice.17), channel_id=1, source_target_pairs={{0,1},{1,0},{2,3},{3,2},{4,5},{5,4},{6,7},{7,6},{8,9},{9,8},{10,11... | collective-permute-start | bytes 1228808 | tf_op jit(solution)/shard_map/ppermute | solution.py:684
  55.3 5.8 %collective-permute-start.2 = (f32[40,2560]{1,0:T(8,128)S(1)}, f32[40,2560]{1,0:T(8,128)S(1)}, u32[]{:S(2)}, u32[]{:S(2)}) collective-permute-start(f32[40,2560]{1,0:T(8,128)S(1)} %slice.16), channel_id=1, source_target_pairs={{0,1},{1,0},{2,3},{3,2},{4,5},{5,4},{6,7},{7,6},{8,9},{9,8},{10,11... | collective-permute-start | bytes 1228808 | tf_op jit(solution)/shard_map/ppermute | solution.py:684
  58.4 3.6 %collective-permute-start.11 = (f32[40,2560]{1,0:T(8,128)S(1)}, f32[40,2560]{1,0:T(8,128)S(1)}, u32[]{:S(2)}, u32[]{:S(2)}) collective-permute-start(f32[40,2560]{1,0:T(8,128)S(1)} %slice.19), channel_id=1, source_target_pairs={{0,1},{1,0},{2,3},{3,2},{4,5},{5,4},{6,7},{7,6},{8,9},{9,8},{10,11... | collective-permute-start | bytes 1228808 | tf_op jit(solution)/shard_map/ppermute | solution.py:684
  60.6 1.9 %collective-permute-start.9 = (f32[40,2560]{1,0:T(8,128)S(1)}, f32[40,2560]{1,0:T(8,128)S(1)}, u32[]{:S(2)}, u32[]{:S(2)}) collective-permute-start(f32[40,2560]{1,0:T(8,128)S(1)} %slice.18), channel_id=1, source_target_pairs={{0,1},{1,0},{2,3},{3,2},{4,5},{5,4},{6,7},{7,6},{8,9},{9,8},{10,11... | collective-permute-start | bytes 1228808 | tf_op jit(solution)/shard_map/ppermute | solution.py:684
  60.9 16.9 %slice-start = ((s8[4587520]{0:T(1024)(128)(4,1)}), s8[4194304]{0:T(1024)(128)(4,1)S(1)}, s32[]{:S(2)}) async-start(s8[4587520]{0:T(1024)(128)(4,1)} %bitcast.4), calls=%async_computation | async-start | bytes 8388608
  61.1 16.7 %slice-start.1 = ((s8[4587520]{0:T(1024)(128)(4,1)}), s8[393216]{0:T(1024)(128)(4,1)S(1)}, s32[]{:S(2)}) async-start(s8[4587520]{0:T(1024)(128)(4,1)} %bitcast.4), calls=%async_computation.1 | async-start | bytes 786432
  63.3 14.5 %collective-permute-start.14 = (f32[24,5120]{1,0:T(8,128)S(1)}, f32[24,5120]{1,0:T(8,128)S(1)}, u32[]{:S(2)}, u32[]{:S(2)}) collective-permute-start(f32[24,5120]{1,0:T(8,128)S(1)} %relay_pack.1), channel_id=1, source_target_pairs={{0,2},{1,3},{2,4},{3,5},{4,6},{5,7},{6,8},{7,9},{8,10},{9,11},{10,... | collective-permute-start | bytes 1474568 | tf_op jit(solution)/shard_map/ppermute | solution.py:678
  63.5 6.5 %collective-permute-start.15 = (f32[4,5120]{1,0:T(4,128)S(1)}, f32[4,5120]{1,0:T(4,128)S(1)}, u32[]{:S(2)}, u32[]{:S(2)}) collective-permute-start(f32[4,5120]{1,0:T(4,128)S(1)} %far_pack.1), channel_id=1, source_target_pairs={{0,12},{1,13},{2,14},{3,15},{4,0},{5,1},{6,2},{7,3},{8,4},{9,5},{1... | collective-permute-start | bytes 245768 | tf_op jit(solution)/shard_map/ppermute | solution.py:678
  65.5 11.1 %collective-permute-start.13 = (f32[2,5120]{1,0:T(2,128)S(1)}, f32[2,5120]{1,0:T(2,128)S(1)}, u32[]{:S(2)}, u32[]{:S(2)}) collective-permute-start(f32[2,5120]{1,0:T(2,128)S(1)} %get-tuple-element.34), channel_id=1, source_target_pairs={{0,6},{1,7},{2,8},{3,9},{4,10},{5,11},{6,12},{7,13},{8,14},{9,15},... | collective-permute-start | bytes 122888 | tf_op jit(solution)/shard_map/ppermute | solution.py:678
  65.5 11.0 %collective-permute-start.12 = (f32[2,5120]{1,0:T(2,128)S(1)}, f32[2,5120]{1,0:T(2,128)S(1)}, u32[]{:S(2)}, u32[]{:S(2)}) collective-permute-start(f32[2,5120]{1,0:T(2,128)S(1)} %get-tuple-element.33.refs_4_.sum_a), channel_id=1, source_target_pairs={{0,10},{1,11},{2,12},{3,13},{4,14},{5,15},{6,0},{7,1},{8,2},{9,3},... | collective-permute-start | bytes 122888 | tf_op jit(solution)/shard_map/ppermute | solution.py:678
  79.5 6.2 %copy-start.4 = (s32[128]{0:T(128)S(1)}, s32[128]{0:T(128)}, u32[]{:S(2)}) copy-start(s32[128]{0:T(128)} %counts_ref.1) | copy-start | bytes 1540
  79.5 6.2 %copy-start.5 = (s32[2]{0:T(128)S(1)}, s32[2]{0:T(128)}, u32[]{:S(2)}) copy-start(s32[2]{0:T(128)} %get-tuple-element.25.refs_2_.state_ref) | copy-start | bytes 28
  79.5 4.5 %collective-permute-start.17 = (f32[40,2560]{1,0:T(8,128)S(1)}, f32[40,2560]{1,0:T(8,128)S(1)}, u32[]{:S(2)}, u32[]{:S(2)}) collective-permute-start(f32[40,2560]{1,0:T(8,128)S(1)} %get-tuple-element.38), channel_id=1, source_target_pairs={{0,1},{1,0},{2,3},{3,2},{4,5},{5,4},{6,7},{7,6},{8,9},{9,8},{10,11... | collective-permute-start | bytes 1228808 | tf_op jit(solution)/shard_map/ppermute | solution.py:684
  83.9 1.8 %collective-permute-start.16 = (f32[40,2560]{1,0:T(8,128)S(1)}, f32[40,2560]{1,0:T(8,128)S(1)}, u32[]{:S(2)}, u32[]{:S(2)}) collective-permute-start(f32[40,2560]{1,0:T(8,128)S(1)} %get-tuple-element.36), channel_id=1, source_target_pairs={{0,1},{1,0},{2,3},{3,2},{4,5},{5,4},{6,7},{7,6},{8,9},{9,8},{10,11... | collective-permute-start | bytes 1228808 | tf_op jit(solution)/shard_map/ppermute | solution.py:684

commit v5 on v3

--- a/solution.py
+++ b/solution.py
@@ -340,7 +340,7 @@
         send_ref[:ROWS, lanes(j)] = other
         return 0
 
-    lax.fori_loop(0, half, emit, 0, unroll=2)
+    lax.fori_loop(0, half, emit, 0, unroll=10)
     none = jnp.zeros((PAD - ROWS, send_ref.shape[1]), jnp.float32)
     both_ref[ROWS:PAD, :] = none
     both_ref[PAD + ROWS :, :] = none
@@ -590,7 +590,7 @@
             held[base + (1 - core) * half + j] = other[:, lanes(j)]
             return 0
 
-        lax.fori_loop(0, half, fill, 0, unroll=2)
+        lax.fori_loop(0, half, fill, 0, unroll=10)
         base += tiles
     lane = lax.broadcasted_iota(jnp.int32, (PAD, TILE), 1)
 

time: 86.5 us -> 86.6 us (level)
  no operation moved by 1% of the time
where the time goes in v5:
time: 86.6 us; the launch traced here: 85.5 us
  starting transfers between devices  37.2 us (43%)
  Pallas kernels  24.8 us (29%)
  waiting for transfers between devices  22.3 us (26%)
    ppermute x9, waiting for transfers between devices, shift(): lax.ppermute(x, 'spec', [(s, (s + hops) % N_SPEC) for s in range(N_SPEC)])  19.5 us
    ppermute x9, starting transfers between devices, shift(): lax.ppermute(x, 'spec', [(s, (s + hops) % N_SPEC) for s in range(N_SPEC)])  15.9 us
    ppermute x8, starting transfers between devices, swap(): return lax.ppermute(x, 'spec', [(s, s ^ 1) for s in range(N_SPEC)])  15.3 us
    pallas_call x2, Pallas kernels, advect(): pl.pallas_call(partial(advect_kernel, last, base, tiles), grid_spec=pltpu...  14.3 us
    ppermute x1, starting transfers between devices, per_device(): lax.ppermute(to_lower, 'space', [(s, (s - 1) % N_SPACE) for s in range(N_...  3.72 us
    pallas_call x1, Pallas kernels, expand(): pl.pallas_call(expand_kernel, grid_spec=pltpu.PrefetchScalarGridSpec(num_...  3.67 us
    pallas_call x2, Pallas kernels, sources(): pl.pallas_call(sources_kernel, grid_spec=pltpu.PrefetchScalarGridSpec(num...  3.29 us
    ppermute x8, waiting for transfers between devices, swap(): return lax.ppermute(x, 'spec', [(s, s ^ 1) for s in range(N_SPEC)])  2.87 us
  transfers between devices with their start and end apart: 19, of which 7 were waited for; matrix products, arithmetic and copies ran while one was open for 0% of the time, Pallas kernels for 22%

profile of v5, /device:TPU:1, one launch (start us, length us, event | category | flops | bytes accessed | tf_op | source)
XLA Modules:
  0.0 85.5 jit_solution(3000922184383187171)
XLA Ops:
  0.0 2.4 %edges.1 = (f32[40,128]{1,0:T(8,128)}, f32[40,128]{1,0:T(8,128)}, f32[128,128]{1,0:T(8,128)}, f32[128,128]{1,0:T(8,128)}, f32[40,128]{1,0:T(8,128)}, /*index=5*/f32[40,128]{1,0:T(8,128)}) custom-call(s32[1]{0:T(128)} %bitcast.dev_ref.refs_0_, f32[39,16384]{1,0:T(8,128)} %refs_3_.3, f32[39,16384]{1,0:T(8,128)} %refs_3_.3, s32[2,128]{1,0:T(2,128)} %bitcast.8, ...), custom_call_target="tpu_custom_call" | custom-call | tf_op jit(solution)/shard_map/edges/pallas_call | solution.py:185
  2.4 2.2 %collective-permute-start.5 = (f32[40,128]{1,0:T(8,128)}, f32[40,128]{1,0:T(8,128)S(1)}, u32[]{:S(2)}, u32[]{:S(2)}) collective-permute-start(f32[40,128]{1,0:T(8,128)} %get-tuple-element.29), channel_id=1, source_target_pairs={{0,16},{16,32},{32,48},{48,64},{64,80},{80,96},{96,112},{112,128},... | collective-permute-start | bytes 61448 | tf_op jit(solution)/shard_map/ppermute | solution.py:683
  4.6 3.7 %collective-permute-start.6 = (f32[40,128]{1,0:T(8,128)}, f32[40,128]{1,0:T(8,128)S(1)}, u32[]{:S(2)}, u32[]{:S(2)}) collective-permute-start(f32[40,128]{1,0:T(8,128)} %get-tuple-element.30), channel_id=1, source_target_pairs={{0,240},{16,0},{32,16},{48,32},{64,48},{80,64},{96,80},{112,96},{1... | collective-permute-start | bytes 61448 | tf_op jit(solution)/shard_map/ppermute | solution.py:684
  8.3 6.9 %advect.2 = (f32[80,2560]{1,0:T(8,128)}, f32[40,2560]{1,0:T(8,128)}, s32[2]{0:T(128)}) custom-call(s32[1]{0:T(128)} %bitcast.dev_ref.refs_0_, s32[128]{0:T(128)} %counts_ref.1, f32[39,16384]{1,0:T(8,128)} %refs_3_.3, s32[4,16384]{1,0:T(4,128)} %refs_4_.3, s32[4,16384]{1,0:T(4,128)} %refs_5_.1, f32[128,128]{1,0:T(8,128)} %get-tuple-element.22.refs_5_.refs_8_.refs_6_.refs_11_, ...), custom_call_target="tpu_custom_call" | custom-call | tf_op jit(solution)/shard_map/advect/pallas_call | solution.py:364
  15.3 0.0 copy-start.8
  15.3 5.7 %collective-permute-start.3 = (f32[80,2560]{1,0:T(8,128)}, f32[80,2560]{1,0:T(8,128)S(1)}, u32[]{:S(2)}, u32[]{:S(2)}) collective-permute-start(f32[80,2560]{1,0:T(8,128)} %get-tuple-element.27.mine_ref.refs_0_), channel_id=1, source_target_pairs={{0,14},{1,15},{2,0},{3,1},{4,2},{5,3},{6,4},{7,5},{8,6},{9,7},{10,... | collective-permute-start | bytes 2457608 | tf_op jit(solution)/shard_map/ppermute | solution.py:674
  20.9 0.0 collective-permute-start.1
  20.9 0.0 collective-permute-done.5.refs_9_
  20.9 0.0 collective-permute-done.6.refs_10_
  20.9 0.0 copy-start.7
  21.0 0.6 copy-done.6
  21.5 0.0 copy-done.7
  21.6 7.3 %advect.3 = (f32[80,2560]{1,0:T(8,128)}, f32[40,2560]{1,0:T(8,128)}) custom-call(s32[1]{0:T(128)} %bitcast.dev_ref.refs_0_, s32[128]{0:T(128)} %counts_ref.1, s32[2]{0:T(128)} %get-tuple-element.25.refs_2_.state_ref, f32[39,16384]{1,0:T(8,128)} %refs_3_.3, s32[4,16384]{1,0:T(4,128)} %refs_4_.3, s32[4,16384]{1,0:T(4,128)} %refs_5_.1, ...), custom_call_target="tpu_custom_call" | custom-call | tf_op jit(solution)/shard_map/advect/pallas_call | solution.py:364
  28.9 0.0 copy-start
  28.9 2.7 %collective-permute-start.10 = (f32[80,2560]{1,0:T(8,128)}, f32[80,2560]{1,0:T(8,128)S(1)}, u32[]{:S(2)}, u32[]{:S(2)}) collective-permute-start(f32[80,2560]{1,0:T(8,128)} %get-tuple-element.31.mine_ref.refs_2_.refs_0_), channel_id=1, source_target_pairs={{0,14},{1,15},{2,0},{3,1},{4,2},{5,3},{6,4},{7,5},{8,6},{9,7},{10,... | collective-permute-start | bytes 2457608 | tf_op jit(solution)/shard_map/ppermute | solution.py:674
  31.7 0.0 collective-permute-start.8
  31.7 0.0 copy-done.8
  31.7 1.8 %collective-permute-start = (f32[40,2560]{1,0:T(8,128)S(1)}, f32[40,2560]{1,0:T(8,128)S(1)}, u32[]{:S(2)}, u32[]{:S(2)}) collective-permute-start(f32[40,2560]{1,0:T(8,128)S(1)} %copy-done.8), channel_id=1, source_target_pairs={{0,1},{1,0},{2,3},{3,2},{4,5},{5,4},{6,7},{7,6},{8,9},{9,8},{10,11... | collective-permute-start | bytes 1228808 | tf_op jit(solution)/shard_map/ppermute | solution.py:680
  33.5 4.3 %collective-permute-done.3.refs_3_.refs_4_ = f32[80,2560]{1,0:T(8,128)S(1)} collective-permute-done((f32[80,2560]{1,0:T(8,128)}, f32[80,2560]{1,0:T(8,128)S(1)}, u32[]{:S(2)}, u32[]{:S(2)}) %collective-permute-start.3) | collective-permute-done | bytes 819232 | tf_op jit(solution)/shard_map/ppermute | solution.py:674
  37.8 3.4 %collective-permute-start.7 = (f32[40,2560]{1,0:T(8,128)}, f32[40,2560]{1,0:T(8,128)S(1)}, u32[]{:S(2)}, u32[]{:S(2)}) collective-permute-start(f32[40,2560]{1,0:T(8,128)} %get-tuple-element.32), channel_id=1, source_target_pairs={{0,1},{1,0},{2,3},{3,2},{4,5},{5,4},{6,7},{7,6},{8,9},{9,8},{10,11... | collective-permute-start | bytes 1228808 | tf_op jit(solution)/shard_map/ppermute | solution.py:680
  41.3 0.0 collective-permute-done.1.refs_1_.mine_ref.refs_2_
  41.3 3.6 %collective-permute-start.4 = (f32[40,2560]{1,0:T(8,128)S(1)}, f32[40,2560]{1,0:T(8,128)S(1)}, u32[]{:S(2)}, u32[]{:S(2)}) collective-permute-start(f32[40,2560]{1,0:T(8,128)S(1)} %slice.17), channel_id=1, source_target_pairs={{0,1},{1,0},{2,3},{3,2},{4,5},{5,4},{6,7},{7,6},{8,9},{9,8},{10,11... | collective-permute-start | bytes 1228808 | tf_op jit(solution)/shard_map/ppermute | solution.py:680
  44.8 10.5 %collective-permute-done.10.refs_8_.refs_4_ = f32[80,2560]{1,0:T(8,128)S(1)} collective-permute-done((f32[80,2560]{1,0:T(8,128)}, f32[80,2560]{1,0:T(8,128)S(1)}, u32[]{:S(2)}, u32[]{:S(2)}) %collective-permute-start.10) | collective-permute-done | bytes 819232 | tf_op jit(solution)/shard_map/ppermute | solution.py:674
  55.3 1.9 %collective-permute-start.2 = (f32[40,2560]{1,0:T(8,128)S(1)}, f32[40,2560]{1,0:T(8,128)S(1)}, u32[]{:S(2)}, u32[]{:S(2)}) collective-permute-start(f32[40,2560]{1,0:T(8,128)S(1)} %slice.16), channel_id=1, source_target_pairs={{0,1},{1,0},{2,3},{3,2},{4,5},{5,4},{6,7},{7,6},{8,9},{9,8},{10,11... | collective-permute-start | bytes 1228808 | tf_op jit(solution)/shard_map/ppermute | solution.py:680
  57.3 1.1 %collective-permute-done.8.refs_6_.mine_ref.refs_2_ = f32[80,2560]{1,0:T(8,128)S(1)} collective-permute-done((f32[80,2560]{1,0:T(8,128)}, f32[80,2560]{1,0:T(8,128)S(1)}, u32[]{:S(2)}, u32[]{:S(2)}) %collective-permute-start.8) | collective-permute-done | bytes 819232 | tf_op jit(solution)/shard_map/ppermute | solution.py:674
  58.4 2.2 %collective-permute-start.11 = (f32[40,2560]{1,0:T(8,128)S(1)}, f32[40,2560]{1,0:T(8,128)S(1)}, u32[]{:S(2)}, u32[]{:S(2)}) collective-permute-start(f32[40,2560]{1,0:T(8,128)S(1)} %slice.19), channel_id=1, source_target_pairs={{0,1},{1,0},{2,3},{3,2},{4,5},{5,4},{6,7},{7,6},{8,9},{9,8},{10,11... | collective-permute-start | bytes 1228808 | tf_op jit(solution)/shard_map/ppermute | solution.py:680
  60.6 0.0 collective-permute-done.other_ref.refs_1_
  60.6 0.1 collective-permute-start.9
  60.7 0.0 copy-done.1
  60.7 0.0 copy-done.2
  60.7 0.0 copy-done.3
  60.7 0.2 moments.2.refs_0_
  60.9 0.0 collective-permute-done.7.other_ref.refs_3_.refs_1_
  60.9 0.0 copy-done
  60.9 0.2 moments.3.refs_5_
  61.1 0.0 collective-permute-done.2.refs_2_.other_ref.refs_3_
  61.1 0.0 slice-start
  61.2 0.0 slice-start.1
  61.2 0.1 collective-permute-start.14
  61.3 0.0 collective-permute-done.4.refs_4_.refs_5_
  61.3 0.6 collective-permute-done.11.refs_9_.refs_5_
  61.9 0.6 collective-permute-done.9.refs_7_.other_ref.refs_3_
  62.5 0.7 moment_windows.1
  63.3 0.3 collective-permute-start.17
  63.6 2.7 %collective-permute-start.15 = (f32[4,5120]{1,0:T(4,128)S(1)}, f32[4,5120]{1,0:T(4,128)S(1)}, u32[]{:S(2)}, u32[]{:S(2)}) collective-permute-start(f32[4,5120]{1,0:T(4,128)S(1)} %far_pack.1), channel_id=1, source_target_pairs={{0,12},{1,13},{2,14},{3,15},{4,0},{5,1},{6,2},{7,3},{8,4},{9,5},{1... | collective-permute-start | bytes 245768 | tf_op jit(solution)/shard_map/ppermute | solution.py:674
  66.3 0.0 collective-permute-start.13
  66.3 4.5 %collective-permute-start.12 = (f32[2,5120]{1,0:T(2,128)S(1)}, f32[2,5120]{1,0:T(2,128)S(1)}, u32[]{:S(2)}, u32[]{:S(2)}) collective-permute-start(f32[2,5120]{1,0:T(2,128)S(1)} %get-tuple-element.33.sum_a.refs_0_), channel_id=1, source_target_pairs={{0,10},{1,11},{2,12},{3,13},{4,14},{5,15},{6,0},{7,1},{8,2},{9,3},... | collective-permute-start | bytes 122888 | tf_op jit(solution)/shard_map/ppermute | solution.py:674
  70.8 0.0 collective-permute-done.15.refs_7_
  70.8 3.6 %collective-permute-done.13.sum_c = f32[2,5120]{1,0:T(2,128)S(1)} collective-permute-done((f32[2,5120]{1,0:T(2,128)S(1)}, f32[2,5120]{1,0:T(2,128)S(1)}, u32[]{:S(2)}, u32[]{:S(2)}) %collective-permute-start.13) | collective-permute-done | bytes 40992 | tf_op jit(solution)/shard_map/ppermute | solution.py:674
  74.4 0.0 collective-permute-done.12.sum_b
  74.4 0.0 collective-permute-done.14.refs_6_
  74.4 0.0 slice-done
  74.4 0.0 slice-done.1
  74.4 1.7 %sources.2 = (f32[40,2560]{1,0:T(8,128)S(1)}, f32[40,2560]{1,0:T(8,128)S(1)}) custom-call(s32[1]{0:T(128)} %bitcast.dev_ref.refs_0_, bf16[16,160,816]{2,1,0:T(8,128)(2,1)S(1)} %bitcast.5, f32[40,128]{1,0:T(8,128)S(1)} %copy-done.2, f32[40,128]{1,0:T(8,128)S(1)} %copy-done.3, f32[2,5120]{1,0:T(2,128)S(1)} %get-tuple-element.33.sum_a.refs_0_, ...), custom_call_target="tpu_custom_call" | custom-call | tf_op jit(solution)/shard_map/sources/pallas_call | solution.py:559
  76.1 0.0 copy-start.4
  76.1 0.0 copy-start.5
  76.1 2.1 %collective-permute-start.16 = (f32[40,2560]{1,0:T(8,128)S(1)}, f32[40,2560]{1,0:T(8,128)S(1)}, u32[]{:S(2)}, u32[]{:S(2)}) collective-permute-start(f32[40,2560]{1,0:T(8,128)S(1)} %get-tuple-element.36), channel_id=1, source_target_pairs={{0,1},{1,0},{2,3},{3,2},{4,5},{5,4},{6,7},{7,6},{8,9},{9,8},{10,11... | collective-permute-start | bytes 1228808 | tf_op jit(solution)/shard_map/ppermute | solution.py:680
  78.2 0.0 collective-permute-done.17.refs_6_
  78.2 1.6 %sources.3 = (f32[40,2560]{1,0:T(8,128)S(1)}, f32[40,2560]{1,0:T(8,128)S(1)}) custom-call(s32[1]{0:T(128)} %bitcast.dev_ref.refs_0_, bf16[16,160,816]{2,1,0:T(8,128)(2,1)S(1)} %bitcast.5, f32[40,128]{1,0:T(8,128)S(1)} %copy-done.2, f32[40,128]{1,0:T(8,128)S(1)} %copy-done.3, f32[2,5120]{1,0:T(2,128)S(1)} %get-tuple-element.33.sum_a.refs_0_, ...), custom_call_target="tpu_custom_call" | custom-call | tf_op jit(solution)/shard_map/sources/pallas_call | solution.py:559
  79.9 0.2 collective-permute-start.18
  80.1 0.0 collective-permute-done.16.refs_1_
  80.1 1.6 %collective-permute-done.18.refs_3_ = f32[40,2560]{1,0:T(8,128)S(1)} collective-permute-done((f32[40,2560]{1,0:T(8,128)S(1)}, f32[40,2560]{1,0:T(8,128)S(1)}, u32[]{:S(2)}, u32[]{:S(2)}) %collective-permute-start.18) | collective-permute-done | bytes 409632 | tf_op jit(solution)/shard_map/ppermute | solution.py:680
  81.7 0.0 copy-done.4
  81.7 3.7 %expand.1 = f32[39,16384]{1,0:T(8,128)} custom-call(s32[1]{0:T(128)} %bitcast.dev_ref.refs_0_, s32[128]{0:T(128)S(1)} %copy-done.4, s32[2]{0:T(128)S(1)} %copy-done.5, f32[40,2560]{1,0:T(8,128)S(1)} %get-tuple-element.35.refs_0_, f32[40,2560]{1,0:T(8,128)S(1)} %collective-permute-done.16.refs_1_, f32[40,2560]{1,0:T(8,128)S(1)} %get-tuple-element.37.refs_2_, ...), custom_call_target="tpu_custom_call" | custom-call | tf_op jit(solution)/shard_map/expand/pallas_call | solution.py:648
  (13 shorter events, 0.2 us)
Async XLA Ops:
  2.4 18.5 %collective-permute-start.5 = (f32[40,128]{1,0:T(8,128)}, f32[40,128]{1,0:T(8,128)S(1)}, u32[]{:S(2)}, u32[]{:S(2)}) collective-permute-start(f32[40,128]{1,0:T(8,128)} %get-tuple-element.29), channel_id=1, source_target_pairs={{0,16},{16,32},{32,48},{48,64},{64,80},{80,96},{96,112},{112,128},... | collective-permute-start | bytes 61448 | tf_op jit(solution)/shard_map/ppermute | solution.py:683
  4.6 16.3 %collective-permute-start.6 = (f32[40,128]{1,0:T(8,128)}, f32[40,128]{1,0:T(8,128)S(1)}, u32[]{:S(2)}, u32[]{:S(2)}) collective-permute-start(f32[40,128]{1,0:T(8,128)} %get-tuple-element.30), channel_id=1, source_target_pairs={{0,240},{16,0},{32,16},{48,32},{64,48},{80,64},{96,80},{112,96},{1... | collective-permute-start | bytes 61448 | tf_op jit(solution)/shard_map/ppermute | solution.py:684
  15.3 16.4 %copy-start.8 = (f32[40,2560]{1,0:T(8,128)S(1)}, f32[40,2560]{1,0:T(8,128)}, u32[]{:S(2)}) copy-start(f32[40,2560]{1,0:T(8,128)} %get-tuple-element.28) | copy-start | bytes 1228804
  15.3 22.5 %collective-permute-start.3 = (f32[80,2560]{1,0:T(8,128)}, f32[80,2560]{1,0:T(8,128)S(1)}, u32[]{:S(2)}, u32[]{:S(2)}) collective-permute-start(f32[80,2560]{1,0:T(8,128)} %get-tuple-element.27.mine_ref.refs_0_), channel_id=1, source_target_pairs={{0,14},{1,15},{2,0},{3,1},{4,2},{5,3},{6,4},{7,5},{8,6},{9,7},{10,... | collective-permute-start | bytes 2457608 | tf_op jit(solution)/shard_map/ppermute | solution.py:674
  20.9 20.3 %collective-permute-start.1 = (f32[80,2560]{1,0:T(8,128)}, f32[80,2560]{1,0:T(8,128)S(1)}, u32[]{:S(2)}, u32[]{:S(2)}) collective-permute-start(f32[80,2560]{1,0:T(8,128)} %get-tuple-element.27.mine_ref.refs_0_), channel_id=1, source_target_pairs={{0,2},{1,3},{2,4},{3,5},{4,6},{5,7},{6,8},{7,9},{8,10},{9,11},{10,... | collective-permute-start | bytes 2457608 | tf_op jit(solution)/shard_map/ppermute | solution.py:674
  20.9 0.6 copy-start.6
  20.9 0.6 copy-start.7
  21.5 39.2 %copy-start.1 = (f32[80,2560]{1,0:T(8,128)S(1)}, f32[80,2560]{1,0:T(8,128)}, u32[]{:S(2)}) copy-start(f32[80,2560]{1,0:T(8,128)} %get-tuple-element.27.mine_ref.refs_0_) | copy-start | bytes 2457604
  21.5 39.2 %copy-start.2 = (f32[40,128]{1,0:T(8,128)S(1)}, f32[40,128]{1,0:T(8,128)}, u32[]{:S(2)}) copy-start(f32[40,128]{1,0:T(8,128)} %get-tuple-element.24.refs_7_.tab_a.refs_8_.refs_10_) | copy-start | bytes 61444
  21.6 39.2 %copy-start.3 = (f32[40,128]{1,0:T(8,128)S(1)}, f32[40,128]{1,0:T(8,128)}, u32[]{:S(2)}) copy-start(f32[40,128]{1,0:T(8,128)} %get-tuple-element.26.tab_b.refs_11_) | copy-start | bytes 61444
  28.9 32.0 %copy-start = (f32[80,2560]{1,0:T(8,128)S(1)}, f32[80,2560]{1,0:T(8,128)}, u32[]{:S(2)}) copy-start(f32[80,2560]{1,0:T(8,128)} %get-tuple-element.31.mine_ref.refs_2_.refs_0_) | copy-start | bytes 2457604
  28.9 26.4 %collective-permute-start.10 = (f32[80,2560]{1,0:T(8,128)}, f32[80,2560]{1,0:T(8,128)S(1)}, u32[]{:S(2)}, u32[]{:S(2)}) collective-permute-start(f32[80,2560]{1,0:T(8,128)} %get-tuple-element.31.mine_ref.refs_2_.refs_0_), channel_id=1, source_target_pairs={{0,14},{1,15},{2,0},{3,1},{4,2},{5,3},{6,4},{7,5},{8,6},{9,7},{10,... | collective-permute-start | bytes 2457608 | tf_op jit(solution)/shard_map/ppermute | solution.py:674
  31.7 26.7 %collective-permute-start.8 = (f32[80,2560]{1,0:T(8,128)}, f32[80,2560]{1,0:T(8,128)S(1)}, u32[]{:S(2)}, u32[]{:S(2)}) collective-permute-start(f32[80,2560]{1,0:T(8,128)} %get-tuple-element.31.mine_ref.refs_2_.refs_0_), channel_id=1, source_target_pairs={{0,2},{1,3},{2,4},{3,5},{4,6},{5,7},{6,8},{7,9},{8,10},{9,11},{10,... | collective-permute-start | bytes 2457608 | tf_op jit(solution)/shard_map/ppermute | solution.py:674
  31.7 28.9 %collective-permute-start = (f32[40,2560]{1,0:T(8,128)S(1)}, f32[40,2560]{1,0:T(8,128)S(1)}, u32[]{:S(2)}, u32[]{:S(2)}) collective-permute-start(f32[40,2560]{1,0:T(8,128)S(1)} %copy-done.8), channel_id=1, source_target_pairs={{0,1},{1,0},{2,3},{3,2},{4,5},{5,4},{6,7},{7,6},{8,9},{9,8},{10,11... | collective-permute-start | bytes 1228808 | tf_op jit(solution)/shard_map/ppermute | solution.py:680
  37.8 23.1 %collective-permute-start.7 = (f32[40,2560]{1,0:T(8,128)}, f32[40,2560]{1,0:T(8,128)S(1)}, u32[]{:S(2)}, u32[]{:S(2)}) collective-permute-start(f32[40,2560]{1,0:T(8,128)} %get-tuple-element.32), channel_id=1, source_target_pairs={{0,1},{1,0},{2,3},{3,2},{4,5},{5,4},{6,7},{7,6},{8,9},{9,8},{10,11... | collective-permute-start | bytes 1228808 | tf_op jit(solution)/shard_map/ppermute | solution.py:680
  41.3 20.0 %collective-permute-start.4 = (f32[40,2560]{1,0:T(8,128)S(1)}, f32[40,2560]{1,0:T(8,128)S(1)}, u32[]{:S(2)}, u32[]{:S(2)}) collective-permute-start(f32[40,2560]{1,0:T(8,128)S(1)} %slice.17), channel_id=1, source_target_pairs={{0,1},{1,0},{2,3},{3,2},{4,5},{5,4},{6,7},{7,6},{8,9},{9,8},{10,11... | collective-permute-start | bytes 1228808 | tf_op jit(solution)/shard_map/ppermute | solution.py:680
  55.3 5.8 %collective-permute-start.2 = (f32[40,2560]{1,0:T(8,128)S(1)}, f32[40,2560]{1,0:T(8,128)S(1)}, u32[]{:S(2)}, u32[]{:S(2)}) collective-permute-start(f32[40,2560]{1,0:T(8,128)S(1)} %slice.16), channel_id=1, source_target_pairs={{0,1},{1,0},{2,3},{3,2},{4,5},{5,4},{6,7},{7,6},{8,9},{9,8},{10,11... | collective-permute-start | bytes 1228808 | tf_op jit(solution)/shard_map/ppermute | solution.py:680
  58.4 3.6 %collective-permute-start.11 = (f32[40,2560]{1,0:T(8,128)S(1)}, f32[40,2560]{1,0:T(8,128)S(1)}, u32[]{:S(2)}, u32[]{:S(2)}) collective-permute-start(f32[40,2560]{1,0:T(8,128)S(1)} %slice.19), channel_id=1, source_target_pairs={{0,1},{1,0},{2,3},{3,2},{4,5},{5,4},{6,7},{7,6},{8,9},{9,8},{10,11... | collective-permute-start | bytes 1228808 | tf_op jit(solution)/shard_map/ppermute | solution.py:680
  60.6 1.9 %collective-permute-start.9 = (f32[40,2560]{1,0:T(8,128)S(1)}, f32[40,2560]{1,0:T(8,128)S(1)}, u32[]{:S(2)}, u32[]{:S(2)}) collective-permute-start(f32[40,2560]{1,0:T(8,128)S(1)} %slice.18), channel_id=1, source_target_pairs={{0,1},{1,0},{2,3},{3,2},{4,5},{5,4},{6,7},{7,6},{8,9},{9,8},{10,11... | collective-permute-start | bytes 1228808 | tf_op jit(solution)/shard_map/ppermute | solution.py:680
  61.1 13.3 %slice-start = ((s8[4587520]{0:T(1024)(128)(4,1)}), s8[4194304]{0:T(1024)(128)(4,1)S(1)}, s32[]{:S(2)}) async-start(s8[4587520]{0:T(1024)(128)(4,1)} %bitcast.4), calls=%async_computation | async-start | bytes 8388608
  61.2 13.2 %slice-start.1 = ((s8[4587520]{0:T(1024)(128)(4,1)}), s8[393216]{0:T(1024)(128)(4,1)S(1)}, s32[]{:S(2)}) async-start(s8[4587520]{0:T(1024)(128)(4,1)} %bitcast.4), calls=%async_computation.1 | async-start | bytes 786432
  61.2 13.2 %collective-permute-start.14 = (f32[24,2560]{1,0:T(8,128)S(1)}, f32[24,2560]{1,0:T(8,128)S(1)}, u32[]{:S(2)}, u32[]{:S(2)}) collective-permute-start(f32[24,2560]{1,0:T(8,128)S(1)} %relay_pack.2), channel_id=1, source_target_pairs={{0,2},{1,3},{2,4},{3,5},{4,6},{5,7},{6,8},{7,9},{8,10},{9,11},{10,... | collective-permute-start | bytes 737288 | tf_op jit(solution)/shard_map/ppermute | solution.py:674
  63.3 14.9 %collective-permute-start.17 = (f32[24,2560]{1,0:T(8,128)S(1)}, f32[24,2560]{1,0:T(8,128)S(1)}, u32[]{:S(2)}, u32[]{:S(2)}) collective-permute-start(f32[24,2560]{1,0:T(8,128)S(1)} %relay_pack.3), channel_id=1, source_target_pairs={{0,2},{1,3},{2,4},{3,5},{4,6},{5,7},{6,8},{7,9},{8,10},{9,11},{10,... | collective-permute-start | bytes 737288 | tf_op jit(solution)/shard_map/ppermute | solution.py:674
  63.6 7.2 %collective-permute-start.15 = (f32[4,5120]{1,0:T(4,128)S(1)}, f32[4,5120]{1,0:T(4,128)S(1)}, u32[]{:S(2)}, u32[]{:S(2)}) collective-permute-start(f32[4,5120]{1,0:T(4,128)S(1)} %far_pack.1), channel_id=1, source_target_pairs={{0,12},{1,13},{2,14},{3,15},{4,0},{5,1},{6,2},{7,3},{8,4},{9,5},{1... | collective-permute-start | bytes 245768 | tf_op jit(solution)/shard_map/ppermute | solution.py:674
  66.3 8.1 %collective-permute-start.13 = (f32[2,5120]{1,0:T(2,128)S(1)}, f32[2,5120]{1,0:T(2,128)S(1)}, u32[]{:S(2)}, u32[]{:S(2)}) collective-permute-start(f32[2,5120]{1,0:T(2,128)S(1)} %get-tuple-element.34), channel_id=1, source_target_pairs={{0,6},{1,7},{2,8},{3,9},{4,10},{5,11},{6,12},{7,13},{8,14},{9,15},... | collective-permute-start | bytes 122888 | tf_op jit(solution)/shard_map/ppermute | solution.py:674
  66.3 8.1 %collective-permute-start.12 = (f32[2,5120]{1,0:T(2,128)S(1)}, f32[2,5120]{1,0:T(2,128)S(1)}, u32[]{:S(2)}, u32[]{:S(2)}) collective-permute-start(f32[2,5120]{1,0:T(2,128)S(1)} %get-tuple-element.33.sum_a.refs_0_), channel_id=1, source_target_pairs={{0,10},{1,11},{2,12},{3,13},{4,14},{5,15},{6,0},{7,1},{8,2},{9,3},... | collective-permute-start | bytes 122888 | tf_op jit(solution)/shard_map/ppermute | solution.py:674
  76.1 5.6 %copy-start.4 = (s32[128]{0:T(128)S(1)}, s32[128]{0:T(128)}, u32[]{:S(2)}) copy-start(s32[128]{0:T(128)} %counts_ref.1) | copy-start | bytes 1540
  76.1 5.6 %copy-start.5 = (s32[2]{0:T(128)S(1)}, s32[2]{0:T(128)}, u32[]{:S(2)}) copy-start(s32[2]{0:T(128)} %get-tuple-element.25.refs_2_.state_ref) | copy-start | bytes 28
  76.1 3.9 %collective-permute-start.16 = (f32[40,2560]{1,0:T(8,128)S(1)}, f32[40,2560]{1,0:T(8,128)S(1)}, u32[]{:S(2)}, u32[]{:S(2)}) collective-permute-start(f32[40,2560]{1,0:T(8,128)S(1)} %get-tuple-element.36), channel_id=1, source_target_pairs={{0,1},{1,0},{2,3},{3,2},{4,5},{5,4},{6,7},{7,6},{8,9},{9,8},{10,11... | collective-permute-start | bytes 1228808 | tf_op jit(solution)/shard_map/ppermute | solution.py:680
  79.9 1.8 %collective-permute-start.18 = (f32[40,2560]{1,0:T(8,128)S(1)}, f32[40,2560]{1,0:T(8,128)S(1)}, u32[]{:S(2)}, u32[]{:S(2)}) collective-permute-start(f32[40,2560]{1,0:T(8,128)S(1)} %get-tuple-element.38), channel_id=1, source_target_pairs={{0,1},{1,0},{2,3},{3,2},{4,5},{5,4},{6,7},{7,6},{8,9},{9,8},{10,11... | collective-permute-start | bytes 1228808 | tf_op jit(solution)/shard_map/ppermute | solution.py:680
